TPU v7x, 256 devices: a whole 4x4x8 slice. The times are simulated.
256 devices in a mesh: seq: 64 (over x_lo, z, y), tensor: 4 (over x_hi, core).
Axes of the slice: x: 4 (x_hi: 2, x_lo: 2; x = x_hi * 2 + x_lo), y: 4, z: 8, core: 2. Of those that a mesh axis runs over, the one named last changes fastest.
Arguments:
- queries: bfloat16 [16384, 2048], P('seq', 'tensor'), may hold values from -120 to 120
- key_heads: bfloat16 [16384, 2, 128], P('seq'), may hold values from -6 to 6
- value_heads: bfloat16 [16384, 2, 128], P('seq'), may hold values from -6 to 6
- doc_lengths: int32 [8], replicated, may hold values from 1 to 8448, 16384 in all
- out_weight: bfloat16 [2048, 8192], P('tensor'), may hold values from -0.75 to 0.75
Outputs:
- projected: bfloat16 [16384, 8192], P('seq', 'tensor')
Inputs may be any that keep to these rules, and one draw needn't show every extreme that they name: `doc_lengths`: they sum to 16384; the longest document has exactly 8448 tokens.
All inputs are finite; a program needn't handle non-finite values.
Results may differ from a plain program's by a relative error of at most 0.015.
Values may be sent and summed in bfloat16 or wider, within the bound.
No kernel may reach another device: no remote copies, remote signals or barrier semaphores. Data moves between devices by JAX's collectives and lax.ppermute only.
A program may use at most 192 MiB of HBM per device.

v0:
```python
import functools
import math

import jax
import jax.numpy as jnp
from jax import lax
from jax.experimental import pallas as pl
from jax.experimental.pallas import tpu as pltpu
from jax.sharding import PartitionSpec as P

HQ = 16
KVH = 2
HD = 128
SEQ = 64
TENSOR = 4
ROW = 4
THETA = 500000.0
EMPTY = -1e30
MASKED = -1e32
LOG2E = math.log2(math.e)
BLOCK = 256
ROW_TOKENS = ROW * BLOCK
HEADS = 8
LANES = HEADS * BLOCK
STATE = HD + 8
TILE = 512
WIDE = 1024
NOWHERE = 1 << 24
MIB = 1024 * 1024


def device_perm(move):
    pairs = []
    for s in range(SEQ):
        for hi in range(2):
            for core in range(2):
                to = move(s, hi, core)
                if to is not None:
                    pairs.append((s * TENSOR + hi * 2 + core, to[0] * TENSOR + to[1] * 2 + to[2]))
    return pairs


def permute(x, move):
    return lax.ppermute(x, ("seq", "tensor"), device_perm(move))


def in_row(shift):
    return lambda s, hi, core: (s - s % ROW + (s + shift) % ROW, hi, core)


def other_core(s, hi, core):
    return s, hi, 1 - core


def other_hi(s, hi, core):
    return s, 1 - hi, core


def far_block(s, hi, core):
    if core == 0 and s % ROW == ROW - 1 and s + 33 < SEQ:
        return s + 33, hi, core
    return None


def along_rows(step):
    def move(s, hi, core):
        if core == 0:
            return (s + step * ROW, hi, core) if s + step * ROW < SEQ else None
        return (s + (9 - step) * ROW) % SEQ, hi, core

    return move


def rope_tables(positions):
    half = HD // 2
    exponents = jnp.arange(half, dtype=jnp.float32) * (2.0 / HD)
    inverse = jnp.power(jnp.float32(THETA), -exponents)
    angles = positions.astype(jnp.float32)[:, None] * inverse[None, :]
    return jnp.cos(angles), jnp.sin(angles)


def rope(values, cosine, sine):
    half = HD // 2
    first, second = values[..., :half], values[..., half:]
    return jnp.concatenate(
        [first * cosine - second * sine, second * cosine + first * sine], axis=-1
    )


def attend_kernel(sizes, fresh, scalars, q_ref, bounds, *rest):
    state = rest[-1]
    kept, refs = (None, rest[:-1]) if fresh else (rest[-2], rest[:-2])
    parts = []
    for ref in refs:
        at = 0
        while at < ref.shape[0]:
            size = sizes[len(parts)]
            parts.append(ref.at[at : at + size])
            at += size
    scale = HD**-0.5 * LOG2E
    mode = scalars[0]

    def step(lanes, masked):
        q = q_ref[:, lanes]
        scores = []
        for i, part in enumerate(parts):
            s = jnp.dot(part[:, :HD], q, preferred_element_type=jnp.float32)
            if masked:
                at = lax.broadcasted_iota(jnp.int32, s.shape, 0) + scalars[1 + i]
                live = (at >= bounds[0:1, lanes]) & (at <= bounds[1:2, lanes])
                s = jnp.where(live, s, MASKED)
            scores.append(s)
        s = jnp.concatenate(scores, axis=0) if len(scores) > 1 else scores[0]
        values = [part[:, HD:].T for part in parts]
        values = jnp.concatenate(values, axis=1) if len(values) > 1 else values[0]
        values = jnp.concatenate([values, jnp.ones((16, values.shape[1]), jnp.bfloat16)], axis=0)
        peak = jnp.max(s, axis=0, keepdims=True) * scale
        old = jnp.full_like(peak, EMPTY) if fresh else kept[HD : HD + 1, lanes]
        new = jnp.maximum(old, peak)
        weights = jnp.exp2(s * scale - new).astype(jnp.bfloat16)
        summed = jnp.dot(values, weights, preferred_element_type=jnp.float32)
        denom = summed[HD : HD + 1]
        summed = summed[:HD]
        if not fresh:
            alpha = jnp.exp2(old - new)
            summed = summed + kept[:HD, lanes] * alpha
            denom = denom + kept[HD + 1 : HD + 2, lanes] * alpha
        state[:HD, lanes] = summed
        state[HD:, lanes] = jnp.concatenate([new, denom, jnp.zeros((6, WIDE), jnp.float32)], axis=0)

    def steps(masked):
        def one(i, carry):
            step(pl.ds(pl.multiple_of(i * WIDE, WIDE), WIDE), masked)
            return carry

        lax.fori_loop(0, LANES // WIDE, one, 0)

    @pl.when(mode == 0)
    def _():
        if fresh:
            state[:HD, :] = jnp.zeros((HD, LANES), jnp.float32)
            state[HD:, :] = jnp.concatenate(
                [jnp.full((1, LANES), EMPTY, jnp.float32), jnp.zeros((7, LANES), jnp.float32)],
                axis=0,
            )
        else:
            state[...] = kept[...]

    if not fresh:

        @pl.when(mode == 1)
        def _():
            steps(False)

    @pl.when(mode == 2)
    def _():
        steps(True)


def attend(scalars, q_all, bounds, parts, state=None, sizes=None):
    sizes = tuple(sizes or [part.shape[0] for part in parts])
    operands = list(parts) + ([] if state is None else [state])
    return pl.pallas_call(
        functools.partial(attend_kernel, sizes, state is None),
        out_shape=jax.ShapeDtypeStruct((STATE, LANES), jnp.float32),
        in_specs=[pl.BlockSpec(memory_space=pltpu.SMEM)]
        + [pl.BlockSpec(memory_space=pltpu.VMEM)] * (2 + len(operands)),
        out_specs=pl.BlockSpec(memory_space=pltpu.VMEM),
        input_output_aliases={} if state is None else {2 + len(operands): 0},
        compiler_params=pltpu.CompilerParams(vmem_limit_bytes=32 * MIB),
        cost_estimate=pl.CostEstimate(flops=1, bytes_accessed=1, transcendentals=0),
        name="attend",
    )(scalars, q_all, bounds, *operands)


def merge_kernel(mine, theirs, out):
    for h in range(HEADS):
        a = slice(h * BLOCK, (h + 1) * BLOCK)
        g = (h + HEADS // 2) % HEADS
        b = slice(g * BLOCK, (g + 1) * BLOCK)
        peak_a, peak_b = mine[HD : HD + 1, a], theirs[HD : HD + 1, b]
        peak = jnp.maximum(peak_a, peak_b)
        scale_a, scale_b = jnp.exp2(peak_a - peak), jnp.exp2(peak_b - peak)
        denom = mine[HD + 1 : HD + 2, a] * scale_a + theirs[HD + 1 : HD + 2, b] * scale_b
        summed = mine[:HD, a] * scale_a + theirs[:HD, b] * scale_b
        out[:, h * HD : (h + 1) * HD] = (summed / denom).T.astype(jnp.bfloat16)


def merge(mine, theirs):
    return pl.pallas_call(
        merge_kernel,
        out_shape=jax.ShapeDtypeStruct((BLOCK, HEADS * HD), jnp.bfloat16),
        in_specs=[pl.BlockSpec(memory_space=pltpu.VMEM)] * 2,
        out_specs=pl.BlockSpec(memory_space=pltpu.VMEM),
        compiler_params=pltpu.CompilerParams(vmem_limit_bytes=24 * MIB),
        cost_estimate=pl.CostEstimate(flops=8 * LANES * HD, bytes_accessed=3 * MIB, transcendentals=0),
        name="merge",
    )(mine, theirs)


def project_kernel(first, attended, own_weight, other_weight, out):
    half = HEADS * HD // 2
    columns = slice(first, first + out.shape[1])
    total = jnp.dot(attended[:, :half], own_weight[:, columns], preferred_element_type=jnp.float32)
    total += jnp.dot(attended[:, half:], other_weight[:, columns], preferred_element_type=jnp.float32)
    out[...] = total.astype(out.dtype)


def project(attended, own_weight, other_weight, first, columns, dtype):
    return pl.pallas_call(
        functools.partial(project_kernel, first),
        out_shape=jax.ShapeDtypeStruct((BLOCK, columns), dtype),
        in_specs=[pl.BlockSpec(memory_space=pltpu.VMEM)] * 3,
        out_specs=pl.BlockSpec(memory_space=pltpu.VMEM),
        compiler_params=pltpu.CompilerParams(vmem_limit_bytes=32 * MIB),
        cost_estimate=pl.CostEstimate(flops=1, bytes_accessed=1, transcendentals=0),
        name="project",
    )(attended, own_weight, other_weight)


def finish_kernel(kept, received, *rest):
    rest[-1][...] = (kept[...] + received[...].astype(jnp.float32)).astype(jnp.bfloat16)


def finish(kept, received, first, out):
    columns, start = received.shape[1], first // TILE
    tile = pl.BlockSpec((BLOCK, TILE), lambda j: (0, start + j))
    in_specs = [tile, pl.BlockSpec((BLOCK, TILE), lambda j: (0, j))]
    operands = [kept, received]
    if out is not None:
        in_specs.append(pl.BlockSpec(memory_space=pl.ANY))
        operands.append(out)
    return pl.pallas_call(
        finish_kernel,
        out_shape=jax.ShapeDtypeStruct(kept.shape, jnp.bfloat16),
        grid=(columns // TILE,),
        in_specs=in_specs,
        out_specs=tile,
        input_output_aliases={} if out is None else {2: 0},
        compiler_params=pltpu.CompilerParams(vmem_limit_bytes=32 * MIB),
        cost_estimate=pl.CostEstimate(
            flops=BLOCK * columns, bytes_accessed=8 * BLOCK * columns, transcendentals=0
        ),
        name="finish",
    )(*operands)


def body(queries, key_heads, value_heads, doc_lengths, out_weight):
    s = lax.axis_index("seq")
    t = lax.axis_index("tensor")
    hi, core = t // 2, t % 2
    row, col = s // ROW, s % ROW

    query_pos = s * BLOCK + jnp.arange(BLOCK, dtype=jnp.int32)
    cosine, sine = rope_tables(query_pos)
    own_key = lax.dynamic_index_in_dim(key_heads, hi, 1, keepdims=False).astype(jnp.float32)
    own_key = rope(own_key, cosine, sine).astype(jnp.bfloat16)
    own_value = lax.dynamic_index_in_dim(value_heads, hi, 1, keepdims=False)
    block = jnp.concatenate([own_key, own_value], axis=1)

    near = [permute(block, along_rows(step)) for step in (1, 2, 3, 4)]
    far = permute(block, far_block)
    half = lax.dynamic_slice_in_dim(block, core * (BLOCK // 2), BLOCK // 2, 0)
    shifts = (1, -1, 2)
    group_1 = jnp.concatenate([half, near[0], near[1]], axis=0)
    columns_1 = [permute(group_1, in_row(shift)) for shift in shifts]
    group_2 = jnp.concatenate([near[2], near[3]], axis=0)

    heads = queries.shape[1] // HD
    q_rot = rope(
        queries.astype(jnp.float32).reshape(BLOCK, heads, HD), cosine[:, None], sine[:, None]
    ).astype(jnp.bfloat16)
    q_own = jnp.transpose(q_rot, (2, 1, 0)).reshape(HD, heads * BLOCK)
    q_all = jnp.concatenate([q_own, permute(q_own, other_core)], axis=1)

    doc_ends = jnp.cumsum(doc_lengths)
    low = jnp.max(
        jnp.where(doc_ends[None, :] <= query_pos[:, None], doc_ends[None, :], 0), axis=1
    )
    low_first = jnp.max(jnp.where(doc_ends <= s * BLOCK, doc_ends, 0))
    low_last = jnp.max(jnp.where(doc_ends <= s * BLOCK + BLOCK - 1, doc_ends, 0))
    bounds = jnp.tile(
        jnp.concatenate([low[None], query_pos[None], jnp.zeros((6, BLOCK), jnp.int32)], axis=0),
        (1, HEADS),
    )

    def rows_of(steps):
        return [jnp.where(core == 0, row - k, row - 9 + k) for k in steps]

    def bases_1(shift):
        at = (col - shift) % ROW
        own = (row * ROW + at) * BLOCK + core * (BLOCK // 2)
        return [own] + [(r * ROW + at) * BLOCK for r in rows_of((1, 2))]

    def bases_2(shift):
        at = (col - shift) % ROW
        return [(r * ROW + at) * BLOCK for r in rows_of((3, 4))]

    def scalars_of(bases, sizes):
        none, whole = True, True
        for base, size in zip(bases, sizes):
            none = none & ((base < 0) | (low_first >= base + size) | (base >= (s + 1) * BLOCK))
            whole = whole & (base >= 0) & (low_last <= base) & (base + size <= s * BLOCK)
        mode = jnp.where(none, 0, jnp.where(whole, 1, 2))
        return jnp.stack([mode] + bases).astype(jnp.int32)

    sizes_1, sizes_2 = [BLOCK // 2, BLOCK, BLOCK], [BLOCK, BLOCK]

    columns = out_weight.shape[1] // TENSOR

    def weight_of(to_hi, to_core):
        return lax.dynamic_slice_in_dim(out_weight, (2 * to_hi + to_core) * columns, columns, 1)

    far_base = jnp.where((core == 0) & (col == 0) & (s >= 33), (s - 33) * BLOCK, NOWHERE)
    state = attend(
        scalars_of([far_base] + bases_1(0) + bases_2(0), [BLOCK] + sizes_1 + sizes_2),
        q_all,
        bounds,
        [far, half] + near,
    )
    send_own, keep_own = weight_of(1 - hi, core), weight_of(hi, core)
    send_other = permute(weight_of(1 - hi, 1 - core), other_core)
    keep_other = permute(weight_of(hi, 1 - core), other_core)
    group_2, send_own, keep_own, send_other, keep_other, state = lax.optimization_barrier(
        (group_2, send_own, keep_own, send_other, keep_other, state)
    )
    columns_2 = [permute(group_2, in_row(shift)) for shift in shifts]
    for shift, keys in zip(shifts, columns_1):
        state = attend(scalars_of(bases_1(shift), sizes_1), q_all, bounds, [keys], state, sizes_1)
    state = attend(
        scalars_of(bases_2(1) + bases_2(-1), sizes_2 * 2), q_all, bounds, columns_2[:2], state, sizes_2 * 2
    )
    state = attend(scalars_of(bases_2(2), sizes_2), q_all, bounds, columns_2[2:], state, sizes_2)

    attended = merge(state, permute(state, other_core))

    pieces = ((0, 512), (512, 512), (1024, 512), (1536, 512))
    received = []
    for first, width in pieces:
        partial = project(attended, send_own, send_other, first, width, jnp.bfloat16)
        received.append(permute(partial, other_hi))
    kept = project(attended, keep_own, keep_other, 0, columns, jnp.float32)
    out = None
    for (first, _), piece in zip(pieces, received):
        out = finish(kept, piece, first, out)
    return out


def solution(mesh):
    return jax.shard_map(
        body,
        mesh=mesh,
        in_specs=(
            P("seq", "tensor"),
            P("seq", None, None),
            P("seq", None, None),
            P(),
            P("tensor", None),
        ),
        out_specs=P("seq", "tensor"),
        check_vma=False,
    )
```

profile of v0, /device:TPU:102, one launch (start us, length us, event | category | flops | bytes accessed | tf_op | source)
XLA Modules:
  0.0 145.7 jit_solution(10750326038653919656)
XLA Ops:
  0.0 6.8 %constant_dynamic-slice_fusion.1 = (bf16[512,2048]{1,0:T(8,128)(2,1)}, bf16[512,2048]{1,0:T(8,128)(2,1)}, bf16[512,2048]{1,0:T(8,128)(2,1)S(1)}, bf16[512,2048]{1,0:T(8,128)(2,1)}) fusion(bf16[512,8192]{1,0:T(8,128)(2,1)} %param.9, s32[]{:T(128)S(6)} %select_n.155, s32[]{:T(128)S(6)} %select_n.153, s32[]{:T(128)S(6)} %select_n.152, s32[]{:T(128)S(6)} %select_n.154), kind=kLoop, calls=%fused_computation.20 | loop fusion | bytes 16777232 | tf_op jit(solution)/shard_map/dynamic_slice | solution.py:312
  8.2 0.8 pad_maximum_fusion.3
  9.0 5.9 %collective-permute-start.1 = (bf16[256,256]{1,0:T(8,128)(2,1)}, bf16[256,256]{1,0:T(8,128)(2,1)S(1)}, u32[]{:S(2)}, u32[]{:S(2)}) collective-permute-start(bf16[256,256]{1,0:T(8,128)(2,1)} %pad_maximum_fusion.3), channel_id=1, source_target_pairs={{0,48},{1,97},{2,50},{3,99},{4,52},{5,101},{6,54},{7,103},{8,56},{... | collective-permute-start | bytes 393224 | tf_op jit(solution)/shard_map/ppermute | solution.py:44
  14.9 2.9 %collective-permute-start.6 = (bf16[256,256]{1,0:T(8,128)(2,1)}, bf16[256,256]{1,0:T(8,128)(2,1)S(1)}, u32[]{:S(2)}, u32[]{:S(2)}) collective-permute-start(bf16[256,256]{1,0:T(8,128)(2,1)} %pad_maximum_fusion.3), channel_id=1, source_target_pairs={{0,16},{1,129},{2,18},{3,131},{4,20},{5,133},{6,22},{7,135},{8,24}... | collective-permute-start | bytes 393224 | tf_op jit(solution)/shard_map/ppermute | solution.py:44
  17.9 1.9 %collective-permute-start.7 = (bf16[256,256]{1,0:T(8,128)(2,1)}, bf16[256,256]{1,0:T(8,128)(2,1)S(1)}, u32[]{:S(2)}, u32[]{:S(2)}) collective-permute-start(bf16[256,256]{1,0:T(8,128)(2,1)} %pad_maximum_fusion.3), channel_id=1, source_target_pairs={{0,32},{1,113},{2,34},{3,115},{4,36},{5,117},{6,38},{7,119},{8,40}... | collective-permute-start | bytes 393224 | tf_op jit(solution)/shard_map/ppermute | solution.py:44
  20.4 1.3 fusion.4
  21.6 1.2 copy.38
  22.9 1.2 copy.39
  25.0 0.8 constant_dynamic-slice_fusion.rest_1_
  39.7 4.7 %collective-permute-start.2 = (bf16[256,256]{1,0:T(8,128)(2,1)}, bf16[256,256]{1,0:T(8,128)(2,1)S(1)}, u32[]{:S(2)}, u32[]{:S(2)}) collective-permute-start(bf16[256,256]{1,0:T(8,128)(2,1)} %pad_maximum_fusion.3), channel_id=1, source_target_pairs={{0,64},{1,81},{2,66},{3,83},{4,68},{5,85},{6,70},{7,87},{8,72},{9,... | collective-permute-start | bytes 393224 | tf_op jit(solution)/shard_map/ppermute | solution.py:44
  44.4 0.8 pad_maximum_fusion
  45.1 1.6 %collective-permute-start.13 = (bf16[640,256]{1,0:T(8,128)(2,1)}, bf16[640,256]{1,0:T(8,128)(2,1)S(1)}, u32[]{:S(2)}, u32[]{:S(2)}) collective-permute-start(bf16[640,256]{1,0:T(8,128)(2,1)} %pad_maximum_fusion), channel_id=1, source_target_pairs={{0,4},{1,5},{2,6},{3,7},{4,8},{5,9},{6,10},{7,11},{8,12},{9,13},{1... | collective-permute-start | bytes 983048 | tf_op jit(solution)/shard_map/ppermute | solution.py:44
  46.8 7.6 %collective-permute-done.2.rest_5_ = bf16[256,256]{1,0:T(8,128)(2,1)S(1)} collective-permute-done((bf16[256,256]{1,0:T(8,128)(2,1)}, bf16[256,256]{1,0:T(8,128)(2,1)S(1)}, u32[]{:S(2)}, u32[]{:S(2)}) %collective-permute-start.2) | collective-permute-done | bytes 131104 | tf_op jit(solution)/shard_map/ppermute | solution.py:44
  54.4 1.3 collective-permute-start.5
  55.7 0.7 pad_maximum_fusion.2
  56.5 2.4 %collective-permute-start.12 = (bf16[640,256]{1,0:T(8,128)(2,1)}, bf16[640,256]{1,0:T(8,128)(2,1)}, u32[]{:S(2)}, u32[]{:S(2)}) collective-permute-start(bf16[640,256]{1,0:T(8,128)(2,1)} %pad_maximum_fusion), channel_id=1, source_target_pairs={{0,12},{1,13},{2,14},{3,15},{4,0},{5,1},{6,2},{7,3},{8,4},{9,5},{1... | collective-permute-start | bytes 983048 | tf_op jit(solution)/shard_map/ppermute | solution.py:44
  58.9 0.8 copy-done
  59.7 4.8 %collective-permute-done.5.rest_0_ = bf16[256,256]{1,0:T(8,128)(2,1)S(1)} collective-permute-done((bf16[256,256]{1,0:T(8,128)(2,1)}, bf16[256,256]{1,0:T(8,128)(2,1)S(1)}, u32[]{:S(2)}, u32[]{:S(2)}) %collective-permute-start.5) | collective-permute-done | bytes 131104 | tf_op jit(solution)/shard_map/ppermute | solution.py:44
  64.5 1.0 copy-done.1
  65.6 0.9 copy-done.5
  66.5 0.9 copy-done.7
  67.4 5.7 %attend.6.rest_1_ = f32[136,2048]{1,0:T(8,128)S(1)} custom-call(s32[7]{0:T(128)S(1)} %stack.110.scalars, bf16[128,2048]{1,0:T(8,128)(2,1)S(1)} %copy-done.1, s32[8,2048]{1,0:T(8,128)S(1)} %bitcast.44, bf16[256,256]{1,0:T(8,128)(2,1)S(1)} %collective-permute-done.5.rest_0_, bf16[128,256]{1,0:T(8,128)(2,1)S(1)} %constant_dynamic-slice_fusion.rest_1_, ...), custom_call_target="tpu_custom_call" | custom-call | flops 1 | bytes 1 | tf_op jit(solution)/shard_map/attend/pallas_call | solution.py:163
  73.3 2.0 %collective-permute-start.9 = (bf16[512,256]{1,0:T(8,128)(2,1)}, bf16[512,256]{1,0:T(8,128)(2,1)}, u32[]{:S(2)}, u32[]{:S(2)}) collective-permute-start(bf16[512,256]{1,0:T(8,128)(2,1)} %pad_maximum_fusion.2), channel_id=1, source_target_pairs={{0,4},{1,5},{2,6},{3,7},{4,8},{5,9},{6,10},{7,11},{8,12},{9,13},{1... | collective-permute-start | bytes 786440 | tf_op jit(solution)/shard_map/ppermute | solution.py:44
  75.3 0.7 copy-done.8
  76.0 3.5 %collective-permute-start.8 = (bf16[512,256]{1,0:T(8,128)(2,1)}, bf16[512,256]{1,0:T(8,128)(2,1)S(1)}, u32[]{:S(2)}, u32[]{:S(2)}) collective-permute-start(bf16[512,256]{1,0:T(8,128)(2,1)} %pad_maximum_fusion.2), channel_id=1, source_target_pairs={{0,8},{1,9},{2,10},{3,11},{4,12},{5,13},{6,14},{7,15},{8,0},{9,1},... | collective-permute-start | bytes 786440 | tf_op jit(solution)/shard_map/ppermute | solution.py:44
  91.8 1.0 copy-done.2
  92.9 1.0 copy-done.9
  93.9 3.3 %attend.7.rest_1_ = f32[136,2048]{1,0:T(8,128)S(1)} custom-call(s32[4]{0:T(128)S(1)} %pad_add_fusion.3.scalars, bf16[128,2048]{1,0:T(8,128)(2,1)S(1)} %copy-done.2, s32[8,2048]{1,0:T(8,128)S(1)} %bitcast.45, bf16[640,256]{1,0:T(8,128)(2,1)S(1)} %copy-done.9, f32[136,2048]{1,0:T(8,128)S(1)} %attend.6.rest_1_), custom_call_target="tpu_custom_call", output_to_operand_aliasing={{}: (4, {})} | custom-call | flops 1 | bytes 1 | tf_op jit(solution)/shard_map/attend/pallas_call | solution.py:163
  97.2 3.8 %attend.8.rest_1_ = f32[136,2048]{1,0:T(8,128)S(1)} custom-call(s32[4]{0:T(128)S(1)} %pad_add_fusion.2.scalars, bf16[128,2048]{1,0:T(8,128)(2,1)S(1)} %copy-done.2, s32[8,2048]{1,0:T(8,128)S(1)} %bitcast.46, bf16[640,256]{1,0:T(8,128)(2,1)} %collective-permute-done.12.rest_0_, f32[136,2048]{1,0:T(8,128)S(1)} %attend.7.rest_1_), custom_call_target="tpu_custom_call", output_to_operand_aliasing={{}: (4, {})} | custom-call | flops 1 | bytes 1 | tf_op jit(solution)/shard_map/attend/pallas_call | solution.py:163
  101.0 3.7 %attend.9.rest_2_ = f32[136,2048]{1,0:T(8,128)S(1)} custom-call(s32[4]{0:T(128)S(1)} %pad_add_fusion.1.scalars, bf16[128,2048]{1,0:T(8,128)(2,1)S(1)} %copy-done.2, s32[8,2048]{1,0:T(8,128)S(1)} %bitcast.47, bf16[640,256]{1,0:T(8,128)(2,1)} %collective-permute-done.11.rest_0_, f32[136,2048]{1,0:T(8,128)S(1)} %attend.8.rest_1_), custom_call_target="tpu_custom_call", output_to_operand_aliasing={{}: (4, {})} | custom-call | flops 1 | bytes 1 | tf_op jit(solution)/shard_map/attend/pallas_call | solution.py:163
  104.8 5.1 %attend.10.rest_1_ = f32[136,2048]{1,0:T(8,128)S(1)} custom-call(s32[5]{0:T(128)S(1)} %stack.116.scalars, bf16[128,2048]{1,0:T(8,128)(2,1)S(1)} %copy-done.2, s32[8,2048]{1,0:T(8,128)S(1)} %bitcast.48, bf16[512,256]{1,0:T(8,128)(2,1)} %collective-permute-done.9.rest_0_, ...), custom_call_target="tpu_custom_call", output_to_operand_aliasing={{}: (5, {})} | custom-call | flops 1 | bytes 1 | tf_op jit(solution)/shard_map/attend/pallas_call | solution.py:163
  109.9 3.1 %attend.11.mine = f32[136,2048]{1,0:T(8,128)S(1)} custom-call(s32[3]{0:T(128)S(1)} %pad_add_fusion.scalars, bf16[128,2048]{1,0:T(8,128)(2,1)S(1)} %copy-done.2, s32[8,2048]{1,0:T(8,128)S(1)} %bitcast.49, bf16[512,256]{1,0:T(8,128)(2,1)S(1)} %collective-permute-done.8.rest_0_, f32[136,2048]{1,0:T(8,128)S(1)} %attend.10.rest_1_), custom_call_target="tpu_custom_call", output_to_operand_aliasing={{}: (4, {})} | custom-call | flops 1 | bytes 1 | tf_op jit(solution)/shard_map/attend/pallas_call | solution.py:163
  113.1 2.7 %collective-permute-done.14.theirs = f32[136,2048]{1,0:T(8,128)S(1)} collective-permute-done((f32[136,2048]{1,0:T(8,128)S(1)}, f32[136,2048]{1,0:T(8,128)S(1)}, u32[]{:S(2)}, u32[]{:S(2)}) %collective-permute-start.14) | collective-permute-done | bytes 1114144 | tf_op jit(solution)/shard_map/ppermute | solution.py:44
  116.1 2.0 %project.9 = bf16[256,512]{1,0:T(8,128)(2,1)S(1)} custom-call(bf16[256,1024]{1,0:T(8,128)(2,1)S(1)} %merge.1.attended, bf16[512,2048]{1,0:T(8,128)(2,1)S(1)} %get-tuple-element.15.own_weight, bf16[512,2048]{1,0:T(8,128)(2,1)} %collective-permute-done.3.other_weight), custom_call_target="tpu_custom_call" | custom-call | flops 1 | bytes 1 | tf_op jit(solution)/shard_map/project/pallas_call | solution.py:210
  118.1 1.5 %collective-permute-start.18 = (bf16[256,512]{1,0:T(8,128)(2,1)S(1)}, bf16[256,512]{1,0:T(8,128)(2,1)S(1)}, u32[]{:S(2)}, u32[]{:S(2)}) collective-permute-start(bf16[256,512]{1,0:T(8,128)(2,1)S(1)} %project.9), channel_id=1, source_target_pairs={{0,2},{1,3},{2,0},{3,1},{4,6},{5,7},{6,4},{7,5},{8,10},{9,11},{10,... | collective-permute-start | bytes 786440 | tf_op jit(solution)/shard_map/ppermute | solution.py:44
  119.6 2.0 %project.8 = bf16[256,512]{1,0:T(8,128)(2,1)S(1)} custom-call(bf16[256,1024]{1,0:T(8,128)(2,1)S(1)} %merge.1.attended, bf16[512,2048]{1,0:T(8,128)(2,1)S(1)} %get-tuple-element.15.own_weight, bf16[512,2048]{1,0:T(8,128)(2,1)} %collective-permute-done.3.other_weight), custom_call_target="tpu_custom_call" | custom-call | flops 1 | bytes 1 | tf_op jit(solution)/shard_map/project/pallas_call | solution.py:210
  121.6 2.2 %collective-permute-start.17 = (bf16[256,512]{1,0:T(8,128)(2,1)S(1)}, bf16[256,512]{1,0:T(8,128)(2,1)S(1)}, u32[]{:S(2)}, u32[]{:S(2)}) collective-permute-start(bf16[256,512]{1,0:T(8,128)(2,1)S(1)} %project.8), channel_id=1, source_target_pairs={{0,2},{1,3},{2,0},{3,1},{4,6},{5,7},{6,4},{7,5},{8,10},{9,11},{10,... | collective-permute-start | bytes 786440 | tf_op jit(solution)/shard_map/ppermute | solution.py:44
  123.9 2.0 %project.7 = bf16[256,512]{1,0:T(8,128)(2,1)S(1)} custom-call(bf16[256,1024]{1,0:T(8,128)(2,1)S(1)} %merge.1.attended, bf16[512,2048]{1,0:T(8,128)(2,1)S(1)} %get-tuple-element.15.own_weight, bf16[512,2048]{1,0:T(8,128)(2,1)} %collective-permute-done.3.other_weight), custom_call_target="tpu_custom_call" | custom-call | flops 1 | bytes 1 | tf_op jit(solution)/shard_map/project/pallas_call | solution.py:210
  125.9 1.5 %collective-permute-start.16 = (bf16[256,512]{1,0:T(8,128)(2,1)S(1)}, bf16[256,512]{1,0:T(8,128)(2,1)S(1)}, u32[]{:S(2)}, u32[]{:S(2)}) collective-permute-start(bf16[256,512]{1,0:T(8,128)(2,1)S(1)} %project.7), channel_id=1, source_target_pairs={{0,2},{1,3},{2,0},{3,1},{4,6},{5,7},{6,4},{7,5},{8,10},{9,11},{10,... | collective-permute-start | bytes 786440 | tf_op jit(solution)/shard_map/ppermute | solution.py:44
  127.4 2.0 %project.6 = bf16[256,512]{1,0:T(8,128)(2,1)S(1)} custom-call(bf16[256,1024]{1,0:T(8,128)(2,1)S(1)} %merge.1.attended, bf16[512,2048]{1,0:T(8,128)(2,1)S(1)} %get-tuple-element.15.own_weight, bf16[512,2048]{1,0:T(8,128)(2,1)} %collective-permute-done.3.other_weight), custom_call_target="tpu_custom_call" | custom-call | flops 1 | bytes 1 | tf_op jit(solution)/shard_map/project/pallas_call | solution.py:210
  129.4 2.2 %collective-permute-start.15 = (bf16[256,512]{1,0:T(8,128)(2,1)S(1)}, bf16[256,512]{1,0:T(8,128)(2,1)S(1)}, u32[]{:S(2)}, u32[]{:S(2)}) collective-permute-start(bf16[256,512]{1,0:T(8,128)(2,1)S(1)} %project.6), channel_id=1, source_target_pairs={{0,2},{1,3},{2,0},{3,1},{4,6},{5,7},{6,4},{7,5},{8,10},{9,11},{10,... | collective-permute-start | bytes 786440 | tf_op jit(solution)/shard_map/ppermute | solution.py:44
  131.6 2.8 %project.5.kept = f32[256,2048]{1,0:T(8,128)S(1)} custom-call(bf16[256,1024]{1,0:T(8,128)(2,1)S(1)} %merge.1.attended, bf16[512,2048]{1,0:T(8,128)(2,1)S(1)} %copy-done.3, bf16[512,2048]{1,0:T(8,128)(2,1)} %collective-permute-done.4.other_weight), custom_call_target="tpu_custom_call" | custom-call | flops 1 | bytes 1 | tf_op jit(solution)/shard_map/project/pallas_call | solution.py:210
  134.5 0.7 finish.4.rest_0_
  135.2 0.7 finish.5.rest_0_
  136.0 4.1 %collective-permute-done.16.received = bf16[256,512]{1,0:T(8,128)(2,1)S(1)} collective-permute-done((bf16[256,512]{1,0:T(8,128)(2,1)S(1)}, bf16[256,512]{1,0:T(8,128)(2,1)S(1)}, u32[]{:S(2)}, u32[]{:S(2)}) %collective-permute-start.16) | collective-permute-done | bytes 262176 | tf_op jit(solution)/shard_map/ppermute | solution.py:44
  140.1 0.7 finish.6.rest_0_
  140.8 4.1 %collective-permute-done.15.received = bf16[256,512]{1,0:T(8,128)(2,1)S(1)} collective-permute-done((bf16[256,512]{1,0:T(8,128)(2,1)S(1)}, bf16[256,512]{1,0:T(8,128)(2,1)S(1)}, u32[]{:S(2)}, u32[]{:S(2)}) %collective-permute-start.15) | collective-permute-done | bytes 262176 | tf_op jit(solution)/shard_map/ppermute | solution.py:44
  144.9 0.7 finish.7
  (70 shorter events, 4.3 us)
Async XLA Ops:
  0.0 7.3 %copy-start.11 = (bf16[256,2,128]{2,1,0:T(2,128)(2,1)S(1)}, bf16[256,2,128]{2,1,0:T(2,128)(2,1)}, u32[]{:S(2)}) copy-start(bf16[256,2,128]{2,1,0:T(2,128)(2,1)} %param.7) | copy-start | bytes 393220
  0.0 7.3 %copy-start.12 = (bf16[256,2,128]{2,1,0:T(2,128)(2,1)S(1)}, bf16[256,2,128]{2,1,0:T(2,128)(2,1)}, u32[]{:S(2)}) copy-start(bf16[256,2,128]{2,1,0:T(2,128)(2,1)} %param.6) | copy-start | bytes 393220
  0.0 19.8 %copy-start.13 = (s32[8]{0:T(128)S(1)}, s32[8]{0:T(128)}, u32[]{:S(2)}) copy-start(s32[8]{0:T(128)} %param.8) | copy-start | bytes 100
  6.8 13.4 %copy-start.10 = (bf16[256,512]{1,0:T(8,128)(2,1)S(1)}, bf16[256,512]{1,0:T(8,128)(2,1)}, u32[]{:S(2)}) copy-start(bf16[256,512]{1,0:T(8,128)(2,1)} %param.5) | copy-start | bytes 786436
  6.8 66.4 %collective-permute-start.3 = (bf16[512,2048]{1,0:T(8,128)(2,1)}, bf16[512,2048]{1,0:T(8,128)(2,1)}, u32[]{:S(2)}, u32[]{:S(2)}) collective-permute-start(bf16[512,2048]{1,0:T(8,128)(2,1)} %get-tuple-element.22), channel_id=1, source_target_pairs={{0,1},{1,0},{2,3},{3,2},{4,5},{5,4},{6,7},{7,6},{8,9},{9,8},{10,11... | collective-permute-start | bytes 6291464 | tf_op jit(solution)/shard_map/ppermute | solution.py:44
  6.8 66.4 %collective-permute-start.4 = (bf16[512,2048]{1,0:T(8,128)(2,1)}, bf16[512,2048]{1,0:T(8,128)(2,1)}, u32[]{:S(2)}, u32[]{:S(2)}) collective-permute-start(bf16[512,2048]{1,0:T(8,128)(2,1)} %get-tuple-element.19), channel_id=1, source_target_pairs={{0,1},{1,0},{2,3},{3,2},{4,5},{5,4},{6,7},{7,6},{8,9},{9,8},{10,11... | collective-permute-start | bytes 6291464 | tf_op jit(solution)/shard_map/ppermute | solution.py:44
  9.0 36.1 %collective-permute-start.1 = (bf16[256,256]{1,0:T(8,128)(2,1)}, bf16[256,256]{1,0:T(8,128)(2,1)S(1)}, u32[]{:S(2)}, u32[]{:S(2)}) collective-permute-start(bf16[256,256]{1,0:T(8,128)(2,1)} %pad_maximum_fusion.3), channel_id=1, source_target_pairs={{0,48},{1,97},{2,50},{3,99},{4,52},{5,101},{6,54},{7,103},{8,56},{... | collective-permute-start | bytes 393224 | tf_op jit(solution)/shard_map/ppermute | solution.py:44
  14.9 24.7 %collective-permute-start.6 = (bf16[256,256]{1,0:T(8,128)(2,1)}, bf16[256,256]{1,0:T(8,128)(2,1)S(1)}, u32[]{:S(2)}, u32[]{:S(2)}) collective-permute-start(bf16[256,256]{1,0:T(8,128)(2,1)} %pad_maximum_fusion.3), channel_id=1, source_target_pairs={{0,16},{1,129},{2,18},{3,131},{4,20},{5,133},{6,22},{7,135},{8,24}... | collective-permute-start | bytes 393224 | tf_op jit(solution)/shard_map/ppermute | solution.py:44
  17.9 21.8 %collective-permute-start.7 = (bf16[256,256]{1,0:T(8,128)(2,1)}, bf16[256,256]{1,0:T(8,128)(2,1)S(1)}, u32[]{:S(2)}, u32[]{:S(2)}) collective-permute-start(bf16[256,256]{1,0:T(8,128)(2,1)} %pad_maximum_fusion.3), channel_id=1, source_target_pairs={{0,32},{1,113},{2,34},{3,115},{4,36},{5,117},{6,38},{7,119},{8,40}... | collective-permute-start | bytes 393224 | tf_op jit(solution)/shard_map/ppermute | solution.py:44
  39.6 16.8 %collective-permute-start = (bf16[128,1024]{1,0:T(8,128)(2,1)S(1)}, bf16[128,1024]{1,0:T(8,128)(2,1)S(1)}, u32[]{:S(2)}, u32[]{:S(2)}) collective-permute-start(bf16[128,1024]{1,0:T(8,128)(2,1)S(1)} %bitcast.51), channel_id=1, source_target_pairs={{0,1},{1,0},{2,3},{3,2},{4,5},{5,4},{6,7},{7,6},{8,9},{9,8},{10,11... | collective-permute-start | bytes 786440 | tf_op jit(solution)/shard_map/ppermute | solution.py:44
  39.7 24.8 %copy-start.4 = (bf16[256,256]{1,0:T(8,128)(2,1)}, bf16[256,256]{1,0:T(8,128)(2,1)S(1)}, u32[]{:S(2)}) copy-start(bf16[256,256]{1,0:T(8,128)(2,1)S(1)} %collective-permute-done.7.rest_3_) | copy-start | bytes 393220
  39.7 14.7 %collective-permute-start.2 = (bf16[256,256]{1,0:T(8,128)(2,1)}, bf16[256,256]{1,0:T(8,128)(2,1)S(1)}, u32[]{:S(2)}, u32[]{:S(2)}) collective-permute-start(bf16[256,256]{1,0:T(8,128)(2,1)} %pad_maximum_fusion.3), channel_id=1, source_target_pairs={{0,64},{1,81},{2,66},{3,83},{4,68},{5,85},{6,70},{7,87},{8,72},{9,... | collective-permute-start | bytes 393224 | tf_op jit(solution)/shard_map/ppermute | solution.py:44
  45.1 19.4 %copy-start.6 = (bf16[256,256]{1,0:T(8,128)(2,1)}, bf16[256,256]{1,0:T(8,128)(2,1)S(1)}, u32[]{:S(2)}) copy-start(bf16[256,256]{1,0:T(8,128)(2,1)S(1)} %collective-permute-done.1.rest_4_) | copy-start | bytes 393220
  45.1 30.1 %collective-permute-start.13 = (bf16[640,256]{1,0:T(8,128)(2,1)}, bf16[640,256]{1,0:T(8,128)(2,1)S(1)}, u32[]{:S(2)}, u32[]{:S(2)}) collective-permute-start(bf16[640,256]{1,0:T(8,128)(2,1)} %pad_maximum_fusion), channel_id=1, source_target_pairs={{0,4},{1,5},{2,6},{3,7},{4,8},{5,9},{6,10},{7,11},{8,12},{9,13},{1... | collective-permute-start | bytes 983048 | tf_op jit(solution)/shard_map/ppermute | solution.py:44
  54.4 10.1 %collective-permute-start.5 = (bf16[256,256]{1,0:T(8,128)(2,1)}, bf16[256,256]{1,0:T(8,128)(2,1)S(1)}, u32[]{:S(2)}, u32[]{:S(2)}) collective-permute-start(bf16[256,256]{1,0:T(8,128)(2,1)} %pad_maximum_fusion.3), channel_id=1, source_target_pairs={{12,144},{14,146},{28,160},{30,162},{44,176},{46,178},{60,192},{62... | collective-permute-start | bytes 393224 | tf_op jit(solution)/shard_map/ppermute | solution.py:44
  56.5 40.7 %collective-permute-start.12 = (bf16[640,256]{1,0:T(8,128)(2,1)}, bf16[640,256]{1,0:T(8,128)(2,1)}, u32[]{:S(2)}, u32[]{:S(2)}) collective-permute-start(bf16[640,256]{1,0:T(8,128)(2,1)} %pad_maximum_fusion), channel_id=1, source_target_pairs={{0,12},{1,13},{2,14},{3,15},{4,0},{5,1},{6,2},{7,3},{8,4},{9,5},{1... | collective-permute-start | bytes 983048 | tf_op jit(solution)/shard_map/ppermute | solution.py:44
  58.9 0.8 copy-start
  64.5 36.5 %collective-permute-start.11 = (bf16[640,256]{1,0:T(8,128)(2,1)}, bf16[640,256]{1,0:T(8,128)(2,1)}, u32[]{:S(2)}, u32[]{:S(2)}) collective-permute-start(bf16[640,256]{1,0:T(8,128)(2,1)} %pad_maximum_fusion), channel_id=1, source_target_pairs={{0,8},{1,9},{2,10},{3,11},{4,12},{5,13},{6,14},{7,15},{8,0},{9,1},... | collective-permute-start | bytes 983048 | tf_op jit(solution)/shard_map/ppermute | solution.py:44
  64.5 1.0 copy-start.1
  65.6 0.9 copy-start.5
  66.5 0.9 copy-start.7
  73.2 31.6 %collective-permute-start.10 = (bf16[512,256]{1,0:T(8,128)(2,1)}, bf16[512,256]{1,0:T(8,128)(2,1)}, u32[]{:S(2)}, u32[]{:S(2)}) collective-permute-start(bf16[512,256]{1,0:T(8,128)(2,1)} %pad_maximum_fusion.2), channel_id=1, source_target_pairs={{0,12},{1,13},{2,14},{3,15},{4,0},{5,1},{6,2},{7,3},{8,4},{9,5},{1... | collective-permute-start | bytes 786440 | tf_op jit(solution)/shard_map/ppermute | solution.py:44
  73.3 31.5 %collective-permute-start.9 = (bf16[512,256]{1,0:T(8,128)(2,1)}, bf16[512,256]{1,0:T(8,128)(2,1)}, u32[]{:S(2)}, u32[]{:S(2)}) collective-permute-start(bf16[512,256]{1,0:T(8,128)(2,1)} %pad_maximum_fusion.2), channel_id=1, source_target_pairs={{0,4},{1,5},{2,6},{3,7},{4,8},{5,9},{6,10},{7,11},{8,12},{9,13},{1... | collective-permute-start | bytes 786440 | tf_op jit(solution)/shard_map/ppermute | solution.py:44
  75.3 0.7 copy-start.8
  76.0 33.8 %collective-permute-start.8 = (bf16[512,256]{1,0:T(8,128)(2,1)}, bf16[512,256]{1,0:T(8,128)(2,1)S(1)}, u32[]{:S(2)}, u32[]{:S(2)}) collective-permute-start(bf16[512,256]{1,0:T(8,128)(2,1)} %pad_maximum_fusion.2), channel_id=1, source_target_pairs={{0,8},{1,9},{2,10},{3,11},{4,12},{5,13},{6,14},{7,15},{8,0},{9,1},... | collective-permute-start | bytes 786440 | tf_op jit(solution)/shard_map/ppermute | solution.py:44
  91.8 1.0 copy-start.2
  92.9 1.0 copy-start.9
  113.0 2.8 %collective-permute-start.14 = (f32[136,2048]{1,0:T(8,128)S(1)}, f32[136,2048]{1,0:T(8,128)S(1)}, u32[]{:S(2)}, u32[]{:S(2)}) collective-permute-start(f32[136,2048]{1,0:T(8,128)S(1)} %attend.11.mine), channel_id=1, source_target_pairs={{0,1},{1,0},{2,3},{3,2},{4,5},{5,4},{6,7},{7,6},{8,9},{9,8},{10,11... | collective-permute-start | bytes 3342344 | tf_op jit(solution)/shard_map/ppermute | solution.py:44
  118.1 16.4 %collective-permute-start.18 = (bf16[256,512]{1,0:T(8,128)(2,1)S(1)}, bf16[256,512]{1,0:T(8,128)(2,1)S(1)}, u32[]{:S(2)}, u32[]{:S(2)}) collective-permute-start(bf16[256,512]{1,0:T(8,128)(2,1)S(1)} %project.9), channel_id=1, source_target_pairs={{0,2},{1,3},{2,0},{3,1},{4,6},{5,7},{6,4},{7,5},{8,10},{9,11},{10,... | collective-permute-start | bytes 786440 | tf_op jit(solution)/shard_map/ppermute | solution.py:44
  121.6 13.6 %collective-permute-start.17 = (bf16[256,512]{1,0:T(8,128)(2,1)S(1)}, bf16[256,512]{1,0:T(8,128)(2,1)S(1)}, u32[]{:S(2)}, u32[]{:S(2)}) collective-permute-start(bf16[256,512]{1,0:T(8,128)(2,1)S(1)} %project.8), channel_id=1, source_target_pairs={{0,2},{1,3},{2,0},{3,1},{4,6},{5,7},{6,4},{7,5},{8,10},{9,11},{10,... | collective-permute-start | bytes 786440 | tf_op jit(solution)/shard_map/ppermute | solution.py:44
  125.9 5.7 %copy-start.3 = (bf16[512,2048]{1,0:T(8,128)(2,1)S(1)}, bf16[512,2048]{1,0:T(8,128)(2,1)}, u32[]{:S(2)}) copy-start(bf16[512,2048]{1,0:T(8,128)(2,1)} %get-tuple-element.13.own_weight) | copy-start | bytes 6291460
  125.9 14.2 %collective-permute-start.16 = (bf16[256,512]{1,0:T(8,128)(2,1)S(1)}, bf16[256,512]{1,0:T(8,128)(2,1)S(1)}, u32[]{:S(2)}, u32[]{:S(2)}) collective-permute-start(bf16[256,512]{1,0:T(8,128)(2,1)S(1)} %project.7), channel_id=1, source_target_pairs={{0,2},{1,3},{2,0},{3,1},{4,6},{5,7},{6,4},{7,5},{8,10},{9,11},{10,... | collective-permute-start | bytes 786440 | tf_op jit(solution)/shard_map/ppermute | solution.py:44
  129.4 15.5 %collective-permute-start.15 = (bf16[256,512]{1,0:T(8,128)(2,1)S(1)}, bf16[256,512]{1,0:T(8,128)(2,1)S(1)}, u32[]{:S(2)}, u32[]{:S(2)}) collective-permute-start(bf16[256,512]{1,0:T(8,128)(2,1)S(1)} %project.6), channel_id=1, source_target_pairs={{0,2},{1,3},{2,0},{3,1},{4,6},{5,7},{6,4},{7,5},{8,10},{9,11},{10,... | collective-permute-start | bytes 786440 | tf_op jit(solution)/shard_map/ppermute | solution.py:44
where the time goes:
time: 147 us; the launch traced here: 146 us
  Pallas kernels  38.9 us (26%)
  starting transfers between devices  34.4 us (23%)
  between operations  25.7 us (17%)
  waiting for transfers between devices  23.5 us (16%)
  local copies, waits for them, and re-layouts  18.7 us (13%)
  other arithmetic  4.45 us (3%)
    ppermute x19, starting transfers between devices, permute(): return lax.ppermute(x, ('seq', 'tensor'), device_perm(move))  34.4 us
    pallas_call x6, Pallas kernels, attend(): pl.pallas_call(functools.partial(attend_kernel, sizes, state is None), ou...  24.7 us
    ppermute x19, waiting for transfers between devices, permute(): return lax.ppermute(x, ('seq', 'tensor'), device_perm(move))  23.5 us
    pallas_call x5, Pallas kernels, project(): pl.pallas_call(functools.partial(project_kernel, first), out_shape=jax.Sh...  10.9 us
    unnamed x33, local copies, waits for them, and re-layouts  8.97 us
    dynamic_slice x1, local copies, waits for them, and re-layouts, weight_of(): lax.dynamic_slice_in_dim(out_weight, (2 * to_hi + to_core) * columns, col...  6.78 us
    pallas_call x4, Pallas kernels, finish(): pl.pallas_call(finish_kernel, out_shape=jax.ShapeDtypeStruct(kept.shape,...  2.99 us
  transfers between devices with their start and end apart: 19, of which 5 were waited for; matrix products, arithmetic and copies ran while one was open for 7% of the time, Pallas kernels for 23%

commit v1 on v0

v1 whole, which is shorter than its diff:
```python
import functools
import math

import jax
import jax.numpy as jnp
from jax import lax
from jax.experimental import pallas as pl
from jax.experimental.pallas import tpu as pltpu
from jax.sharding import PartitionSpec as P

HQ = 16
KVH = 2
HD = 128
SEQ = 64
TENSOR = 4
ROW = 4
THETA = 500000.0
EMPTY = -1e30
MASKED = -1e32
LOG2E = math.log2(math.e)
BLOCK = 256
ROW_TOKENS = ROW * BLOCK
HEADS = 8
LANES = HEADS * BLOCK
STATE = HD + 8
TILE = 512
WIDE = 1024
NOWHERE = 1 << 24
OUT_COLUMNS = 2048
MIB = 1024 * 1024


def device_perm(move):
    pairs = []
    for s in range(SEQ):
        for hi in range(2):
            for core in range(2):
                to = move(s, hi, core)
                if to is not None:
                    pairs.append((s * TENSOR + hi * 2 + core, to[0] * TENSOR + to[1] * 2 + to[2]))
    return pairs


def permute(x, move):
    return lax.ppermute(x, ("seq", "tensor"), device_perm(move))


def in_row(shift):
    return lambda s, hi, core: (s - s % ROW + (s + shift) % ROW, hi, core)


def other_core(s, hi, core):
    return s, hi, 1 - core


def other_hi(s, hi, core):
    return s, 1 - hi, core


def far_block(s, hi, core):
    if core == 0 and s % ROW == ROW - 1 and s + 33 < SEQ:
        return s + 33, hi, core
    return None


def along_rows(step):
    def move(s, hi, core):
        if core == 0:
            return (s + step * ROW, hi, core) if s + step * ROW < SEQ else None
        return (s + (9 - step) * ROW) % SEQ, hi, core

    return move


def rope_tables(positions):
    half = HD // 2
    exponents = jnp.arange(half, dtype=jnp.float32) * (2.0 / HD)
    inverse = jnp.power(jnp.float32(THETA), -exponents)
    angles = positions.astype(jnp.float32)[:, None] * inverse[None, :]
    return jnp.cos(angles), jnp.sin(angles)


def rope(values, cosine, sine):
    half = HD // 2
    first, second = values[..., :half], values[..., half:]
    return jnp.concatenate(
        [first * cosine - second * sine, second * cosine + first * sine], axis=-1
    )


def place(ids):
    s, t = ids[0], ids[1]
    return s, t >> 1, t & 1, s >> 2, s & 3


def part_at(ids, kind, shift):
    s, _, core, row, col = place(ids)
    at = (col + ROW - shift) & 3
    if kind == "far":
        there = (core == 0) & (col == 0) & (s >= 33)
        return jnp.where(there, (s - 33) * BLOCK, NOWHERE), BLOCK
    if kind == "half":
        return (row * ROW + at) * BLOCK + core * (BLOCK // 2), BLOCK // 2
    return (jnp.where(core == 0, row - kind, row - 9 + kind) * ROW + at) * BLOCK, BLOCK


def attend_kernel(kinds, fresh, ids, lengths, q_ref, *rest):
    state = rest[-1]
    kept, refs = (None, rest[:-1]) if fresh else (rest[-2], rest[:-2])
    scale = HD**-0.5 * LOG2E
    first_query = ids[0] * BLOCK
    ends, end = [], 0
    for i in range(lengths.shape[0]):
        end = end + lengths[i]
        ends.append(end)
    low_first, low_last = 0, 0
    for end in ends:
        low_first = jnp.where(end <= first_query, end, low_first)
        low_last = jnp.where(end <= first_query + BLOCK - 1, end, low_last)
    parts, bases, none, whole = [], [], True, True
    at, i = 0, 0
    for kind, shift in kinds:
        base, size = part_at(ids, kind, shift)
        parts.append(refs[i].at[at : at + size])
        at += size
        if at == refs[i].shape[0]:
            at, i = 0, i + 1
        bases.append(base)
        dead = (base < 0) | (low_first >= base + size) | (base >= first_query + BLOCK)
        full = (base >= 0) & (low_last <= base) & (base + size <= first_query)
        none, whole = dead & none, full & whole

    def step(lanes, masked):
        q = q_ref[:, lanes]
        if masked:
            high = lax.broadcasted_iota(jnp.int32, (1, WIDE), 1) % BLOCK + first_query
            low = jnp.zeros_like(high)
            for end in ends:
                low = jnp.where(end <= high, end, low)
        scores = []
        for part, base in zip(parts, bases):
            s = jnp.dot(part[:, :HD], q, preferred_element_type=jnp.float32)
            if masked:
                at = lax.broadcasted_iota(jnp.int32, s.shape, 0) + base
                s = jnp.where((at >= low) & (at <= high), s, MASKED)
            scores.append(s)
        s = jnp.concatenate(scores, axis=0) if len(scores) > 1 else scores[0]
        values = [part[:, HD:].T for part in parts]
        values = jnp.concatenate(values, axis=1) if len(values) > 1 else values[0]
        values = jnp.concatenate([values, jnp.ones((16, values.shape[1]), jnp.bfloat16)], axis=0)
        peak = jnp.max(s, axis=0, keepdims=True) * scale
        old = jnp.full_like(peak, EMPTY) if fresh else kept[HD : HD + 1, lanes]
        new = jnp.maximum(old, peak)
        weights = jnp.exp2(s * scale - new).astype(jnp.bfloat16)
        summed = jnp.dot(values, weights, preferred_element_type=jnp.float32)
        denom = summed[HD : HD + 1]
        summed = summed[:HD]
        if not fresh:
            alpha = jnp.exp2(old - new)
            summed = summed + kept[:HD, lanes] * alpha
            denom = denom + kept[HD + 1 : HD + 2, lanes] * alpha
        state[:HD, lanes] = summed
        state[HD:, lanes] = jnp.concatenate([new, denom, jnp.zeros((6, WIDE), jnp.float32)], axis=0)

    def steps(masked):
        def one(i, carry):
            step(pl.ds(pl.multiple_of(i * WIDE, WIDE), WIDE), masked)
            return carry

        lax.fori_loop(0, LANES // WIDE, one, 0)

    if fresh:
        steps(True)
    else:

        @pl.when(none)
        def _():
            state[...] = kept[...]

        @pl.when(whole)
        def _():
            steps(False)

        @pl.when(jnp.logical_not(none | whole))
        def _():
            steps(True)


def attend(ids, lengths, q_all, refs, kinds, state=None):
    operands = list(refs) + ([] if state is None else [state])
    return pl.pallas_call(
        functools.partial(attend_kernel, kinds, state is None),
        out_shape=jax.ShapeDtypeStruct((STATE, LANES), jnp.float32),
        in_specs=[pl.BlockSpec(memory_space=pltpu.SMEM)] * 2
        + [pl.BlockSpec(memory_space=pltpu.VMEM)] * (1 + len(operands)),
        out_specs=pl.BlockSpec(memory_space=pltpu.VMEM),
        input_output_aliases={} if state is None else {2 + len(operands): 0},
        compiler_params=pltpu.CompilerParams(vmem_limit_bytes=32 * MIB),
        cost_estimate=pl.CostEstimate(flops=1, bytes_accessed=1, transcendentals=0),
        name="attend",
    )(ids, lengths, q_all, *operands)


def turn_kernel(queries, cosine, sine, out):
    half = HD // 2
    for h in range(queries.shape[1] // HD):
        x = queries[:, h * HD : (h + 1) * HD].astype(jnp.float32)
        turned = rope(x, cosine[...], sine[...]).astype(jnp.bfloat16)
        out[:, h * BLOCK : (h + 1) * BLOCK] = turned.T


def turn(queries, cosine, sine):
    return pl.pallas_call(
        turn_kernel,
        out_shape=jax.ShapeDtypeStruct((HD, queries.shape[1] // HD * BLOCK), jnp.bfloat16),
        in_specs=[pl.BlockSpec(memory_space=pltpu.VMEM)] * 3,
        out_specs=pl.BlockSpec(memory_space=pltpu.VMEM),
        compiler_params=pltpu.CompilerParams(vmem_limit_bytes=16 * MIB),
        cost_estimate=pl.CostEstimate(flops=1, bytes_accessed=1, transcendentals=0),
        name="turn",
    )(queries, cosine, sine)


def merged(mine, theirs, out):
    for h in range(HEADS):
        a = slice(h * BLOCK, (h + 1) * BLOCK)
        g = (h + HEADS // 2) % HEADS
        b = slice(g * BLOCK, (g + 1) * BLOCK)
        peak_a, peak_b = mine[HD : HD + 1, a], theirs[HD : HD + 1, b]
        peak = jnp.maximum(peak_a, peak_b)
        scale_a, scale_b = jnp.exp2(peak_a - peak), jnp.exp2(peak_b - peak)
        denom = mine[HD + 1 : HD + 2, a] * scale_a + theirs[HD + 1 : HD + 2, b] * scale_b
        summed = mine[:HD, a] * scale_a + theirs[:HD, b] * scale_b
        out[:, h * HD : (h + 1) * HD] = (summed / denom).T.astype(jnp.bfloat16)


def project_kernel(other_side, first, merging, ids, *rest):
    half = HEADS * HD // 2
    _, hi, core, _, _ = place(ids)
    weights, sems = rest[-2:]
    if merging:
        mine, theirs, own_weight, other_weight, attended = rest[:5]
        outs = rest[5:-2]
    else:
        attended, own_weight, other_weight = rest[:3]
        outs = rest[3:-2]
    at = (2 * (1 - hi if other_side else hi) + core) * OUT_COLUMNS + first
    pieces = weights.shape[0]
    for i in range(pieces):
        columns = pl.ds(pl.multiple_of(at + i * TILE, TILE), TILE)
        for j, weight in enumerate((own_weight, other_weight)):
            pltpu.make_async_copy(weight.at[:, columns], weights.at[i, j], sems.at[i, j]).start()
    if merging:
        merged(mine, theirs, attended)
    out, filled = 0, 0
    for i in range(pieces):
        columns = pl.ds(pl.multiple_of(at + i * TILE, TILE), TILE)
        for j, weight in enumerate((own_weight, other_weight)):
            pltpu.make_async_copy(weight.at[:, columns], weights.at[i, j], sems.at[i, j]).wait()
        total = jnp.dot(attended[:, :half], weights[i, 0], preferred_element_type=jnp.float32)
        total += jnp.dot(attended[:, half:], weights[i, 1], preferred_element_type=jnp.float32)
        outs[out][:, filled : filled + TILE] = total.astype(outs[out].dtype)
        filled += TILE
        if filled == outs[out].shape[1]:
            out, filled = out + 1, 0


def project(ids, operands, weights, other_side, first, widths, dtype, merging=False):
    half = HEADS * HD // 2
    shapes = [jax.ShapeDtypeStruct((BLOCK, width), dtype) for width in widths]
    if merging:
        shapes = [jax.ShapeDtypeStruct((BLOCK, 2 * half), jnp.bfloat16)] + shapes
    pieces = sum(widths) // TILE
    vmem = pl.BlockSpec(memory_space=pltpu.VMEM)
    return pl.pallas_call(
        functools.partial(project_kernel, other_side, first, merging),
        out_shape=shapes,
        in_specs=[pl.BlockSpec(memory_space=pltpu.SMEM)]
        + [vmem] * len(operands)
        + [pl.BlockSpec(memory_space=pltpu.HBM)] * 2,
        out_specs=[vmem] * len(shapes),
        scratch_shapes=[
            pltpu.VMEM((pieces, 2, half, TILE), jnp.bfloat16),
            pltpu.SemaphoreType.DMA((pieces, 2)),
        ],
        compiler_params=pltpu.CompilerParams(vmem_limit_bytes=32 * MIB),
        cost_estimate=pl.CostEstimate(flops=1, bytes_accessed=1, transcendentals=0),
        name="project",
    )(ids, *operands, *weights)


def finish_kernel(kept, received, *rest):
    rest[-1][...] = (kept[...] + received[...].astype(jnp.float32)).astype(jnp.bfloat16)


def finish(kept, received, first, out):
    columns, start = received.shape[1], first // TILE
    tile = pl.BlockSpec((BLOCK, TILE), lambda j: (0, start + j))
    in_specs = [tile, pl.BlockSpec((BLOCK, TILE), lambda j: (0, j))]
    operands = [kept, received]
    if out is not None:
        in_specs.append(pl.BlockSpec(memory_space=pl.ANY))
        operands.append(out)
    return pl.pallas_call(
        finish_kernel,
        out_shape=jax.ShapeDtypeStruct(kept.shape, jnp.bfloat16),
        grid=(columns // TILE,),
        in_specs=in_specs,
        out_specs=tile,
        input_output_aliases={} if out is None else {2: 0},
        compiler_params=pltpu.CompilerParams(vmem_limit_bytes=32 * MIB),
        cost_estimate=pl.CostEstimate(
            flops=BLOCK * columns, bytes_accessed=8 * BLOCK * columns, transcendentals=0
        ),
        name="finish",
    )(*operands)


def body(queries, key_heads, value_heads, doc_lengths, out_weight):
    s = lax.axis_index("seq")
    t = lax.axis_index("tensor")
    hi, core = t // 2, t % 2
    ids = jnp.stack([s, t]).astype(jnp.int32)

    query_pos = s * BLOCK + jnp.arange(BLOCK, dtype=jnp.int32)
    cosine, sine = rope_tables(query_pos)
    own_key = lax.dynamic_index_in_dim(key_heads, hi, 1, keepdims=False).astype(jnp.float32)
    own_key = rope(own_key, cosine, sine).astype(jnp.bfloat16)
    own_value = lax.dynamic_index_in_dim(value_heads, hi, 1, keepdims=False)
    block = jnp.concatenate([own_key, own_value], axis=1)

    near = [permute(block, along_rows(step)) for step in (1, 2, 3, 4)]
    far = permute(block, far_block)
    half = lax.dynamic_slice_in_dim(block, core * (BLOCK // 2), BLOCK // 2, 0)
    shifts = (1, -1, 2)
    group_1 = jnp.concatenate([half, near[0], near[1]], axis=0)
    group_1, far, out_weight = lax.optimization_barrier((group_1, far, out_weight))
    other_weight = permute(out_weight, other_core)
    columns_1 = [permute(group_1, in_row(shift)) for shift in shifts]
    group_2 = jnp.concatenate([near[2], near[3]], axis=0)

    q_own = turn(queries, cosine, sine)
    q_all = jnp.concatenate([q_own, permute(q_own, other_core)], axis=1)
    step = functools.partial(attend, ids, doc_lengths, q_all)

    state = step([half] + near, [("half", 0)] + [(k, 0) for k in (1, 2, 3, 4)])
    group_2, state = lax.optimization_barrier((group_2, state))
    columns_2 = [permute(group_2, in_row(shift)) for shift in shifts]
    for shift, keys in zip(shifts, columns_1):
        kinds = [("half", shift), (1, shift), (2, shift)]
        if shift == 2:
            state = step([keys, far], kinds + [("far", 0)], state)
        else:
            state = step([keys], kinds, state)
    state, other_weight = lax.optimization_barrier((state, other_weight))
    weights = (out_weight, other_weight)
    state = step(columns_2[:2], [(k, shift) for shift in shifts[:2] for k in (3, 4)], state)
    state = step(columns_2[2:], [(3, 2), (4, 2)], state)

    theirs = permute(state, other_core)
    attended, partial = project(ids, (state, theirs), weights, True, 0, (512,), jnp.bfloat16, True)
    received = [permute(partial, other_hi)]
    for partial in project(ids, (attended,), weights, True, 512, (512,) * 3, jnp.bfloat16):
        received.append(permute(partial, other_hi))
    (kept,) = project(ids, (attended,), weights, False, 0, (OUT_COLUMNS,), jnp.float32)
    out, first = None, 0
    for piece in received:
        out = finish(kept, piece, first, out)
        first += piece.shape[1]
    return out


def solution(mesh):
    return jax.shard_map(
        body,
        mesh=mesh,
        in_specs=(
            P("seq", "tensor"),
            P("seq", None, None),
            P("seq", None, None),
            P(),
            P("tensor", None),
        ),
        out_specs=P("seq", "tensor"),
        check_vma=False,
    )
```

time: 147 us -> 105 us (0.71)
  the two profiles are of different devices: /device:TPU:102 before, /device:TPU:104 now
where the time goes in v1:
time: 105 us
  starting transfers between devices  49.9 us (48%)
  Pallas kernels  34.7 us (33%)
  waiting for transfers between devices  17.9 us (17%)
  local copies, waits for them, and re-layouts  1.3 us (1%)
    ppermute x18, starting transfers between devices, permute(): return lax.ppermute(x, ('seq', 'tensor'), device_perm(move))  49.9 us
    pallas_call x6, Pallas kernels, attend(): pl.pallas_call(functools.partial(attend_kernel, kinds, state is None), ou...  23.9 us
    ppermute x18, waiting for transfers between devices, permute(): return lax.ppermute(x, ('seq', 'tensor'), device_perm(move))  17.9 us
    pallas_call x3, Pallas kernels, project(): pl.pallas_call(functools.partial(project_kernel, other_side, first, mergi...  6.8 us
    pallas_call x4, Pallas kernels, finish(): pl.pallas_call(finish_kernel, out_shape=jax.ShapeDtypeStruct(kept.shape,...  3.01 us
  transfers between devices with their start and end apart: 18, of which 5 were waited for; matrix products, arithmetic and copies ran while one was open for 0% of the time, Pallas kernels for 28%

profile of v1, /device:TPU:104, one launch (start us, length us, event | category | flops | bytes accessed | tf_op | source)
XLA Modules:
  0.0 105.1 jit_solution(18445026043333989085)
XLA Ops:
  0.1 1.2 %constant_dynamic-slice_fusion.1 = (bf16[256,1,128]{2,1,0:T(2,128)(2,1)S(1)}, bf16[256,1,128]{2,1,0:T(2,128)(2,1)S(1)}) fusion(bf16[256,2,128]{2,1,0:T(2,128)(2,1)} %param.7, s32[]{:T(128)S(6)} %select_n.20, bf16[256,2,128]{2,1,0:T(2,128)(2,1)} %param.6), kind=kLoop, calls=%fused_computation.13 | loop fusion | bytes 262148 | tf_op jit(solution)/shard_map/jit(dynamic_index_in_dim)/dynamic_slice | solution.py:329
  1.3 0.0 copy-start
  1.4 0.6 subtract_convert_fusion
  1.9 0.1 pad_maximum_fusion.3
  2.1 5.5 %collective-permute-start.4 = (bf16[256,256]{1,0:T(8,128)(2,1)S(1)}, bf16[256,256]{1,0:T(8,128)(2,1)S(1)}, u32[]{:S(2)}, u32[]{:S(2)}) collective-permute-start(bf16[256,256]{1,0:T(8,128)(2,1)S(1)} %pad_maximum_fusion.3), channel_id=1, source_target_pairs={{0,32},{1,113},{2,34},{3,115},{4,36},{5,117},{6,38},{7,119},{8,40}... | collective-permute-start | bytes 393224 | tf_op jit(solution)/shard_map/ppermute | solution.py:45
  7.6 2.9 %collective-permute-start.3 = (bf16[256,256]{1,0:T(8,128)(2,1)S(1)}, bf16[256,256]{1,0:T(8,128)(2,1)S(1)}, u32[]{:S(2)}, u32[]{:S(2)}) collective-permute-start(bf16[256,256]{1,0:T(8,128)(2,1)S(1)} %pad_maximum_fusion.3), channel_id=1, source_target_pairs={{0,16},{1,129},{2,18},{3,131},{4,20},{5,133},{6,22},{7,135},{8,24}... | collective-permute-start | bytes 393224 | tf_op jit(solution)/shard_map/ppermute | solution.py:45
  10.5 0.7 collective-permute-start.8
  11.2 3.2 %collective-permute-done.3.rest_1_ = bf16[256,256]{1,0:T(8,128)(2,1)S(1)} collective-permute-done((bf16[256,256]{1,0:T(8,128)(2,1)S(1)}, bf16[256,256]{1,0:T(8,128)(2,1)S(1)}, u32[]{:S(2)}, u32[]{:S(2)}) %collective-permute-start.3) | collective-permute-done | bytes 131104 | tf_op jit(solution)/shard_map/ppermute | solution.py:45
  14.4 0.1 collective-permute-start.12
  14.6 0.0 copy-start.1
  14.6 1.0 turn.1
  15.6 0.6 collective-permute-start
  16.2 3.7 %collective-permute-start.2 = (bf16[256,256]{1,0:T(8,128)(2,1)S(1)}, bf16[256,256]{1,0:T(8,128)(2,1)S(1)}, u32[]{:S(2)}, u32[]{:S(2)}) collective-permute-start(bf16[256,256]{1,0:T(8,128)(2,1)S(1)} %pad_maximum_fusion.3), channel_id=1, source_target_pairs={{0,64},{1,81},{2,66},{3,83},{4,68},{5,85},{6,70},{7,87},{8,72},{9,... | collective-permute-start | bytes 393224 | tf_op jit(solution)/shard_map/ppermute | solution.py:45
  19.8 6.5 %collective-permute-start.1 = (bf16[256,256]{1,0:T(8,128)(2,1)S(1)}, bf16[256,256]{1,0:T(8,128)(2,1)S(1)}, u32[]{:S(2)}, u32[]{:S(2)}) collective-permute-start(bf16[256,256]{1,0:T(8,128)(2,1)S(1)} %pad_maximum_fusion.3), channel_id=1, source_target_pairs={{0,48},{1,97},{2,50},{3,99},{4,52},{5,101},{6,54},{7,103},{8,56},{... | collective-permute-start | bytes 393224 | tf_op jit(solution)/shard_map/ppermute | solution.py:45
  26.4 0.1 pad_add_fusion.ids
  26.5 1.6 %collective-permute-start.11 = (bf16[640,256]{1,0:T(8,128)(2,1)S(1)}, bf16[640,256]{1,0:T(8,128)(2,1)S(1)}, u32[]{:S(2)}, u32[]{:S(2)}) collective-permute-start(bf16[640,256]{1,0:T(8,128)(2,1)S(1)} %pad_maximum_fusion.1), channel_id=1, source_target_pairs={{0,4},{1,5},{2,6},{3,7},{4,8},{5,9},{6,10},{7,11},{8,12},{9,13},{1... | collective-permute-start | bytes 983048 | tf_op jit(solution)/shard_map/ppermute | solution.py:45
  28.1 0.0 collective-permute-done.2.rest_4_
  28.1 4.8 %collective-permute-start.10 = (bf16[640,256]{1,0:T(8,128)(2,1)S(1)}, bf16[640,256]{1,0:T(8,128)(2,1)S(1)}, u32[]{:S(2)}, u32[]{:S(2)}) collective-permute-start(bf16[640,256]{1,0:T(8,128)(2,1)S(1)} %pad_maximum_fusion.1), channel_id=1, source_target_pairs={{0,12},{1,13},{2,14},{3,15},{4,0},{5,1},{6,2},{7,3},{8,4},{9,5},{1... | collective-permute-start | bytes 983048 | tf_op jit(solution)/shard_map/ppermute | solution.py:45
  32.8 0.0 collective-permute-done.1.rest_3_
  32.8 2.1 %collective-permute-start.9 = (bf16[640,256]{1,0:T(8,128)(2,1)S(1)}, bf16[640,256]{1,0:T(8,128)(2,1)S(1)}, u32[]{:S(2)}, u32[]{:S(2)}) collective-permute-start(bf16[640,256]{1,0:T(8,128)(2,1)S(1)} %pad_maximum_fusion.1), channel_id=1, source_target_pairs={{0,8},{1,9},{2,10},{3,11},{4,12},{5,13},{6,14},{7,15},{8,0},{9,1},... | collective-permute-start | bytes 983048 | tf_op jit(solution)/shard_map/ppermute | solution.py:45
  34.9 0.0 collective-permute-done
  35.0 4.9 %attend.6.rest_1_ = f32[136,2048]{1,0:T(8,128)S(1)} custom-call(s32[2]{0:T(128)S(1)} %pad_add_fusion.ids, s32[8]{0:T(128)S(1)} %copy-done.1, bf16[128,2048]{1,0:T(8,128)(2,1)S(1)} %pad_maximum_fusion.q_ref, bf16[128,256]{1,0:T(8,128)(2,1)S(1)} %constant_dynamic-slice_fusion.rest_0_, bf16[256,256]{1,0:T(8,128)(2,1)S(1)} %collective-permute-done.3.rest_1_, ...), custom_call_target="tpu_custom_call" | custom-call | flops 1 | bytes 1 | tf_op jit(solution)/shard_map/attend/pallas_call | solution.py:191
  39.9 1.7 %collective-permute-start.7 = (bf16[512,256]{1,0:T(8,128)(2,1)S(1)}, bf16[512,256]{1,0:T(8,128)(2,1)S(1)}, u32[]{:S(2)}, u32[]{:S(2)}) collective-permute-start(bf16[512,256]{1,0:T(8,128)(2,1)S(1)} %pad_maximum_fusion.2), channel_id=1, source_target_pairs={{0,12},{1,13},{2,14},{3,15},{4,0},{5,1},{6,2},{7,3},{8,4},{9,5},{1... | collective-permute-start | bytes 786440 | tf_op jit(solution)/shard_map/ppermute | solution.py:45
  41.7 0.0 collective-permute-done.11.rest_0_
  41.7 1.6 %collective-permute-start.6 = (bf16[512,256]{1,0:T(8,128)(2,1)S(1)}, bf16[512,256]{1,0:T(8,128)(2,1)S(1)}, u32[]{:S(2)}, u32[]{:S(2)}) collective-permute-start(bf16[512,256]{1,0:T(8,128)(2,1)S(1)} %pad_maximum_fusion.2), channel_id=1, source_target_pairs={{0,4},{1,5},{2,6},{3,7},{4,8},{5,9},{6,10},{7,11},{8,12},{9,13},{1... | collective-permute-start | bytes 786440 | tf_op jit(solution)/shard_map/ppermute | solution.py:45
  43.2 10.9 %collective-permute-start.5 = (bf16[512,256]{1,0:T(8,128)(2,1)S(1)}, bf16[512,256]{1,0:T(8,128)(2,1)S(1)}, u32[]{:S(2)}, u32[]{:S(2)}) collective-permute-start(bf16[512,256]{1,0:T(8,128)(2,1)S(1)} %pad_maximum_fusion.2), channel_id=1, source_target_pairs={{0,8},{1,9},{2,10},{3,11},{4,12},{5,13},{6,14},{7,15},{8,0},{9,1},... | collective-permute-start | bytes 786440 | tf_op jit(solution)/shard_map/ppermute | solution.py:45
  54.1 3.3 %attend.7.rest_1_ = f32[136,2048]{1,0:T(8,128)S(1)} custom-call(s32[2]{0:T(128)S(1)} %pad_add_fusion.ids, s32[8]{0:T(128)S(1)} %copy-done.1, bf16[128,2048]{1,0:T(8,128)(2,1)S(1)} %pad_maximum_fusion.q_ref, bf16[640,256]{1,0:T(8,128)(2,1)S(1)} %collective-permute-done.11.rest_0_, f32[136,2048]{1,0:T(8,128)S(1)} %attend.6.rest_1_), custom_call_target="tpu_custom_call", output_to_operand_aliasing={{}: (4, {})} | custom-call | flops 1 | bytes 1 | tf_op jit(solution)/shard_map/attend/pallas_call | solution.py:191
  57.4 3.4 %attend.8.rest_2_ = f32[136,2048]{1,0:T(8,128)S(1)} custom-call(s32[2]{0:T(128)S(1)} %pad_add_fusion.ids, s32[8]{0:T(128)S(1)} %copy-done.1, bf16[128,2048]{1,0:T(8,128)(2,1)S(1)} %pad_maximum_fusion.q_ref, bf16[640,256]{1,0:T(8,128)(2,1)S(1)} %collective-permute-done.10.rest_0_, f32[136,2048]{1,0:T(8,128)S(1)} %attend.7.rest_1_), custom_call_target="tpu_custom_call", output_to_operand_aliasing={{}: (4, {})} | custom-call | flops 1 | bytes 1 | tf_op jit(solution)/shard_map/attend/pallas_call | solution.py:191
  60.8 0.0 slice-start.1
  60.9 4.4 %attend.9.rest_2_ = f32[136,2048]{1,0:T(8,128)S(1)} custom-call(s32[2]{0:T(128)S(1)} %pad_add_fusion.ids, s32[8]{0:T(128)S(1)} %copy-done.1, bf16[128,2048]{1,0:T(8,128)(2,1)S(1)} %pad_maximum_fusion.q_ref, bf16[640,256]{1,0:T(8,128)(2,1)S(1)} %collective-permute-done.9.rest_0_, ...), custom_call_target="tpu_custom_call", output_to_operand_aliasing={{}: (5, {})} | custom-call | flops 1 | bytes 1 | tf_op jit(solution)/shard_map/attend/pallas_call | solution.py:191
  65.3 4.7 %attend.10.rest_1_ = f32[136,2048]{1,0:T(8,128)S(1)} custom-call(s32[2]{0:T(128)S(1)} %pad_add_fusion.ids, s32[8]{0:T(128)S(1)} %copy-done.1, bf16[128,2048]{1,0:T(8,128)(2,1)S(1)} %pad_maximum_fusion.q_ref, bf16[512,256]{1,0:T(8,128)(2,1)S(1)} %collective-permute-done.6.rest_0_, ...), custom_call_target="tpu_custom_call", output_to_operand_aliasing={{}: (5, {})} | custom-call | flops 1 | bytes 1 | tf_op jit(solution)/shard_map/attend/pallas_call | solution.py:191
  70.1 3.1 %attend.11.rest_0_ = f32[136,2048]{1,0:T(8,128)S(1)} custom-call(s32[2]{0:T(128)S(1)} %pad_add_fusion.ids, s32[8]{0:T(128)S(1)} %copy-done.1, bf16[128,2048]{1,0:T(8,128)(2,1)S(1)} %pad_maximum_fusion.q_ref, bf16[512,256]{1,0:T(8,128)(2,1)S(1)} %collective-permute-done.5.rest_0_, f32[136,2048]{1,0:T(8,128)S(1)} %attend.10.rest_1_), custom_call_target="tpu_custom_call", output_to_operand_aliasing={{}: (4, {})} | custom-call | flops 1 | bytes 1 | tf_op jit(solution)/shard_map/attend/pallas_call | solution.py:191
  73.2 0.1 collective-permute-start.13
  73.3 2.7 %collective-permute-done.13.rest_1_ = f32[136,2048]{1,0:T(8,128)S(1)} collective-permute-done((f32[136,2048]{1,0:T(8,128)S(1)}, f32[136,2048]{1,0:T(8,128)S(1)}, u32[]{:S(2)}, u32[]{:S(2)}) %collective-permute-start.13) | collective-permute-done | bytes 1114144 | tf_op jit(solution)/shard_map/ppermute | solution.py:45
  76.0 1.5 %project.3 = (bf16[256,1024]{1,0:T(8,128)(2,1)S(1)}, bf16[256,512]{1,0:T(8,128)(2,1)S(1)}) custom-call(s32[2]{0:T(128)S(1)} %pad_add_fusion.ids, f32[136,2048]{1,0:T(8,128)S(1)} %attend.11.rest_0_, f32[136,2048]{1,0:T(8,128)S(1)} %collective-permute-done.13.rest_1_, bf16[512,8192]{1,0:T(8,128)(2,1)S(1)} %bitcast.11, ...), custom_call_target="tpu_custom_call" | custom-call | flops 1 | bytes 1 | tf_op jit(solution)/shard_map/project/pallas_call | solution.py:275
  77.5 2.3 %collective-permute-start.17 = (bf16[256,512]{1,0:T(8,128)(2,1)S(1)}, bf16[256,512]{1,0:T(8,128)(2,1)S(1)}, u32[]{:S(2)}, u32[]{:S(2)}) collective-permute-start(bf16[256,512]{1,0:T(8,128)(2,1)S(1)} %get-tuple-element.28), channel_id=1, source_target_pairs={{0,2},{1,3},{2,0},{3,1},{4,6},{5,7},{6,4},{7,5},{8,10},{9,11},{10,... | collective-permute-start | bytes 786440 | tf_op jit(solution)/shard_map/ppermute | solution.py:45
  79.8 2.4 %project.5 = (bf16[256,512]{1,0:T(8,128)(2,1)S(1)}, bf16[256,512]{1,0:T(8,128)(2,1)S(1)}, bf16[256,512]{1,0:T(8,128)(2,1)S(1)}) custom-call(s32[2]{0:T(128)S(1)} %pad_add_fusion.ids, bf16[256,1024]{1,0:T(8,128)(2,1)S(1)} %get-tuple-element.24.rest_0_, bf16[512,8192]{1,0:T(8,128)(2,1)S(1)} %bitcast.11, ...), custom_call_target="tpu_custom_call" | custom-call | flops 1 | bytes 1 | tf_op jit(solution)/shard_map/project/pallas_call | solution.py:275
  82.2 1.4 %collective-permute-start.16 = (bf16[256,512]{1,0:T(8,128)(2,1)S(1)}, bf16[256,512]{1,0:T(8,128)(2,1)S(1)}, u32[]{:S(2)}, u32[]{:S(2)}) collective-permute-start(bf16[256,512]{1,0:T(8,128)(2,1)S(1)} %get-tuple-element.27), channel_id=1, source_target_pairs={{0,2},{1,3},{2,0},{3,1},{4,6},{5,7},{6,4},{7,5},{8,10},{9,11},{10,... | collective-permute-start | bytes 786440 | tf_op jit(solution)/shard_map/ppermute | solution.py:45
  83.6 2.2 %collective-permute-start.15 = (bf16[256,512]{1,0:T(8,128)(2,1)S(1)}, bf16[256,512]{1,0:T(8,128)(2,1)S(1)}, u32[]{:S(2)}, u32[]{:S(2)}) collective-permute-start(bf16[256,512]{1,0:T(8,128)(2,1)S(1)} %get-tuple-element.26), channel_id=1, source_target_pairs={{0,2},{1,3},{2,0},{3,1},{4,6},{5,7},{6,4},{7,5},{8,10},{9,11},{10,... | collective-permute-start | bytes 786440 | tf_op jit(solution)/shard_map/ppermute | solution.py:45
  85.8 1.3 %collective-permute-start.14 = (bf16[256,512]{1,0:T(8,128)(2,1)S(1)}, bf16[256,512]{1,0:T(8,128)(2,1)S(1)}, u32[]{:S(2)}, u32[]{:S(2)}) collective-permute-start(bf16[256,512]{1,0:T(8,128)(2,1)S(1)} %get-tuple-element.25), channel_id=1, source_target_pairs={{0,2},{1,3},{2,0},{3,1},{4,6},{5,7},{6,4},{7,5},{8,10},{9,11},{10,... | collective-permute-start | bytes 786440 | tf_op jit(solution)/shard_map/ppermute | solution.py:45
  87.1 3.0 %project.4.kept = f32[256,2048]{1,0:T(8,128)S(1)} custom-call(s32[2]{0:T(128)S(1)} %pad_add_fusion.ids, bf16[256,1024]{1,0:T(8,128)(2,1)S(1)} %get-tuple-element.24.rest_0_, bf16[512,8192]{1,0:T(8,128)(2,1)S(1)} %bitcast.11, bf16[512,8192]{1,0:T(8,128)(2,1)S(1)} %collective-permute-done.12.rest_3_.rest_2_), custom_call_target="tpu_custom_call" | custom-call | flops 1 | bytes 1 | tf_op jit(solution)/shard_map/project/pallas_call | solution.py:275
  90.1 0.7 finish.4.rest_0_
  90.9 3.0 %collective-permute-done.16.received = bf16[256,512]{1,0:T(8,128)(2,1)S(1)} collective-permute-done((bf16[256,512]{1,0:T(8,128)(2,1)S(1)}, bf16[256,512]{1,0:T(8,128)(2,1)S(1)}, u32[]{:S(2)}, u32[]{:S(2)}) %collective-permute-start.16) | collective-permute-done | bytes 262176 | tf_op jit(solution)/shard_map/ppermute | solution.py:45
  93.9 0.7 finish.5.rest_0_
  94.6 4.9 %collective-permute-done.15.received = bf16[256,512]{1,0:T(8,128)(2,1)S(1)} collective-permute-done((bf16[256,512]{1,0:T(8,128)(2,1)S(1)}, bf16[256,512]{1,0:T(8,128)(2,1)S(1)}, u32[]{:S(2)}, u32[]{:S(2)}) %collective-permute-start.15) | collective-permute-done | bytes 262176 | tf_op jit(solution)/shard_map/ppermute | solution.py:45
  99.5 0.7 finish.6.rest_0_
  100.2 4.1 %collective-permute-done.14.received = bf16[256,512]{1,0:T(8,128)(2,1)S(1)} collective-permute-done((bf16[256,512]{1,0:T(8,128)(2,1)S(1)}, bf16[256,512]{1,0:T(8,128)(2,1)S(1)}, u32[]{:S(2)}, u32[]{:S(2)}) %collective-permute-start.14) | collective-permute-done | bytes 262176 | tf_op jit(solution)/shard_map/ppermute | solution.py:45
  104.3 0.8 finish.7
  (23 shorter events, 0.2 us)
Async XLA Ops:
  1.3 13.3 %copy-start = (bf16[256,512]{1,0:T(8,128)(2,1)S(1)}, bf16[256,512]{1,0:T(8,128)(2,1)}, u32[]{:S(2)}) copy-start(bf16[256,512]{1,0:T(8,128)(2,1)} %queries.1) | copy-start | bytes 786436
  2.1 9.1 %collective-permute-start.4 = (bf16[256,256]{1,0:T(8,128)(2,1)S(1)}, bf16[256,256]{1,0:T(8,128)(2,1)S(1)}, u32[]{:S(2)}, u32[]{:S(2)}) collective-permute-start(bf16[256,256]{1,0:T(8,128)(2,1)S(1)} %pad_maximum_fusion.3), channel_id=1, source_target_pairs={{0,32},{1,113},{2,34},{3,115},{4,36},{5,117},{6,38},{7,119},{8,40}... | collective-permute-start | bytes 393224 | tf_op jit(solution)/shard_map/ppermute | solution.py:45
  7.6 6.9 %collective-permute-start.3 = (bf16[256,256]{1,0:T(8,128)(2,1)S(1)}, bf16[256,256]{1,0:T(8,128)(2,1)S(1)}, u32[]{:S(2)}, u32[]{:S(2)}) collective-permute-start(bf16[256,256]{1,0:T(8,128)(2,1)S(1)} %pad_maximum_fusion.3), channel_id=1, source_target_pairs={{0,16},{1,129},{2,18},{3,131},{4,20},{5,133},{6,22},{7,135},{8,24}... | collective-permute-start | bytes 393224 | tf_op jit(solution)/shard_map/ppermute | solution.py:45
  10.5 4.0 %collective-permute-start.8 = (bf16[256,256]{1,0:T(8,128)(2,1)S(1)}, bf16[256,256]{1,0:T(8,128)(2,1)S(1)}, u32[]{:S(2)}, u32[]{:S(2)}) collective-permute-start(bf16[256,256]{1,0:T(8,128)(2,1)S(1)} %pad_maximum_fusion.3), channel_id=1, source_target_pairs={{12,144},{14,146},{28,160},{30,162},{44,176},{46,178},{60,192},{62... | collective-permute-start | bytes 393224 | tf_op jit(solution)/shard_map/ppermute | solution.py:45
  14.4 50.8 %collective-permute-start.12 = (bf16[512,8192]{1,0:T(8,128)(2,1)}, bf16[512,8192]{1,0:T(8,128)(2,1)S(1)}, u32[]{:S(2)}, u32[]{:S(2)}) collective-permute-start(bf16[512,8192]{1,0:T(8,128)(2,1)} %rest_1_.1), channel_id=1, source_target_pairs={{0,1},{1,0},{2,3},{3,2},{4,5},{5,4},{6,7},{7,6},{8,9},{9,8},{10,11... | collective-permute-start | bytes 25165832 | tf_op jit(solution)/shard_map/ppermute | solution.py:45
  14.6 20.4 %copy-start.1 = (s32[8]{0:T(128)S(1)}, s32[8]{0:T(128)}, u32[]{:S(2)}) copy-start(s32[8]{0:T(128)} %lengths.11) | copy-start | bytes 100
  15.6 19.3 %collective-permute-start = (bf16[128,1024]{1,0:T(8,128)(2,1)S(1)}, bf16[128,1024]{1,0:T(8,128)(2,1)S(1)}, u32[]{:S(2)}, u32[]{:S(2)}) collective-permute-start(bf16[128,1024]{1,0:T(8,128)(2,1)S(1)} %turn.1), channel_id=1, source_target_pairs={{0,1},{1,0},{2,3},{3,2},{4,5},{5,4},{6,7},{7,6},{8,9},{9,8},{10,11... | collective-permute-start | bytes 786440 | tf_op jit(solution)/shard_map/ppermute | solution.py:45
  16.2 11.9 %collective-permute-start.2 = (bf16[256,256]{1,0:T(8,128)(2,1)S(1)}, bf16[256,256]{1,0:T(8,128)(2,1)S(1)}, u32[]{:S(2)}, u32[]{:S(2)}) collective-permute-start(bf16[256,256]{1,0:T(8,128)(2,1)S(1)} %pad_maximum_fusion.3), channel_id=1, source_target_pairs={{0,64},{1,81},{2,66},{3,83},{4,68},{5,85},{6,70},{7,87},{8,72},{9,... | collective-permute-start | bytes 393224 | tf_op jit(solution)/shard_map/ppermute | solution.py:45
  19.8 13.0 %collective-permute-start.1 = (bf16[256,256]{1,0:T(8,128)(2,1)S(1)}, bf16[256,256]{1,0:T(8,128)(2,1)S(1)}, u32[]{:S(2)}, u32[]{:S(2)}) collective-permute-start(bf16[256,256]{1,0:T(8,128)(2,1)S(1)} %pad_maximum_fusion.3), channel_id=1, source_target_pairs={{0,48},{1,97},{2,50},{3,99},{4,52},{5,101},{6,54},{7,103},{8,56},{... | collective-permute-start | bytes 393224 | tf_op jit(solution)/shard_map/ppermute | solution.py:45
  26.5 15.2 %collective-permute-start.11 = (bf16[640,256]{1,0:T(8,128)(2,1)S(1)}, bf16[640,256]{1,0:T(8,128)(2,1)S(1)}, u32[]{:S(2)}, u32[]{:S(2)}) collective-permute-start(bf16[640,256]{1,0:T(8,128)(2,1)S(1)} %pad_maximum_fusion.1), channel_id=1, source_target_pairs={{0,4},{1,5},{2,6},{3,7},{4,8},{5,9},{6,10},{7,11},{8,12},{9,13},{1... | collective-permute-start | bytes 983048 | tf_op jit(solution)/shard_map/ppermute | solution.py:45
  28.1 15.2 %collective-permute-start.10 = (bf16[640,256]{1,0:T(8,128)(2,1)S(1)}, bf16[640,256]{1,0:T(8,128)(2,1)S(1)}, u32[]{:S(2)}, u32[]{:S(2)}) collective-permute-start(bf16[640,256]{1,0:T(8,128)(2,1)S(1)} %pad_maximum_fusion.1), channel_id=1, source_target_pairs={{0,12},{1,13},{2,14},{3,15},{4,0},{5,1},{6,2},{7,3},{8,4},{9,5},{1... | collective-permute-start | bytes 983048 | tf_op jit(solution)/shard_map/ppermute | solution.py:45
  32.8 28.0 %collective-permute-start.9 = (bf16[640,256]{1,0:T(8,128)(2,1)S(1)}, bf16[640,256]{1,0:T(8,128)(2,1)S(1)}, u32[]{:S(2)}, u32[]{:S(2)}) collective-permute-start(bf16[640,256]{1,0:T(8,128)(2,1)S(1)} %pad_maximum_fusion.1), channel_id=1, source_target_pairs={{0,8},{1,9},{2,10},{3,11},{4,12},{5,13},{6,14},{7,15},{8,0},{9,1},... | collective-permute-start | bytes 983048 | tf_op jit(solution)/shard_map/ppermute | solution.py:45
  39.9 25.4 %collective-permute-start.7 = (bf16[512,256]{1,0:T(8,128)(2,1)S(1)}, bf16[512,256]{1,0:T(8,128)(2,1)S(1)}, u32[]{:S(2)}, u32[]{:S(2)}) collective-permute-start(bf16[512,256]{1,0:T(8,128)(2,1)S(1)} %pad_maximum_fusion.2), channel_id=1, source_target_pairs={{0,12},{1,13},{2,14},{3,15},{4,0},{5,1},{6,2},{7,3},{8,4},{9,5},{1... | collective-permute-start | bytes 786440 | tf_op jit(solution)/shard_map/ppermute | solution.py:45
  41.7 23.6 %collective-permute-start.6 = (bf16[512,256]{1,0:T(8,128)(2,1)S(1)}, bf16[512,256]{1,0:T(8,128)(2,1)S(1)}, u32[]{:S(2)}, u32[]{:S(2)}) collective-permute-start(bf16[512,256]{1,0:T(8,128)(2,1)S(1)} %pad_maximum_fusion.2), channel_id=1, source_target_pairs={{0,4},{1,5},{2,6},{3,7},{4,8},{5,9},{6,10},{7,11},{8,12},{9,13},{1... | collective-permute-start | bytes 786440 | tf_op jit(solution)/shard_map/ppermute | solution.py:45
  43.2 26.8 %collective-permute-start.5 = (bf16[512,256]{1,0:T(8,128)(2,1)S(1)}, bf16[512,256]{1,0:T(8,128)(2,1)S(1)}, u32[]{:S(2)}, u32[]{:S(2)}) collective-permute-start(bf16[512,256]{1,0:T(8,128)(2,1)S(1)} %pad_maximum_fusion.2), channel_id=1, source_target_pairs={{0,8},{1,9},{2,10},{3,11},{4,12},{5,13},{6,14},{7,15},{8,0},{9,1},... | collective-permute-start | bytes 786440 | tf_op jit(solution)/shard_map/ppermute | solution.py:45
  54.1 21.9 %slice-start = ((s8[8388608]{0:T(1024)(128)(4,1)}), s8[4194304]{0:T(1024)(128)(4,1)S(1)}, s32[]{:S(2)}) async-start(s8[8388608]{0:T(1024)(128)(4,1)} %bitcast.10), calls=%async_computation | async-start | bytes 8388608
  60.8 15.2 %slice-start.1 = ((s8[8388608]{0:T(1024)(128)(4,1)}), s8[4194304]{0:T(1024)(128)(4,1)S(1)}, s32[]{:S(2)}) async-start(s8[8388608]{0:T(1024)(128)(4,1)} %bitcast.10), calls=%async_computation.1 | async-start | bytes 8388608
  73.2 2.8 %collective-permute-start.13 = (f32[136,2048]{1,0:T(8,128)S(1)}, f32[136,2048]{1,0:T(8,128)S(1)}, u32[]{:S(2)}, u32[]{:S(2)}) collective-permute-start(f32[136,2048]{1,0:T(8,128)S(1)} %attend.11.rest_0_), channel_id=1, source_target_pairs={{0,1},{1,0},{2,3},{3,2},{4,5},{5,4},{6,7},{7,6},{8,9},{9,8},{10,11... | collective-permute-start | bytes 3342344 | tf_op jit(solution)/shard_map/ppermute | solution.py:45
  77.5 12.6 %collective-permute-start.17 = (bf16[256,512]{1,0:T(8,128)(2,1)S(1)}, bf16[256,512]{1,0:T(8,128)(2,1)S(1)}, u32[]{:S(2)}, u32[]{:S(2)}) collective-permute-start(bf16[256,512]{1,0:T(8,128)(2,1)S(1)} %get-tuple-element.28), channel_id=1, source_target_pairs={{0,2},{1,3},{2,0},{3,1},{4,6},{5,7},{6,4},{7,5},{8,10},{9,11},{10,... | collective-permute-start | bytes 786440 | tf_op jit(solution)/shard_map/ppermute | solution.py:45
  82.2 11.7 %collective-permute-start.16 = (bf16[256,512]{1,0:T(8,128)(2,1)S(1)}, bf16[256,512]{1,0:T(8,128)(2,1)S(1)}, u32[]{:S(2)}, u32[]{:S(2)}) collective-permute-start(bf16[256,512]{1,0:T(8,128)(2,1)S(1)} %get-tuple-element.27), channel_id=1, source_target_pairs={{0,2},{1,3},{2,0},{3,1},{4,6},{5,7},{6,4},{7,5},{8,10},{9,11},{10,... | collective-permute-start | bytes 786440 | tf_op jit(solution)/shard_map/ppermute | solution.py:45
  83.6 15.9 %collective-permute-start.15 = (bf16[256,512]{1,0:T(8,128)(2,1)S(1)}, bf16[256,512]{1,0:T(8,128)(2,1)S(1)}, u32[]{:S(2)}, u32[]{:S(2)}) collective-permute-start(bf16[256,512]{1,0:T(8,128)(2,1)S(1)} %get-tuple-element.26), channel_id=1, source_target_pairs={{0,2},{1,3},{2,0},{3,1},{4,6},{5,7},{6,4},{7,5},{8,10},{9,11},{10,... | collective-permute-start | bytes 786440 | tf_op jit(solution)/shard_map/ppermute | solution.py:45
  85.8 18.5 %collective-permute-start.14 = (bf16[256,512]{1,0:T(8,128)(2,1)S(1)}, bf16[256,512]{1,0:T(8,128)(2,1)S(1)}, u32[]{:S(2)}, u32[]{:S(2)}) collective-permute-start(bf16[256,512]{1,0:T(8,128)(2,1)S(1)} %get-tuple-element.25), channel_id=1, source_target_pairs={{0,2},{1,3},{2,0},{3,1},{4,6},{5,7},{6,4},{7,5},{8,10},{9,11},{10,... | collective-permute-start | bytes 786440 | tf_op jit(solution)/shard_map/ppermute | solution.py:45

commit v2 on v1

--- a/solution.py
+++ b/solution.py
@@ -334,19 +334,23 @@
     half = lax.dynamic_slice_in_dim(block, core * (BLOCK // 2), BLOCK // 2, 0)
     shifts = (1, -1, 2)
     group_1 = jnp.concatenate([half, near[0], near[1]], axis=0)
-    group_1, far, out_weight = lax.optimization_barrier((group_1, far, out_weight))
+    q_own = turn(queries, cosine, sine)
+    q_other = permute(q_own, other_core)
+    group_1, out_weight, q_other, *near[2:] = lax.optimization_barrier(
+        (group_1, out_weight, q_other, *near[2:])
+    )
     other_weight = permute(out_weight, other_core)
     columns_1 = [permute(group_1, in_row(shift)) for shift in shifts]
     group_2 = jnp.concatenate([near[2], near[3]], axis=0)
 
-    q_own = turn(queries, cosine, sine)
-    q_all = jnp.concatenate([q_own, permute(q_own, other_core)], axis=1)
+    q_all = jnp.concatenate([q_own, q_other], axis=1)
     step = functools.partial(attend, ids, doc_lengths, q_all)
 
     state = step([half] + near, [("half", 0)] + [(k, 0) for k in (1, 2, 3, 4)])
-    group_2, state = lax.optimization_barrier((group_2, state))
-    columns_2 = [permute(group_2, in_row(shift)) for shift in shifts]
+    columns_2 = []
     for shift, keys in zip(shifts, columns_1):
+        group_2, state = lax.optimization_barrier((group_2, state))
+        columns_2.append(permute(group_2, in_row(shift)))
         kinds = [("half", shift), (1, shift), (2, shift)]
         if shift == 2:
             state = step([keys, far], kinds + [("far", 0)], state)
@@ -354,8 +358,8 @@
             state = step([keys], kinds, state)
     state, other_weight = lax.optimization_barrier((state, other_weight))
     weights = (out_weight, other_weight)
-    state = step(columns_2[:2], [(k, shift) for shift in shifts[:2] for k in (3, 4)], state)
-    state = step(columns_2[2:], [(3, 2), (4, 2)], state)
+    for shift, keys in zip(shifts, columns_2):
+        state = step([keys], [(3, shift), (4, shift)], state)
 
     theirs = permute(state, other_core)
     attended, partial = project(ids, (state, theirs), weights, True, 0, (512,), jnp.bfloat16, True)

time: 105 us -> 108 us (1.029)
  the two profiles are of different devices: /device:TPU:104 before, /device:TPU:6 now
where the time goes in v2:
time: 108 us
  Pallas kernels  36.1 us (33%)
  starting transfers between devices  35.7 us (33%)
  waiting for transfers between devices  33.8 us (31%)
  local copies, waits for them, and re-layouts  1.32 us (1%)
    ppermute x18, starting transfers between devices, permute(): return lax.ppermute(x, ('seq', 'tensor'), device_perm(move))  35.7 us
    ppermute x18, waiting for transfers between devices, permute(): return lax.ppermute(x, ('seq', 'tensor'), device_perm(move))  33.8 us
    pallas_call x7, Pallas kernels, attend(): pl.pallas_call(functools.partial(attend_kernel, kinds, state is None), ou...  25.2 us
    pallas_call x3, Pallas kernels, project(): pl.pallas_call(functools.partial(project_kernel, other_side, first, mergi...  6.8 us
    pallas_call x4, Pallas kernels, finish(): pl.pallas_call(finish_kernel, out_shape=jax.ShapeDtypeStruct(kept.shape,...  3.01 us
  transfers between devices with their start and end apart: 18, of which 7 were waited for; matrix products, arithmetic and copies ran while one was open for 0% of the time, Pallas kernels for 27%

profile of v2, /device:TPU:6, one launch (start us, length us, event | category | flops | bytes accessed | tf_op | source)
XLA Modules:
  0.0 108.1 jit_solution(5104492820733824278)
XLA Ops:
  0.1 1.3 %constant_dynamic-slice_fusion.1 = (bf16[256,1,128]{2,1,0:T(2,128)(2,1)S(1)}, bf16[256,1,128]{2,1,0:T(2,128)(2,1)S(1)}) fusion(bf16[256,2,128]{2,1,0:T(2,128)(2,1)} %param.7, s32[]{:T(128)S(6)} %select_n.20, bf16[256,2,128]{2,1,0:T(2,128)(2,1)} %param.6), kind=kLoop, calls=%fused_computation.13 | loop fusion | bytes 262148 | tf_op jit(solution)/shard_map/jit(dynamic_index_in_dim)/dynamic_slice | solution.py:329
  1.4 0.6 subtract_convert_fusion
  1.9 1.0 turn.1
  3.0 0.1 collective-permute-start.2
  3.1 0.0 copy-start.1
  3.1 0.1 pad_maximum_fusion.3
  3.2 5.2 %collective-permute-start.1 = (bf16[256,256]{1,0:T(8,128)(2,1)S(1)}, bf16[256,256]{1,0:T(8,128)(2,1)S(1)}, u32[]{:S(2)}, u32[]{:S(2)}) collective-permute-start(bf16[256,256]{1,0:T(8,128)(2,1)S(1)} %pad_maximum_fusion.3), channel_id=1, source_target_pairs={{0,32},{1,113},{2,34},{3,115},{4,36},{5,117},{6,38},{7,119},{8,40}... | collective-permute-start | bytes 393224 | tf_op jit(solution)/shard_map/ppermute | solution.py:45
  8.4 3.8 %collective-permute-start = (bf16[256,256]{1,0:T(8,128)(2,1)S(1)}, bf16[256,256]{1,0:T(8,128)(2,1)S(1)}, u32[]{:S(2)}, u32[]{:S(2)}) collective-permute-start(bf16[256,256]{1,0:T(8,128)(2,1)S(1)} %pad_maximum_fusion.3), channel_id=1, source_target_pairs={{0,16},{1,129},{2,18},{3,131},{4,20},{5,133},{6,22},{7,135},{8,24}... | collective-permute-start | bytes 393224 | tf_op jit(solution)/shard_map/ppermute | solution.py:45
  12.2 6.4 %collective-permute-start.4 = (bf16[256,256]{1,0:T(8,128)(2,1)S(1)}, bf16[256,256]{1,0:T(8,128)(2,1)S(1)}, u32[]{:S(2)}, u32[]{:S(2)}) collective-permute-start(bf16[256,256]{1,0:T(8,128)(2,1)S(1)} %pad_maximum_fusion.3), channel_id=1, source_target_pairs={{0,64},{1,81},{2,66},{3,83},{4,68},{5,85},{6,70},{7,87},{8,72},{9,... | collective-permute-start | bytes 393224 | tf_op jit(solution)/shard_map/ppermute | solution.py:45
  18.6 1.9 %collective-permute-start.3 = (bf16[256,256]{1,0:T(8,128)(2,1)S(1)}, bf16[256,256]{1,0:T(8,128)(2,1)S(1)}, u32[]{:S(2)}, u32[]{:S(2)}) collective-permute-start(bf16[256,256]{1,0:T(8,128)(2,1)S(1)} %pad_maximum_fusion.3), channel_id=1, source_target_pairs={{0,48},{1,97},{2,50},{3,99},{4,52},{5,101},{6,54},{7,103},{8,56},{... | collective-permute-start | bytes 393224 | tf_op jit(solution)/shard_map/ppermute | solution.py:45
  20.6 0.0 collective-permute-done.rest_1_
  20.7 4.8 %collective-permute-done.4.rest_4_ = bf16[256,256]{1,0:T(8,128)(2,1)S(1)} collective-permute-done((bf16[256,256]{1,0:T(8,128)(2,1)S(1)}, bf16[256,256]{1,0:T(8,128)(2,1)S(1)}, u32[]{:S(2)}, u32[]{:S(2)}) %collective-permute-start.4) | collective-permute-done | bytes 131104 | tf_op jit(solution)/shard_map/ppermute | solution.py:45
  25.4 5.9 %collective-permute-done.3.rest_3_ = bf16[256,256]{1,0:T(8,128)(2,1)S(1)} collective-permute-done((bf16[256,256]{1,0:T(8,128)(2,1)S(1)}, bf16[256,256]{1,0:T(8,128)(2,1)S(1)}, u32[]{:S(2)}, u32[]{:S(2)}) %collective-permute-start.3) | collective-permute-done | bytes 131104 | tf_op jit(solution)/shard_map/ppermute | solution.py:45
  31.4 0.7 collective-permute-start.11
  32.0 0.1 pad_add_fusion.ids
  32.1 3.2 %collective-permute-start.10 = (bf16[640,256]{1,0:T(8,128)(2,1)S(1)}, bf16[640,256]{1,0:T(8,128)(2,1)S(1)}, u32[]{:S(2)}, u32[]{:S(2)}) collective-permute-start(bf16[640,256]{1,0:T(8,128)(2,1)S(1)} %pad_maximum_fusion.1), channel_id=1, source_target_pairs={{0,8},{1,9},{2,10},{3,11},{4,12},{5,13},{6,14},{7,15},{8,0},{9,1},... | collective-permute-start | bytes 983048 | tf_op jit(solution)/shard_map/ppermute | solution.py:45
  35.3 1.1 collective-permute-start.6
  36.4 1.0 collective-permute-start.5
  37.4 4.9 %attend.7.rest_1_ = f32[136,2048]{1,0:T(8,128)S(1)} custom-call(s32[2]{0:T(128)S(1)} %pad_add_fusion.ids, s32[8]{0:T(128)S(1)} %copy-done.1, bf16[128,2048]{1,0:T(8,128)(2,1)S(1)} %pad_maximum_fusion.q_ref, bf16[128,256]{1,0:T(8,128)(2,1)S(1)} %constant_dynamic-slice_fusion.rest_0_, bf16[256,256]{1,0:T(8,128)(2,1)S(1)} %collective-permute-done.rest_1_, ...), custom_call_target="tpu_custom_call" | custom-call | flops 1 | bytes 1 | tf_op jit(solution)/shard_map/attend/pallas_call | solution.py:191
  42.4 8.4 %collective-permute-done.5.rest_0_ = bf16[640,256]{1,0:T(8,128)(2,1)S(1)} collective-permute-done((bf16[640,256]{1,0:T(8,128)(2,1)S(1)}, bf16[640,256]{1,0:T(8,128)(2,1)S(1)}, u32[]{:S(2)}, u32[]{:S(2)}) %collective-permute-start.5) | collective-permute-done | bytes 327712 | tf_op jit(solution)/shard_map/ppermute | solution.py:45
  50.8 1.7 %collective-permute-start.9 = (bf16[512,256]{1,0:T(8,128)(2,1)S(1)}, bf16[512,256]{1,0:T(8,128)(2,1)S(1)}, u32[]{:S(2)}, u32[]{:S(2)}) collective-permute-start(bf16[512,256]{1,0:T(8,128)(2,1)S(1)} %pad_maximum_fusion.2), channel_id=1, source_target_pairs={{0,4},{1,5},{2,6},{3,7},{4,8},{5,9},{6,10},{7,11},{8,12},{9,13},{1... | collective-permute-start | bytes 786440 | tf_op jit(solution)/shard_map/ppermute | solution.py:45
  52.5 3.4 %attend.8.rest_1_ = f32[136,2048]{1,0:T(8,128)S(1)} custom-call(s32[2]{0:T(128)S(1)} %pad_add_fusion.ids, s32[8]{0:T(128)S(1)} %copy-done.1, bf16[128,2048]{1,0:T(8,128)(2,1)S(1)} %pad_maximum_fusion.q_ref, bf16[640,256]{1,0:T(8,128)(2,1)S(1)} %collective-permute-done.5.rest_0_, f32[136,2048]{1,0:T(8,128)S(1)} %attend.7.rest_1_), custom_call_target="tpu_custom_call", output_to_operand_aliasing={{}: (4, {})} | custom-call | flops 1 | bytes 1 | tf_op jit(solution)/shard_map/attend/pallas_call | solution.py:191
  56.0 0.0 collective-permute-done.6.rest_0_
  56.0 1.2 %collective-permute-start.8 = (bf16[512,256]{1,0:T(8,128)(2,1)S(1)}, bf16[512,256]{1,0:T(8,128)(2,1)S(1)}, u32[]{:S(2)}, u32[]{:S(2)}) collective-permute-start(bf16[512,256]{1,0:T(8,128)(2,1)S(1)} %pad_maximum_fusion.2), channel_id=1, source_target_pairs={{0,12},{1,13},{2,14},{3,15},{4,0},{5,1},{6,2},{7,3},{8,4},{9,5},{1... | collective-permute-start | bytes 786440 | tf_op jit(solution)/shard_map/ppermute | solution.py:45
  57.2 3.6 %attend.9.rest_2_ = f32[136,2048]{1,0:T(8,128)S(1)} custom-call(s32[2]{0:T(128)S(1)} %pad_add_fusion.ids, s32[8]{0:T(128)S(1)} %copy-done.1, bf16[128,2048]{1,0:T(8,128)(2,1)S(1)} %pad_maximum_fusion.q_ref, bf16[640,256]{1,0:T(8,128)(2,1)S(1)} %collective-permute-done.6.rest_0_, f32[136,2048]{1,0:T(8,128)S(1)} %attend.8.rest_1_), custom_call_target="tpu_custom_call", output_to_operand_aliasing={{}: (4, {})} | custom-call | flops 1 | bytes 1 | tf_op jit(solution)/shard_map/attend/pallas_call | solution.py:191
  60.8 0.0 collective-permute-done.11.rest_1_
  60.8 2.1 %collective-permute-start.7 = (bf16[512,256]{1,0:T(8,128)(2,1)S(1)}, bf16[512,256]{1,0:T(8,128)(2,1)S(1)}, u32[]{:S(2)}, u32[]{:S(2)}) collective-permute-start(bf16[512,256]{1,0:T(8,128)(2,1)S(1)} %pad_maximum_fusion.2), channel_id=1, source_target_pairs={{0,8},{1,9},{2,10},{3,11},{4,12},{5,13},{6,14},{7,15},{8,0},{9,1},... | collective-permute-start | bytes 786440 | tf_op jit(solution)/shard_map/ppermute | solution.py:45
  62.9 4.4 %attend.10.rest_1_ = f32[136,2048]{1,0:T(8,128)S(1)} custom-call(s32[2]{0:T(128)S(1)} %pad_add_fusion.ids, s32[8]{0:T(128)S(1)} %copy-done.1, bf16[128,2048]{1,0:T(8,128)(2,1)S(1)} %pad_maximum_fusion.q_ref, bf16[640,256]{1,0:T(8,128)(2,1)S(1)} %collective-permute-done.10.rest_0_, ...), custom_call_target="tpu_custom_call", output_to_operand_aliasing={{}: (5, {})} | custom-call | flops 1 | bytes 1 | tf_op jit(solution)/shard_map/attend/pallas_call | solution.py:191
  67.3 0.0 slice-start.1
  67.4 2.9 %attend.11.rest_1_ = f32[136,2048]{1,0:T(8,128)S(1)} custom-call(s32[2]{0:T(128)S(1)} %pad_add_fusion.ids, s32[8]{0:T(128)S(1)} %copy-done.1, bf16[128,2048]{1,0:T(8,128)(2,1)S(1)} %pad_maximum_fusion.q_ref, bf16[512,256]{1,0:T(8,128)(2,1)S(1)} %collective-permute-done.9.rest_0_, f32[136,2048]{1,0:T(8,128)S(1)} %attend.10.rest_1_), custom_call_target="tpu_custom_call", output_to_operand_aliasing={{}: (4, {})} | custom-call | flops 1 | bytes 1 | tf_op jit(solution)/shard_map/attend/pallas_call | solution.py:191
  70.3 2.9 %attend.12.rest_1_ = f32[136,2048]{1,0:T(8,128)S(1)} custom-call(s32[2]{0:T(128)S(1)} %pad_add_fusion.ids, s32[8]{0:T(128)S(1)} %copy-done.1, bf16[128,2048]{1,0:T(8,128)(2,1)S(1)} %pad_maximum_fusion.q_ref, bf16[512,256]{1,0:T(8,128)(2,1)S(1)} %collective-permute-done.8.rest_0_, f32[136,2048]{1,0:T(8,128)S(1)} %attend.11.rest_1_), custom_call_target="tpu_custom_call", output_to_operand_aliasing={{}: (4, {})} | custom-call | flops 1 | bytes 1 | tf_op jit(solution)/shard_map/attend/pallas_call | solution.py:191
  73.2 3.1 %attend.13.rest_0_ = f32[136,2048]{1,0:T(8,128)S(1)} custom-call(s32[2]{0:T(128)S(1)} %pad_add_fusion.ids, s32[8]{0:T(128)S(1)} %copy-done.1, bf16[128,2048]{1,0:T(8,128)(2,1)S(1)} %pad_maximum_fusion.q_ref, bf16[512,256]{1,0:T(8,128)(2,1)S(1)} %collective-permute-done.7.rest_0_, f32[136,2048]{1,0:T(8,128)S(1)} %attend.12.rest_1_), custom_call_target="tpu_custom_call", output_to_operand_aliasing={{}: (4, {})} | custom-call | flops 1 | bytes 1 | tf_op jit(solution)/shard_map/attend/pallas_call | solution.py:191
  76.3 0.1 collective-permute-start.13
  76.4 2.7 %collective-permute-done.13.rest_1_ = f32[136,2048]{1,0:T(8,128)S(1)} collective-permute-done((f32[136,2048]{1,0:T(8,128)S(1)}, f32[136,2048]{1,0:T(8,128)S(1)}, u32[]{:S(2)}, u32[]{:S(2)}) %collective-permute-start.13) | collective-permute-done | bytes 1114144 | tf_op jit(solution)/shard_map/ppermute | solution.py:45
  79.1 1.5 %project.3 = (bf16[256,1024]{1,0:T(8,128)(2,1)S(1)}, bf16[256,512]{1,0:T(8,128)(2,1)S(1)}) custom-call(s32[2]{0:T(128)S(1)} %pad_add_fusion.ids, f32[136,2048]{1,0:T(8,128)S(1)} %attend.13.rest_0_, f32[136,2048]{1,0:T(8,128)S(1)} %collective-permute-done.13.rest_1_, bf16[512,8192]{1,0:T(8,128)(2,1)S(1)} %bitcast.11, ...), custom_call_target="tpu_custom_call" | custom-call | flops 1 | bytes 1 | tf_op jit(solution)/shard_map/project/pallas_call | solution.py:275
  80.6 1.5 %collective-permute-start.17 = (bf16[256,512]{1,0:T(8,128)(2,1)S(1)}, bf16[256,512]{1,0:T(8,128)(2,1)S(1)}, u32[]{:S(2)}, u32[]{:S(2)}) collective-permute-start(bf16[256,512]{1,0:T(8,128)(2,1)S(1)} %get-tuple-element.40), channel_id=1, source_target_pairs={{0,2},{1,3},{2,0},{3,1},{4,6},{5,7},{6,4},{7,5},{8,10},{9,11},{10,... | collective-permute-start | bytes 786440 | tf_op jit(solution)/shard_map/ppermute | solution.py:45
  82.1 2.4 %project.5 = (bf16[256,512]{1,0:T(8,128)(2,1)S(1)}, bf16[256,512]{1,0:T(8,128)(2,1)S(1)}, bf16[256,512]{1,0:T(8,128)(2,1)S(1)}) custom-call(s32[2]{0:T(128)S(1)} %pad_add_fusion.ids, bf16[256,1024]{1,0:T(8,128)(2,1)S(1)} %get-tuple-element.36.rest_0_, bf16[512,8192]{1,0:T(8,128)(2,1)S(1)} %bitcast.11, ...), custom_call_target="tpu_custom_call" | custom-call | flops 1 | bytes 1 | tf_op jit(solution)/shard_map/project/pallas_call | solution.py:275
  84.4 2.2 %collective-permute-start.16 = (bf16[256,512]{1,0:T(8,128)(2,1)S(1)}, bf16[256,512]{1,0:T(8,128)(2,1)S(1)}, u32[]{:S(2)}, u32[]{:S(2)}) collective-permute-start(bf16[256,512]{1,0:T(8,128)(2,1)S(1)} %get-tuple-element.39), channel_id=1, source_target_pairs={{0,2},{1,3},{2,0},{3,1},{4,6},{5,7},{6,4},{7,5},{8,10},{9,11},{10,... | collective-permute-start | bytes 786440 | tf_op jit(solution)/shard_map/ppermute | solution.py:45
  86.7 1.4 %collective-permute-start.15 = (bf16[256,512]{1,0:T(8,128)(2,1)S(1)}, bf16[256,512]{1,0:T(8,128)(2,1)S(1)}, u32[]{:S(2)}, u32[]{:S(2)}) collective-permute-start(bf16[256,512]{1,0:T(8,128)(2,1)S(1)} %get-tuple-element.38), channel_id=1, source_target_pairs={{0,2},{1,3},{2,0},{3,1},{4,6},{5,7},{6,4},{7,5},{8,10},{9,11},{10,... | collective-permute-start | bytes 786440 | tf_op jit(solution)/shard_map/ppermute | solution.py:45
  88.1 2.1 %collective-permute-start.14 = (bf16[256,512]{1,0:T(8,128)(2,1)S(1)}, bf16[256,512]{1,0:T(8,128)(2,1)S(1)}, u32[]{:S(2)}, u32[]{:S(2)}) collective-permute-start(bf16[256,512]{1,0:T(8,128)(2,1)S(1)} %get-tuple-element.37), channel_id=1, source_target_pairs={{0,2},{1,3},{2,0},{3,1},{4,6},{5,7},{6,4},{7,5},{8,10},{9,11},{10,... | collective-permute-start | bytes 786440 | tf_op jit(solution)/shard_map/ppermute | solution.py:45
  90.2 3.0 %project.4.kept = f32[256,2048]{1,0:T(8,128)S(1)} custom-call(s32[2]{0:T(128)S(1)} %pad_add_fusion.ids, bf16[256,1024]{1,0:T(8,128)(2,1)S(1)} %get-tuple-element.36.rest_0_, bf16[512,8192]{1,0:T(8,128)(2,1)S(1)} %bitcast.11, bf16[512,8192]{1,0:T(8,128)(2,1)S(1)} %collective-permute-done.12.rest_3_.rest_2_), custom_call_target="tpu_custom_call" | custom-call | flops 1 | bytes 1 | tf_op jit(solution)/shard_map/project/pallas_call | solution.py:275
  93.2 0.7 finish.4.rest_0_
  93.9 3.0 %collective-permute-done.16.received = bf16[256,512]{1,0:T(8,128)(2,1)S(1)} collective-permute-done((bf16[256,512]{1,0:T(8,128)(2,1)S(1)}, bf16[256,512]{1,0:T(8,128)(2,1)S(1)}, u32[]{:S(2)}, u32[]{:S(2)}) %collective-permute-start.16) | collective-permute-done | bytes 262176 | tf_op jit(solution)/shard_map/ppermute | solution.py:45
  97.0 0.7 finish.5.rest_0_
  97.7 4.9 %collective-permute-done.15.received = bf16[256,512]{1,0:T(8,128)(2,1)S(1)} collective-permute-done((bf16[256,512]{1,0:T(8,128)(2,1)S(1)}, bf16[256,512]{1,0:T(8,128)(2,1)S(1)}, u32[]{:S(2)}, u32[]{:S(2)}) %collective-permute-start.15) | collective-permute-done | bytes 262176 | tf_op jit(solution)/shard_map/ppermute | solution.py:45
  102.6 0.7 finish.6.rest_0_
  103.3 4.1 %collective-permute-done.14.received = bf16[256,512]{1,0:T(8,128)(2,1)S(1)} collective-permute-done((bf16[256,512]{1,0:T(8,128)(2,1)S(1)}, bf16[256,512]{1,0:T(8,128)(2,1)S(1)}, u32[]{:S(2)}, u32[]{:S(2)}) %collective-permute-start.14) | collective-permute-done | bytes 262176 | tf_op jit(solution)/shard_map/ppermute | solution.py:45
  107.4 0.8 finish.7
  (24 shorter events, 0.2 us)
Async XLA Ops:
  0.0 1.9 %copy-start = (bf16[256,512]{1,0:T(8,128)(2,1)S(1)}, bf16[256,512]{1,0:T(8,128)(2,1)}, u32[]{:S(2)}) copy-start(bf16[256,512]{1,0:T(8,128)(2,1)} %queries.1) | copy-start | bytes 786436
  3.0 28.4 %collective-permute-start.2 = (bf16[128,1024]{1,0:T(8,128)(2,1)S(1)}, bf16[128,1024]{1,0:T(8,128)(2,1)S(1)}, u32[]{:S(2)}, u32[]{:S(2)}) collective-permute-start(bf16[128,1024]{1,0:T(8,128)(2,1)S(1)} %turn.1), channel_id=1, source_target_pairs={{0,1},{1,0},{2,3},{3,2},{4,5},{5,4},{6,7},{7,6},{8,9},{9,8},{10,11... | collective-permute-start | bytes 786440 | tf_op jit(solution)/shard_map/ppermute | solution.py:45
  3.1 34.3 %copy-start.1 = (s32[8]{0:T(128)S(1)}, s32[8]{0:T(128)}, u32[]{:S(2)}) copy-start(s32[8]{0:T(128)} %lengths.13) | copy-start | bytes 100
  3.2 17.4 %collective-permute-start.1 = (bf16[256,256]{1,0:T(8,128)(2,1)S(1)}, bf16[256,256]{1,0:T(8,128)(2,1)S(1)}, u32[]{:S(2)}, u32[]{:S(2)}) collective-permute-start(bf16[256,256]{1,0:T(8,128)(2,1)S(1)} %pad_maximum_fusion.3), channel_id=1, source_target_pairs={{0,32},{1,113},{2,34},{3,115},{4,36},{5,117},{6,38},{7,119},{8,40}... | collective-permute-start | bytes 393224 | tf_op jit(solution)/shard_map/ppermute | solution.py:45
  8.4 12.2 %collective-permute-start = (bf16[256,256]{1,0:T(8,128)(2,1)S(1)}, bf16[256,256]{1,0:T(8,128)(2,1)S(1)}, u32[]{:S(2)}, u32[]{:S(2)}) collective-permute-start(bf16[256,256]{1,0:T(8,128)(2,1)S(1)} %pad_maximum_fusion.3), channel_id=1, source_target_pairs={{0,16},{1,129},{2,18},{3,131},{4,20},{5,133},{6,22},{7,135},{8,24}... | collective-permute-start | bytes 393224 | tf_op jit(solution)/shard_map/ppermute | solution.py:45
  12.2 13.2 %collective-permute-start.4 = (bf16[256,256]{1,0:T(8,128)(2,1)S(1)}, bf16[256,256]{1,0:T(8,128)(2,1)S(1)}, u32[]{:S(2)}, u32[]{:S(2)}) collective-permute-start(bf16[256,256]{1,0:T(8,128)(2,1)S(1)} %pad_maximum_fusion.3), channel_id=1, source_target_pairs={{0,64},{1,81},{2,66},{3,83},{4,68},{5,85},{6,70},{7,87},{8,72},{9,... | collective-permute-start | bytes 393224 | tf_op jit(solution)/shard_map/ppermute | solution.py:45
  18.6 12.7 %collective-permute-start.3 = (bf16[256,256]{1,0:T(8,128)(2,1)S(1)}, bf16[256,256]{1,0:T(8,128)(2,1)S(1)}, u32[]{:S(2)}, u32[]{:S(2)}) collective-permute-start(bf16[256,256]{1,0:T(8,128)(2,1)S(1)} %pad_maximum_fusion.3), channel_id=1, source_target_pairs={{0,48},{1,97},{2,50},{3,99},{4,52},{5,101},{6,54},{7,103},{8,56},{... | collective-permute-start | bytes 393224 | tf_op jit(solution)/shard_map/ppermute | solution.py:45
  31.4 36.0 %collective-permute-start.12 = (bf16[512,8192]{1,0:T(8,128)(2,1)}, bf16[512,8192]{1,0:T(8,128)(2,1)S(1)}, u32[]{:S(2)}, u32[]{:S(2)}) collective-permute-start(bf16[512,8192]{1,0:T(8,128)(2,1)} %rest_1_.1), channel_id=1, source_target_pairs={{0,1},{1,0},{2,3},{3,2},{4,5},{5,4},{6,7},{7,6},{8,9},{9,8},{10,11... | collective-permute-start | bytes 25165832 | tf_op jit(solution)/shard_map/ppermute | solution.py:45
  31.4 29.5 %collective-permute-start.11 = (bf16[256,256]{1,0:T(8,128)(2,1)S(1)}, bf16[256,256]{1,0:T(8,128)(2,1)S(1)}, u32[]{:S(2)}, u32[]{:S(2)}) collective-permute-start(bf16[256,256]{1,0:T(8,128)(2,1)S(1)} %pad_maximum_fusion.3), channel_id=1, source_target_pairs={{12,144},{14,146},{28,160},{30,162},{44,176},{46,178},{60,192},{62... | collective-permute-start | bytes 393224 | tf_op jit(solution)/shard_map/ppermute | solution.py:45
  32.1 30.8 %collective-permute-start.10 = (bf16[640,256]{1,0:T(8,128)(2,1)S(1)}, bf16[640,256]{1,0:T(8,128)(2,1)S(1)}, u32[]{:S(2)}, u32[]{:S(2)}) collective-permute-start(bf16[640,256]{1,0:T(8,128)(2,1)S(1)} %pad_maximum_fusion.1), channel_id=1, source_target_pairs={{0,8},{1,9},{2,10},{3,11},{4,12},{5,13},{6,14},{7,15},{8,0},{9,1},... | collective-permute-start | bytes 983048 | tf_op jit(solution)/shard_map/ppermute | solution.py:45
  35.3 20.6 %collective-permute-start.6 = (bf16[640,256]{1,0:T(8,128)(2,1)S(1)}, bf16[640,256]{1,0:T(8,128)(2,1)S(1)}, u32[]{:S(2)}, u32[]{:S(2)}) collective-permute-start(bf16[640,256]{1,0:T(8,128)(2,1)S(1)} %pad_maximum_fusion.1), channel_id=1, source_target_pairs={{0,12},{1,13},{2,14},{3,15},{4,0},{5,1},{6,2},{7,3},{8,4},{9,5},{1... | collective-permute-start | bytes 983048 | tf_op jit(solution)/shard_map/ppermute | solution.py:45
  36.4 14.4 %collective-permute-start.5 = (bf16[640,256]{1,0:T(8,128)(2,1)S(1)}, bf16[640,256]{1,0:T(8,128)(2,1)S(1)}, u32[]{:S(2)}, u32[]{:S(2)}) collective-permute-start(bf16[640,256]{1,0:T(8,128)(2,1)S(1)} %pad_maximum_fusion.1), channel_id=1, source_target_pairs={{0,4},{1,5},{2,6},{3,7},{4,8},{5,9},{6,10},{7,11},{8,12},{9,13},{1... | collective-permute-start | bytes 983048 | tf_op jit(solution)/shard_map/ppermute | solution.py:45
  50.8 16.6 %collective-permute-start.9 = (bf16[512,256]{1,0:T(8,128)(2,1)S(1)}, bf16[512,256]{1,0:T(8,128)(2,1)S(1)}, u32[]{:S(2)}, u32[]{:S(2)}) collective-permute-start(bf16[512,256]{1,0:T(8,128)(2,1)S(1)} %pad_maximum_fusion.2), channel_id=1, source_target_pairs={{0,4},{1,5},{2,6},{3,7},{4,8},{5,9},{6,10},{7,11},{8,12},{9,13},{1... | collective-permute-start | bytes 786440 | tf_op jit(solution)/shard_map/ppermute | solution.py:45
  56.0 14.3 %collective-permute-start.8 = (bf16[512,256]{1,0:T(8,128)(2,1)S(1)}, bf16[512,256]{1,0:T(8,128)(2,1)S(1)}, u32[]{:S(2)}, u32[]{:S(2)}) collective-permute-start(bf16[512,256]{1,0:T(8,128)(2,1)S(1)} %pad_maximum_fusion.2), channel_id=1, source_target_pairs={{0,12},{1,13},{2,14},{3,15},{4,0},{5,1},{6,2},{7,3},{8,4},{9,5},{1... | collective-permute-start | bytes 786440 | tf_op jit(solution)/shard_map/ppermute | solution.py:45
  57.2 21.9 %slice-start = ((s8[8388608]{0:T(1024)(128)(4,1)}), s8[4194304]{0:T(1024)(128)(4,1)S(1)}, s32[]{:S(2)}) async-start(s8[8388608]{0:T(1024)(128)(4,1)} %bitcast.10), calls=%async_computation | async-start | bytes 8388608
  60.8 12.3 %collective-permute-start.7 = (bf16[512,256]{1,0:T(8,128)(2,1)S(1)}, bf16[512,256]{1,0:T(8,128)(2,1)S(1)}, u32[]{:S(2)}, u32[]{:S(2)}) collective-permute-start(bf16[512,256]{1,0:T(8,128)(2,1)S(1)} %pad_maximum_fusion.2), channel_id=1, source_target_pairs={{0,8},{1,9},{2,10},{3,11},{4,12},{5,13},{6,14},{7,15},{8,0},{9,1},... | collective-permute-start | bytes 786440 | tf_op jit(solution)/shard_map/ppermute | solution.py:45
  67.3 11.8 %slice-start.1 = ((s8[8388608]{0:T(1024)(128)(4,1)}), s8[4194304]{0:T(1024)(128)(4,1)S(1)}, s32[]{:S(2)}) async-start(s8[8388608]{0:T(1024)(128)(4,1)} %bitcast.10), calls=%async_computation.1 | async-start | bytes 8388608
  76.3 2.8 %collective-permute-start.13 = (f32[136,2048]{1,0:T(8,128)S(1)}, f32[136,2048]{1,0:T(8,128)S(1)}, u32[]{:S(2)}, u32[]{:S(2)}) collective-permute-start(f32[136,2048]{1,0:T(8,128)S(1)} %attend.13.rest_0_), channel_id=1, source_target_pairs={{0,1},{1,0},{2,3},{3,2},{4,5},{5,4},{6,7},{7,6},{8,9},{9,8},{10,11... | collective-permute-start | bytes 3342344 | tf_op jit(solution)/shard_map/ppermute | solution.py:45
  80.6 12.6 %collective-permute-start.17 = (bf16[256,512]{1,0:T(8,128)(2,1)S(1)}, bf16[256,512]{1,0:T(8,128)(2,1)S(1)}, u32[]{:S(2)}, u32[]{:S(2)}) collective-permute-start(bf16[256,512]{1,0:T(8,128)(2,1)S(1)} %get-tuple-element.40), channel_id=1, source_target_pairs={{0,2},{1,3},{2,0},{3,1},{4,6},{5,7},{6,4},{7,5},{8,10},{9,11},{10,... | collective-permute-start | bytes 786440 | tf_op jit(solution)/shard_map/ppermute | solution.py:45
  84.4 12.5 %collective-permute-start.16 = (bf16[256,512]{1,0:T(8,128)(2,1)S(1)}, bf16[256,512]{1,0:T(8,128)(2,1)S(1)}, u32[]{:S(2)}, u32[]{:S(2)}) collective-permute-start(bf16[256,512]{1,0:T(8,128)(2,1)S(1)} %get-tuple-element.39), channel_id=1, source_target_pairs={{0,2},{1,3},{2,0},{3,1},{4,6},{5,7},{6,4},{7,5},{8,10},{9,11},{10,... | collective-permute-start | bytes 786440 | tf_op jit(solution)/shard_map/ppermute | solution.py:45
  86.7 15.9 %collective-permute-start.15 = (bf16[256,512]{1,0:T(8,128)(2,1)S(1)}, bf16[256,512]{1,0:T(8,128)(2,1)S(1)}, u32[]{:S(2)}, u32[]{:S(2)}) collective-permute-start(bf16[256,512]{1,0:T(8,128)(2,1)S(1)} %get-tuple-element.38), channel_id=1, source_target_pairs={{0,2},{1,3},{2,0},{3,1},{4,6},{5,7},{6,4},{7,5},{8,10},{9,11},{10,... | collective-permute-start | bytes 786440 | tf_op jit(solution)/shard_map/ppermute | solution.py:45
  88.1 19.3 %collective-permute-start.14 = (bf16[256,512]{1,0:T(8,128)(2,1)S(1)}, bf16[256,512]{1,0:T(8,128)(2,1)S(1)}, u32[]{:S(2)}, u32[]{:S(2)}) collective-permute-start(bf16[256,512]{1,0:T(8,128)(2,1)S(1)} %get-tuple-element.37), channel_id=1, source_target_pairs={{0,2},{1,3},{2,0},{3,1},{4,6},{5,7},{6,4},{7,5},{8,10},{9,11},{10,... | collective-permute-start | bytes 786440 | tf_op jit(solution)/shard_map/ppermute | solution.py:45

commit v3 on v2

--- a/solution.py
+++ b/solution.py
@@ -239,24 +239,28 @@
     _, hi, core, _, _ = place(ids)
     weights, sems = rest[-2:]
     if merging:
-        mine, theirs, own_weight, other_weight, attended = rest[:5]
-        outs = rest[5:-2]
+        mine, theirs, pair, attended = rest[:4]
+        outs = rest[4:-2]
     else:
-        attended, own_weight, other_weight = rest[:3]
-        outs = rest[3:-2]
+        attended, pair = rest[:2]
+        outs = rest[2:-2]
     at = (2 * (1 - hi if other_side else hi) + core) * OUT_COLUMNS + first
     pieces = weights.shape[0]
+
+    def copy(i, j):
+        rows = pl.ds(pl.multiple_of((core if j == 0 else 1 - core) * half, half), half)
+        columns = pl.ds(pl.multiple_of(at + i * TILE, TILE), TILE)
+        return pltpu.make_async_copy(pair.at[rows, columns], weights.at[i, j], sems.at[i, j])
+
     for i in range(pieces):
-        columns = pl.ds(pl.multiple_of(at + i * TILE, TILE), TILE)
-        for j, weight in enumerate((own_weight, other_weight)):
-            pltpu.make_async_copy(weight.at[:, columns], weights.at[i, j], sems.at[i, j]).start()
+        copy(i, 0).start()
+        copy(i, 1).start()
     if merging:
         merged(mine, theirs, attended)
     out, filled = 0, 0
     for i in range(pieces):
-        columns = pl.ds(pl.multiple_of(at + i * TILE, TILE), TILE)
-        for j, weight in enumerate((own_weight, other_weight)):
-            pltpu.make_async_copy(weight.at[:, columns], weights.at[i, j], sems.at[i, j]).wait()
+        copy(i, 0).wait()
+        copy(i, 1).wait()
         total = jnp.dot(attended[:, :half], weights[i, 0], preferred_element_type=jnp.float32)
         total += jnp.dot(attended[:, half:], weights[i, 1], preferred_element_type=jnp.float32)
         outs[out][:, filled : filled + TILE] = total.astype(outs[out].dtype)
@@ -277,16 +281,16 @@
         out_shape=shapes,
         in_specs=[pl.BlockSpec(memory_space=pltpu.SMEM)]
         + [vmem] * len(operands)
-        + [pl.BlockSpec(memory_space=pltpu.HBM)] * 2,
+        + [pl.BlockSpec(memory_space=pltpu.HBM)],
         out_specs=[vmem] * len(shapes),
         scratch_shapes=[
             pltpu.VMEM((pieces, 2, half, TILE), jnp.bfloat16),
             pltpu.SemaphoreType.DMA((pieces, 2)),
         ],
-        compiler_params=pltpu.CompilerParams(vmem_limit_bytes=32 * MIB),
+        compiler_params=pltpu.CompilerParams(vmem_limit_bytes=52 * MIB),
         cost_estimate=pl.CostEstimate(flops=1, bytes_accessed=1, transcendentals=0),
         name="project",
-    )(ids, *operands, *weights)
+    )(ids, *operands, weights)
 
 
 def finish_kernel(kept, received, *rest):
@@ -329,24 +333,26 @@
     own_value = lax.dynamic_index_in_dim(value_heads, hi, 1, keepdims=False)
     block = jnp.concatenate([own_key, own_value], axis=1)
 
-    near = [permute(block, along_rows(step)) for step in (1, 2, 3, 4)]
-    far = permute(block, far_block)
-    half = lax.dynamic_slice_in_dim(block, core * (BLOCK // 2), BLOCK // 2, 0)
-    shifts = (1, -1, 2)
-    group_1 = jnp.concatenate([half, near[0], near[1]], axis=0)
+    weights = lax.all_gather(
+        out_weight, "tensor", axis=0, tiled=True, axis_index_groups=[[0, 1], [2, 3]]
+    )
     q_own = turn(queries, cosine, sine)
     q_other = permute(q_own, other_core)
-    group_1, out_weight, q_other, *near[2:] = lax.optimization_barrier(
-        (group_1, out_weight, q_other, *near[2:])
-    )
-    other_weight = permute(out_weight, other_core)
+    near = [permute(block, along_rows(step)) for step in (1, 2)]
+    half = lax.dynamic_slice_in_dim(block, core * (BLOCK // 2), BLOCK // 2, 0)
+    group_1 = jnp.concatenate([half, *near], axis=0)
+    group_1, block, q_other = lax.optimization_barrier((group_1, block, q_other))
+    shifts = (1, -1, 2)
     columns_1 = [permute(group_1, in_row(shift)) for shift in shifts]
-    group_2 = jnp.concatenate([near[2], near[3]], axis=0)
+    near += [permute(block, along_rows(step)) for step in (3, 4)]
+    group_2 = jnp.concatenate(near[2:], axis=0)
 
     q_all = jnp.concatenate([q_own, q_other], axis=1)
     step = functools.partial(attend, ids, doc_lengths, q_all)
 
     state = step([half] + near, [("half", 0)] + [(k, 0) for k in (1, 2, 3, 4)])
+    block, state = lax.optimization_barrier((block, state))
+    far = permute(block, far_block)
     columns_2 = []
     for shift, keys in zip(shifts, columns_1):
         group_2, state = lax.optimization_barrier((group_2, state))
@@ -356,8 +362,6 @@
             state = step([keys, far], kinds + [("far", 0)], state)
         else:
             state = step([keys], kinds, state)
-    state, other_weight = lax.optimization_barrier((state, other_weight))
-    weights = (out_weight, other_weight)
     for shift, keys in zip(shifts, columns_2):
         state = step([keys], [(3, shift), (4, shift)], state)
 

time: 108 us -> 121 us (1.12)
  the two profiles are of different devices: /device:TPU:6 before, /device:TPU:70 now
where the time goes in v3:
time: 121 us; the launch traced here: 120 us
  Pallas kernels  40.6 us (34%)
  starting transfers between devices  34.5 us (29%)
  waiting for transfers between devices  26.9 us (22%)
  between operations  13.7 us (11%)
  local copies, waits for them, and re-layouts  3.11 us (3%)
    ppermute x17, starting transfers between devices, permute(): return lax.ppermute(x, ('seq', 'tensor'), device_perm(move))  34.5 us
    ppermute x17, waiting for transfers between devices, permute(): return lax.ppermute(x, ('seq', 'tensor'), device_perm(move))  26.2 us
    pallas_call x7, Pallas kernels, attend(): pl.pallas_call(functools.partial(attend_kernel, kinds, state is None), ou...  25.4 us
    pallas_call x3, Pallas kernels, project(): pl.pallas_call(functools.partial(project_kernel, other_side, first, mergi...  11.2 us
    pallas_call x4, Pallas kernels, finish(): pl.pallas_call(finish_kernel, out_shape=jax.ShapeDtypeStruct(kept.shape,...  3.06 us
    unnamed x13, local copies, waits for them, and re-layouts  2.83 us
  transfers between devices with their start and end apart: 18, of which 7 were waited for; matrix products, arithmetic and copies ran while one was open for 1% of the time, Pallas kernels for 31%

profile of v3, /device:TPU:70, one launch (start us, length us, event | category | flops | bytes accessed | tf_op | source)
XLA Modules:
  0.0 119.7 jit_solution(6846995991404833369)
XLA Ops:
  6.5 0.7 all-gather.2.cloned.1.call-update
  7.3 0.1 copy-done.4
  7.4 0.1 copy-done.5
  7.5 0.3 constant_dynamic-slice_fusion.1
  7.9 0.6 subtract_convert_fusion
  8.4 0.1 pad_maximum_fusion.3
  8.6 6.4 %collective-permute-start.1 = (bf16[256,256]{1,0:T(8,128)(2,1)S(1)}, bf16[256,256]{1,0:T(8,128)(2,1)S(1)}, u32[]{:S(2)}, u32[]{:S(2)}) collective-permute-start(bf16[256,256]{1,0:T(8,128)(2,1)S(1)} %pad_maximum_fusion.3), channel_id=1, source_target_pairs={{0,32},{1,113},{2,34},{3,115},{4,36},{5,117},{6,38},{7,119},{8,40}... | collective-permute-start | bytes 393224 | tf_op jit(solution)/shard_map/ppermute | solution.py:45
  14.9 2.9 %collective-permute-start = (bf16[256,256]{1,0:T(8,128)(2,1)S(1)}, bf16[256,256]{1,0:T(8,128)(2,1)S(1)}, u32[]{:S(2)}, u32[]{:S(2)}) collective-permute-start(bf16[256,256]{1,0:T(8,128)(2,1)S(1)} %pad_maximum_fusion.3), channel_id=1, source_target_pairs={{0,16},{1,129},{2,18},{3,131},{4,20},{5,133},{6,22},{7,135},{8,24}... | collective-permute-start | bytes 393224 | tf_op jit(solution)/shard_map/ppermute | solution.py:45
  17.9 1.0 turn.1
  18.9 0.1 collective-permute-start.2
  19.0 0.1 pad_add_fusion.ids
  19.1 2.7 %collective-permute-done.rest_1_ = bf16[256,256]{1,0:T(8,128)(2,1)S(1)} collective-permute-done((bf16[256,256]{1,0:T(8,128)(2,1)S(1)}, bf16[256,256]{1,0:T(8,128)(2,1)S(1)}, u32[]{:S(2)}, u32[]{:S(2)}) %collective-permute-start) | collective-permute-done | bytes 131104 | tf_op jit(solution)/shard_map/ppermute | solution.py:45
  21.8 4.2 %collective-permute-start.4 = (bf16[256,256]{1,0:T(8,128)(2,1)S(1)}, bf16[256,256]{1,0:T(8,128)(2,1)S(1)}, u32[]{:S(2)}, u32[]{:S(2)}) collective-permute-start(bf16[256,256]{1,0:T(8,128)(2,1)S(1)} %pad_maximum_fusion.3), channel_id=1, source_target_pairs={{0,64},{1,81},{2,66},{3,83},{4,68},{5,85},{6,70},{7,87},{8,72},{9,... | collective-permute-start | bytes 393224 | tf_op jit(solution)/shard_map/ppermute | solution.py:45
  26.0 1.9 %collective-permute-start.3 = (bf16[256,256]{1,0:T(8,128)(2,1)S(1)}, bf16[256,256]{1,0:T(8,128)(2,1)S(1)}, u32[]{:S(2)}, u32[]{:S(2)}) collective-permute-start(bf16[256,256]{1,0:T(8,128)(2,1)S(1)} %pad_maximum_fusion.3), channel_id=1, source_target_pairs={{0,48},{1,97},{2,50},{3,99},{4,52},{5,101},{6,54},{7,103},{8,56},{... | collective-permute-start | bytes 393224 | tf_op jit(solution)/shard_map/ppermute | solution.py:45
  27.9 1.7 %collective-permute-start.5 = (bf16[640,256]{1,0:T(8,128)(2,1)S(1)}, bf16[640,256]{1,0:T(8,128)(2,1)S(1)}, u32[]{:S(2)}, u32[]{:S(2)}) collective-permute-start(bf16[640,256]{1,0:T(8,128)(2,1)S(1)} %pad_maximum_fusion.1), channel_id=1, source_target_pairs={{0,4},{1,5},{2,6},{3,7},{4,8},{5,9},{6,10},{7,11},{8,12},{9,13},{1... | collective-permute-start | bytes 983048 | tf_op jit(solution)/shard_map/ppermute | solution.py:45
  29.6 1.7 %collective-permute-start.6 = (bf16[640,256]{1,0:T(8,128)(2,1)S(1)}, bf16[640,256]{1,0:T(8,128)(2,1)S(1)}, u32[]{:S(2)}, u32[]{:S(2)}) collective-permute-start(bf16[640,256]{1,0:T(8,128)(2,1)S(1)} %pad_maximum_fusion.1), channel_id=1, source_target_pairs={{0,12},{1,13},{2,14},{3,15},{4,0},{5,1},{6,2},{7,3},{8,4},{9,5},{1... | collective-permute-start | bytes 983048 | tf_op jit(solution)/shard_map/ppermute | solution.py:45
  31.3 2.0 %collective-permute-start.10 = (bf16[640,256]{1,0:T(8,128)(2,1)S(1)}, bf16[640,256]{1,0:T(8,128)(2,1)S(1)}, u32[]{:S(2)}, u32[]{:S(2)}) collective-permute-start(bf16[640,256]{1,0:T(8,128)(2,1)S(1)} %pad_maximum_fusion.1), channel_id=1, source_target_pairs={{0,8},{1,9},{2,10},{3,11},{4,12},{5,13},{6,14},{7,15},{8,0},{9,1},... | collective-permute-start | bytes 983048 | tf_op jit(solution)/shard_map/ppermute | solution.py:45
  33.3 2.2 %collective-permute-done.4.rest_4_ = bf16[256,256]{1,0:T(8,128)(2,1)S(1)} collective-permute-done((bf16[256,256]{1,0:T(8,128)(2,1)S(1)}, bf16[256,256]{1,0:T(8,128)(2,1)S(1)}, u32[]{:S(2)}, u32[]{:S(2)}) %collective-permute-start.4) | collective-permute-done | bytes 131104 | tf_op jit(solution)/shard_map/ppermute | solution.py:45
  35.5 2.3 %collective-permute-done.3.rest_3_ = bf16[256,256]{1,0:T(8,128)(2,1)S(1)} collective-permute-done((bf16[256,256]{1,0:T(8,128)(2,1)S(1)}, bf16[256,256]{1,0:T(8,128)(2,1)S(1)}, u32[]{:S(2)}, u32[]{:S(2)}) %collective-permute-start.3) | collective-permute-done | bytes 131104 | tf_op jit(solution)/shard_map/ppermute | solution.py:45
  37.8 5.0 %attend.7.rest_1_ = f32[136,2048]{1,0:T(8,128)S(1)} custom-call(s32[2]{0:T(128)S(1)} %pad_add_fusion.ids, s32[8]{0:T(128)S(1)} %copy-done.2, bf16[128,2048]{1,0:T(8,128)(2,1)S(1)} %pad_maximum_fusion.q_ref, bf16[128,256]{1,0:T(8,128)(2,1)S(1)} %constant_dynamic-slice_fusion.rest_0_, bf16[256,256]{1,0:T(8,128)(2,1)S(1)} %collective-permute-done.rest_1_, ...), custom_call_target="tpu_custom_call" | custom-call | flops 1 | bytes 1 | tf_op jit(solution)/shard_map/attend/pallas_call | solution.py:191
  42.8 1.7 %collective-permute-start.9 = (bf16[512,256]{1,0:T(8,128)(2,1)S(1)}, bf16[512,256]{1,0:T(8,128)(2,1)S(1)}, u32[]{:S(2)}, u32[]{:S(2)}) collective-permute-start(bf16[512,256]{1,0:T(8,128)(2,1)S(1)} %pad_maximum_fusion.2), channel_id=1, source_target_pairs={{0,4},{1,5},{2,6},{3,7},{4,8},{5,9},{6,10},{7,11},{8,12},{9,13},{1... | collective-permute-start | bytes 786440 | tf_op jit(solution)/shard_map/ppermute | solution.py:45
  44.5 3.5 %attend.8.rest_1_ = f32[136,2048]{1,0:T(8,128)S(1)} custom-call(s32[2]{0:T(128)S(1)} %pad_add_fusion.ids, s32[8]{0:T(128)S(1)} %copy-done.2, bf16[128,2048]{1,0:T(8,128)(2,1)S(1)} %pad_maximum_fusion.q_ref, bf16[640,256]{1,0:T(8,128)(2,1)S(1)} %collective-permute-done.5.rest_0_, f32[136,2048]{1,0:T(8,128)S(1)} %attend.7.rest_1_), custom_call_target="tpu_custom_call", output_to_operand_aliasing={{}: (4, {})} | custom-call | flops 1 | bytes 1 | tf_op jit(solution)/shard_map/attend/pallas_call | solution.py:191
  47.9 1.4 %collective-permute-start.8 = (bf16[512,256]{1,0:T(8,128)(2,1)S(1)}, bf16[512,256]{1,0:T(8,128)(2,1)S(1)}, u32[]{:S(2)}, u32[]{:S(2)}) collective-permute-start(bf16[512,256]{1,0:T(8,128)(2,1)S(1)} %pad_maximum_fusion.2), channel_id=1, source_target_pairs={{0,12},{1,13},{2,14},{3,15},{4,0},{5,1},{6,2},{7,3},{8,4},{9,5},{1... | collective-permute-start | bytes 786440 | tf_op jit(solution)/shard_map/ppermute | solution.py:45
  49.3 3.6 %attend.9.rest_2_ = f32[136,2048]{1,0:T(8,128)S(1)} custom-call(s32[2]{0:T(128)S(1)} %pad_add_fusion.ids, s32[8]{0:T(128)S(1)} %copy-done.2, bf16[128,2048]{1,0:T(8,128)(2,1)S(1)} %pad_maximum_fusion.q_ref, bf16[640,256]{1,0:T(8,128)(2,1)S(1)} %collective-permute-done.6.rest_0_, f32[136,2048]{1,0:T(8,128)S(1)} %attend.8.rest_1_), custom_call_target="tpu_custom_call", output_to_operand_aliasing={{}: (4, {})} | custom-call | flops 1 | bytes 1 | tf_op jit(solution)/shard_map/attend/pallas_call | solution.py:191
  53.0 2.1 %collective-permute-start.7 = (bf16[512,256]{1,0:T(8,128)(2,1)S(1)}, bf16[512,256]{1,0:T(8,128)(2,1)S(1)}, u32[]{:S(2)}, u32[]{:S(2)}) collective-permute-start(bf16[512,256]{1,0:T(8,128)(2,1)S(1)} %pad_maximum_fusion.2), channel_id=1, source_target_pairs={{0,8},{1,9},{2,10},{3,11},{4,12},{5,13},{6,14},{7,15},{8,0},{9,1},... | collective-permute-start | bytes 786440 | tf_op jit(solution)/shard_map/ppermute | solution.py:45
  55.1 1.3 %collective-permute-start.11 = (bf16[256,256]{1,0:T(8,128)(2,1)S(1)}, bf16[256,256]{1,0:T(8,128)(2,1)S(1)}, u32[]{:S(2)}, u32[]{:S(2)}) collective-permute-start(bf16[256,256]{1,0:T(8,128)(2,1)S(1)} %pad_maximum_fusion.3), channel_id=1, source_target_pairs={{12,144},{14,146},{28,160},{30,162},{44,176},{46,178},{60,192},{62... | collective-permute-start | bytes 393224 | tf_op jit(solution)/shard_map/ppermute | solution.py:45
  56.3 8.6 %collective-permute-done.11.rest_1_ = bf16[256,256]{1,0:T(8,128)(2,1)S(1)} collective-permute-done((bf16[256,256]{1,0:T(8,128)(2,1)S(1)}, bf16[256,256]{1,0:T(8,128)(2,1)S(1)}, u32[]{:S(2)}, u32[]{:S(2)}) %collective-permute-start.11) | collective-permute-done | bytes 131104 | tf_op jit(solution)/shard_map/ppermute | solution.py:45
  64.9 4.5 %attend.10.rest_1_ = f32[136,2048]{1,0:T(8,128)S(1)} custom-call(s32[2]{0:T(128)S(1)} %pad_add_fusion.ids, s32[8]{0:T(128)S(1)} %copy-done.2, bf16[128,2048]{1,0:T(8,128)(2,1)S(1)} %pad_maximum_fusion.q_ref, bf16[640,256]{1,0:T(8,128)(2,1)S(1)} %collective-permute-done.10.rest_0_, ...), custom_call_target="tpu_custom_call", output_to_operand_aliasing={{}: (5, {})} | custom-call | flops 1 | bytes 1 | tf_op jit(solution)/shard_map/attend/pallas_call | solution.py:191
  69.4 2.9 %attend.11.rest_1_ = f32[136,2048]{1,0:T(8,128)S(1)} custom-call(s32[2]{0:T(128)S(1)} %pad_add_fusion.ids, s32[8]{0:T(128)S(1)} %copy-done.2, bf16[128,2048]{1,0:T(8,128)(2,1)S(1)} %pad_maximum_fusion.q_ref, bf16[512,256]{1,0:T(8,128)(2,1)S(1)} %collective-permute-done.9.rest_0_, f32[136,2048]{1,0:T(8,128)S(1)} %attend.10.rest_1_), custom_call_target="tpu_custom_call", output_to_operand_aliasing={{}: (4, {})} | custom-call | flops 1 | bytes 1 | tf_op jit(solution)/shard_map/attend/pallas_call | solution.py:191
  72.3 2.9 %attend.12.rest_1_ = f32[136,2048]{1,0:T(8,128)S(1)} custom-call(s32[2]{0:T(128)S(1)} %pad_add_fusion.ids, s32[8]{0:T(128)S(1)} %copy-done.2, bf16[128,2048]{1,0:T(8,128)(2,1)S(1)} %pad_maximum_fusion.q_ref, bf16[512,256]{1,0:T(8,128)(2,1)S(1)} %collective-permute-done.8.rest_0_, f32[136,2048]{1,0:T(8,128)S(1)} %attend.11.rest_1_), custom_call_target="tpu_custom_call", output_to_operand_aliasing={{}: (4, {})} | custom-call | flops 1 | bytes 1 | tf_op jit(solution)/shard_map/attend/pallas_call | solution.py:191
  75.2 3.1 %attend.13.rest_0_ = f32[136,2048]{1,0:T(8,128)S(1)} custom-call(s32[2]{0:T(128)S(1)} %pad_add_fusion.ids, s32[8]{0:T(128)S(1)} %copy-done.2, bf16[128,2048]{1,0:T(8,128)(2,1)S(1)} %pad_maximum_fusion.q_ref, bf16[512,256]{1,0:T(8,128)(2,1)S(1)} %collective-permute-done.7.rest_0_, f32[136,2048]{1,0:T(8,128)S(1)} %attend.12.rest_1_), custom_call_target="tpu_custom_call", output_to_operand_aliasing={{}: (4, {})} | custom-call | flops 1 | bytes 1 | tf_op jit(solution)/shard_map/attend/pallas_call | solution.py:191
  78.3 0.1 collective-permute-start.12
  78.4 2.7 %collective-permute-done.12.rest_1_ = f32[136,2048]{1,0:T(8,128)S(1)} collective-permute-done((f32[136,2048]{1,0:T(8,128)S(1)}, f32[136,2048]{1,0:T(8,128)S(1)}, u32[]{:S(2)}, u32[]{:S(2)}) %collective-permute-start.12) | collective-permute-done | bytes 1114144 | tf_op jit(solution)/shard_map/ppermute | solution.py:45
  81.2 1.0 copy-done.3
  82.2 3.1 %project.3 = (bf16[256,1024]{1,0:T(8,128)(2,1)S(1)}, bf16[256,512]{1,0:T(8,128)(2,1)S(1)}) custom-call(s32[2]{0:T(128)S(1)} %pad_add_fusion.ids, f32[136,2048]{1,0:T(8,128)S(1)} %attend.13.rest_0_, f32[136,2048]{1,0:T(8,128)} %copy-done.3, bf16[1024,8192]{1,0:T(8,128)(2,1)} %all-gather.2.cloned.1.call-done.rest_2_.rest_1_), custom_call_target="tpu_custom_call" | custom-call | flops 1 | bytes 1 | tf_op jit(solution)/shard_map/project/pallas_call | solution.py:279
  85.3 1.3 %collective-permute-start.16 = (bf16[256,512]{1,0:T(8,128)(2,1)S(1)}, bf16[256,512]{1,0:T(8,128)(2,1)S(1)}, u32[]{:S(2)}, u32[]{:S(2)}) collective-permute-start(bf16[256,512]{1,0:T(8,128)(2,1)S(1)} %get-tuple-element.36), channel_id=1, source_target_pairs={{0,2},{1,3},{2,0},{3,1},{4,6},{5,7},{6,4},{7,5},{8,10},{9,11},{10,... | collective-permute-start | bytes 786440 | tf_op jit(solution)/shard_map/ppermute | solution.py:45
  86.7 3.1 %project.5 = (bf16[256,512]{1,0:T(8,128)(2,1)S(1)}, bf16[256,512]{1,0:T(8,128)(2,1)S(1)}, bf16[256,512]{1,0:T(8,128)(2,1)S(1)}) custom-call(s32[2]{0:T(128)S(1)} %pad_add_fusion.ids, bf16[256,1024]{1,0:T(8,128)(2,1)S(1)} %get-tuple-element.32.rest_0_, bf16[1024,8192]{1,0:T(8,128)(2,1)} %all-gather.2.cloned.1.call-done.rest_2_.rest_1_), custom_call_target="tpu_custom_call" | custom-call | flops 1 | bytes 1 | tf_op jit(solution)/shard_map/project/pallas_call | solution.py:279
  89.8 2.4 %collective-permute-start.15 = (bf16[256,512]{1,0:T(8,128)(2,1)S(1)}, bf16[256,512]{1,0:T(8,128)(2,1)S(1)}, u32[]{:S(2)}, u32[]{:S(2)}) collective-permute-start(bf16[256,512]{1,0:T(8,128)(2,1)S(1)} %get-tuple-element.35), channel_id=1, source_target_pairs={{0,2},{1,3},{2,0},{3,1},{4,6},{5,7},{6,4},{7,5},{8,10},{9,11},{10,... | collective-permute-start | bytes 786440 | tf_op jit(solution)/shard_map/ppermute | solution.py:45
  92.2 1.2 %collective-permute-start.14 = (bf16[256,512]{1,0:T(8,128)(2,1)S(1)}, bf16[256,512]{1,0:T(8,128)(2,1)S(1)}, u32[]{:S(2)}, u32[]{:S(2)}) collective-permute-start(bf16[256,512]{1,0:T(8,128)(2,1)S(1)} %get-tuple-element.34), channel_id=1, source_target_pairs={{0,2},{1,3},{2,0},{3,1},{4,6},{5,7},{6,4},{7,5},{8,10},{9,11},{10,... | collective-permute-start | bytes 786440 | tf_op jit(solution)/shard_map/ppermute | solution.py:45
  93.4 2.3 %collective-permute-start.13 = (bf16[256,512]{1,0:T(8,128)(2,1)S(1)}, bf16[256,512]{1,0:T(8,128)(2,1)S(1)}, u32[]{:S(2)}, u32[]{:S(2)}) collective-permute-start(bf16[256,512]{1,0:T(8,128)(2,1)S(1)} %get-tuple-element.33), channel_id=1, source_target_pairs={{0,2},{1,3},{2,0},{3,1},{4,6},{5,7},{6,4},{7,5},{8,10},{9,11},{10,... | collective-permute-start | bytes 786440 | tf_op jit(solution)/shard_map/ppermute | solution.py:45
  95.7 4.9 %project.4.kept = f32[256,2048]{1,0:T(8,128)} custom-call(s32[2]{0:T(128)S(1)} %pad_add_fusion.ids, bf16[256,1024]{1,0:T(8,128)(2,1)S(1)} %get-tuple-element.32.rest_0_, bf16[1024,8192]{1,0:T(8,128)(2,1)} %all-gather.2.cloned.1.call-done.rest_2_.rest_1_), custom_call_target="tpu_custom_call" | custom-call | flops 1 | bytes 1 | tf_op jit(solution)/shard_map/project/pallas_call | solution.py:279
  100.6 1.6 %copy-done = f32[256,2048]{1,0:T(8,128)S(1)} copy-done((f32[256,2048]{1,0:T(8,128)S(1)}, f32[256,2048]{1,0:T(8,128)}, u32[]{:S(2)}) %copy-start) | copy-done | bytes 2097176
  102.2 0.8 finish.4.rest_0_
  103.0 0.8 finish.5.rest_0_
  103.8 3.5 %collective-permute-done.14.received = bf16[256,512]{1,0:T(8,128)(2,1)S(1)} collective-permute-done((bf16[256,512]{1,0:T(8,128)(2,1)S(1)}, bf16[256,512]{1,0:T(8,128)(2,1)S(1)}, u32[]{:S(2)}, u32[]{:S(2)}) %collective-permute-start.14) | collective-permute-done | bytes 262176 | tf_op jit(solution)/shard_map/ppermute | solution.py:45
  107.3 0.8 finish.6.rest_0_
  108.1 4.1 %collective-permute-done.13.received = bf16[256,512]{1,0:T(8,128)(2,1)S(1)} collective-permute-done((bf16[256,512]{1,0:T(8,128)(2,1)S(1)}, bf16[256,512]{1,0:T(8,128)(2,1)S(1)}, u32[]{:S(2)}, u32[]{:S(2)}) %collective-permute-start.13) | collective-permute-done | bytes 262176 | tf_op jit(solution)/shard_map/ppermute | solution.py:45
  112.1 0.8 finish.7
  (28 shorter events, 0.2 us)
Async XLA Ops:
  6.5 0.9 copy-start.4
  6.5 1.0 copy-start.5
  6.5 74.6 %all-gather.2.cloned.1.call-start = ((), (), s32[]{:S(2)}) async-start(), calls=%async_computation | async-start | bytes 25165824 | tf_op jit(solution)/shard_map/all_gather | solution.py:336
  7.3 10.6 %copy-start.1 = (bf16[256,512]{1,0:T(8,128)(2,1)S(1)}, bf16[256,512]{1,0:T(8,128)(2,1)}, u32[]{:S(2)}) copy-start(bf16[256,512]{1,0:T(8,128)(2,1)} %queries.1) | copy-start | bytes 786436
  8.6 10.6 %collective-permute-start.1 = (bf16[256,256]{1,0:T(8,128)(2,1)S(1)}, bf16[256,256]{1,0:T(8,128)(2,1)S(1)}, u32[]{:S(2)}, u32[]{:S(2)}) collective-permute-start(bf16[256,256]{1,0:T(8,128)(2,1)S(1)} %pad_maximum_fusion.3), channel_id=1, source_target_pairs={{0,32},{1,113},{2,34},{3,115},{4,36},{5,117},{6,38},{7,119},{8,40}... | collective-permute-start | bytes 393224 | tf_op jit(solution)/shard_map/ppermute | solution.py:45
  14.9 6.9 %collective-permute-start = (bf16[256,256]{1,0:T(8,128)(2,1)S(1)}, bf16[256,256]{1,0:T(8,128)(2,1)S(1)}, u32[]{:S(2)}, u32[]{:S(2)}) collective-permute-start(bf16[256,256]{1,0:T(8,128)(2,1)S(1)} %pad_maximum_fusion.3), channel_id=1, source_target_pairs={{0,16},{1,129},{2,18},{3,131},{4,20},{5,133},{6,22},{7,135},{8,24}... | collective-permute-start | bytes 393224 | tf_op jit(solution)/shard_map/ppermute | solution.py:45
  18.9 18.9 %copy-start.2 = (s32[8]{0:T(128)S(1)}, s32[8]{0:T(128)}, u32[]{:S(2)}) copy-start(s32[8]{0:T(128)} %lengths.13) | copy-start | bytes 100
  18.9 2.9 %collective-permute-start.2 = (bf16[128,1024]{1,0:T(8,128)(2,1)S(1)}, bf16[128,1024]{1,0:T(8,128)(2,1)S(1)}, u32[]{:S(2)}, u32[]{:S(2)}) collective-permute-start(bf16[128,1024]{1,0:T(8,128)(2,1)S(1)} %turn.1), channel_id=1, source_target_pairs={{0,1},{1,0},{2,3},{3,2},{4,5},{5,4},{6,7},{7,6},{8,9},{9,8},{10,11... | collective-permute-start | bytes 786440 | tf_op jit(solution)/shard_map/ppermute | solution.py:45
  21.8 13.6 %collective-permute-start.4 = (bf16[256,256]{1,0:T(8,128)(2,1)S(1)}, bf16[256,256]{1,0:T(8,128)(2,1)S(1)}, u32[]{:S(2)}, u32[]{:S(2)}) collective-permute-start(bf16[256,256]{1,0:T(8,128)(2,1)S(1)} %pad_maximum_fusion.3), channel_id=1, source_target_pairs={{0,64},{1,81},{2,66},{3,83},{4,68},{5,85},{6,70},{7,87},{8,72},{9,... | collective-permute-start | bytes 393224 | tf_op jit(solution)/shard_map/ppermute | solution.py:45
  26.0 11.8 %collective-permute-start.3 = (bf16[256,256]{1,0:T(8,128)(2,1)S(1)}, bf16[256,256]{1,0:T(8,128)(2,1)S(1)}, u32[]{:S(2)}, u32[]{:S(2)}) collective-permute-start(bf16[256,256]{1,0:T(8,128)(2,1)S(1)} %pad_maximum_fusion.3), channel_id=1, source_target_pairs={{0,48},{1,97},{2,50},{3,99},{4,52},{5,101},{6,54},{7,103},{8,56},{... | collective-permute-start | bytes 393224 | tf_op jit(solution)/shard_map/ppermute | solution.py:45
  27.9 16.5 %collective-permute-start.5 = (bf16[640,256]{1,0:T(8,128)(2,1)S(1)}, bf16[640,256]{1,0:T(8,128)(2,1)S(1)}, u32[]{:S(2)}, u32[]{:S(2)}) collective-permute-start(bf16[640,256]{1,0:T(8,128)(2,1)S(1)} %pad_maximum_fusion.1), channel_id=1, source_target_pairs={{0,4},{1,5},{2,6},{3,7},{4,8},{5,9},{6,10},{7,11},{8,12},{9,13},{1... | collective-permute-start | bytes 983048 | tf_op jit(solution)/shard_map/ppermute | solution.py:45
  29.6 19.7 %collective-permute-start.6 = (bf16[640,256]{1,0:T(8,128)(2,1)S(1)}, bf16[640,256]{1,0:T(8,128)(2,1)S(1)}, u32[]{:S(2)}, u32[]{:S(2)}) collective-permute-start(bf16[640,256]{1,0:T(8,128)(2,1)S(1)} %pad_maximum_fusion.1), channel_id=1, source_target_pairs={{0,12},{1,13},{2,14},{3,15},{4,0},{5,1},{6,2},{7,3},{8,4},{9,5},{1... | collective-permute-start | bytes 983048 | tf_op jit(solution)/shard_map/ppermute | solution.py:45
  31.3 33.7 %collective-permute-start.10 = (bf16[640,256]{1,0:T(8,128)(2,1)S(1)}, bf16[640,256]{1,0:T(8,128)(2,1)S(1)}, u32[]{:S(2)}, u32[]{:S(2)}) collective-permute-start(bf16[640,256]{1,0:T(8,128)(2,1)S(1)} %pad_maximum_fusion.1), channel_id=1, source_target_pairs={{0,8},{1,9},{2,10},{3,11},{4,12},{5,13},{6,14},{7,15},{8,0},{9,1},... | collective-permute-start | bytes 983048 | tf_op jit(solution)/shard_map/ppermute | solution.py:45
  42.8 26.6 %collective-permute-start.9 = (bf16[512,256]{1,0:T(8,128)(2,1)S(1)}, bf16[512,256]{1,0:T(8,128)(2,1)S(1)}, u32[]{:S(2)}, u32[]{:S(2)}) collective-permute-start(bf16[512,256]{1,0:T(8,128)(2,1)S(1)} %pad_maximum_fusion.2), channel_id=1, source_target_pairs={{0,4},{1,5},{2,6},{3,7},{4,8},{5,9},{6,10},{7,11},{8,12},{9,13},{1... | collective-permute-start | bytes 786440 | tf_op jit(solution)/shard_map/ppermute | solution.py:45
  47.9 24.4 %collective-permute-start.8 = (bf16[512,256]{1,0:T(8,128)(2,1)S(1)}, bf16[512,256]{1,0:T(8,128)(2,1)S(1)}, u32[]{:S(2)}, u32[]{:S(2)}) collective-permute-start(bf16[512,256]{1,0:T(8,128)(2,1)S(1)} %pad_maximum_fusion.2), channel_id=1, source_target_pairs={{0,12},{1,13},{2,14},{3,15},{4,0},{5,1},{6,2},{7,3},{8,4},{9,5},{1... | collective-permute-start | bytes 786440 | tf_op jit(solution)/shard_map/ppermute | solution.py:45
  53.0 22.2 %collective-permute-start.7 = (bf16[512,256]{1,0:T(8,128)(2,1)S(1)}, bf16[512,256]{1,0:T(8,128)(2,1)S(1)}, u32[]{:S(2)}, u32[]{:S(2)}) collective-permute-start(bf16[512,256]{1,0:T(8,128)(2,1)S(1)} %pad_maximum_fusion.2), channel_id=1, source_target_pairs={{0,8},{1,9},{2,10},{3,11},{4,12},{5,13},{6,14},{7,15},{8,0},{9,1},... | collective-permute-start | bytes 786440 | tf_op jit(solution)/shard_map/ppermute | solution.py:45
  55.1 9.9 %collective-permute-start.11 = (bf16[256,256]{1,0:T(8,128)(2,1)S(1)}, bf16[256,256]{1,0:T(8,128)(2,1)S(1)}, u32[]{:S(2)}, u32[]{:S(2)}) collective-permute-start(bf16[256,256]{1,0:T(8,128)(2,1)S(1)} %pad_maximum_fusion.3), channel_id=1, source_target_pairs={{12,144},{14,146},{28,160},{30,162},{44,176},{46,178},{60,192},{62... | collective-permute-start | bytes 393224 | tf_op jit(solution)/shard_map/ppermute | solution.py:45
  78.3 2.8 %collective-permute-start.12 = (f32[136,2048]{1,0:T(8,128)S(1)}, f32[136,2048]{1,0:T(8,128)S(1)}, u32[]{:S(2)}, u32[]{:S(2)}) collective-permute-start(f32[136,2048]{1,0:T(8,128)S(1)} %attend.13.rest_0_), channel_id=1, source_target_pairs={{0,1},{1,0},{2,3},{3,2},{4,5},{5,4},{6,7},{7,6},{8,9},{9,8},{10,11... | collective-permute-start | bytes 3342344 | tf_op jit(solution)/shard_map/ppermute | solution.py:45
  81.2 1.0 copy-start.3
  85.3 15.3 %collective-permute-start.16 = (bf16[256,512]{1,0:T(8,128)(2,1)S(1)}, bf16[256,512]{1,0:T(8,128)(2,1)S(1)}, u32[]{:S(2)}, u32[]{:S(2)}) collective-permute-start(bf16[256,512]{1,0:T(8,128)(2,1)S(1)} %get-tuple-element.36), channel_id=1, source_target_pairs={{0,2},{1,3},{2,0},{3,1},{4,6},{5,7},{6,4},{7,5},{8,10},{9,11},{10,... | collective-permute-start | bytes 786440 | tf_op jit(solution)/shard_map/ppermute | solution.py:45
  89.8 13.2 %collective-permute-start.15 = (bf16[256,512]{1,0:T(8,128)(2,1)S(1)}, bf16[256,512]{1,0:T(8,128)(2,1)S(1)}, u32[]{:S(2)}, u32[]{:S(2)}) collective-permute-start(bf16[256,512]{1,0:T(8,128)(2,1)S(1)} %get-tuple-element.35), channel_id=1, source_target_pairs={{0,2},{1,3},{2,0},{3,1},{4,6},{5,7},{6,4},{7,5},{8,10},{9,11},{10,... | collective-permute-start | bytes 786440 | tf_op jit(solution)/shard_map/ppermute | solution.py:45
  92.2 15.1 %collective-permute-start.14 = (bf16[256,512]{1,0:T(8,128)(2,1)S(1)}, bf16[256,512]{1,0:T(8,128)(2,1)S(1)}, u32[]{:S(2)}, u32[]{:S(2)}) collective-permute-start(bf16[256,512]{1,0:T(8,128)(2,1)S(1)} %get-tuple-element.34), channel_id=1, source_target_pairs={{0,2},{1,3},{2,0},{3,1},{4,6},{5,7},{6,4},{7,5},{8,10},{9,11},{10,... | collective-permute-start | bytes 786440 | tf_op jit(solution)/shard_map/ppermute | solution.py:45
  93.4 18.7 %collective-permute-start.13 = (bf16[256,512]{1,0:T(8,128)(2,1)S(1)}, bf16[256,512]{1,0:T(8,128)(2,1)S(1)}, u32[]{:S(2)}, u32[]{:S(2)}) collective-permute-start(bf16[256,512]{1,0:T(8,128)(2,1)S(1)} %get-tuple-element.33), channel_id=1, source_target_pairs={{0,2},{1,3},{2,0},{3,1},{4,6},{5,7},{6,4},{7,5},{8,10},{9,11},{10,... | collective-permute-start | bytes 786440 | tf_op jit(solution)/shard_map/ppermute | solution.py:45
  100.6 1.6 %copy-start = (f32[256,2048]{1,0:T(8,128)S(1)}, f32[256,2048]{1,0:T(8,128)}, u32[]{:S(2)}) copy-start(f32[256,2048]{1,0:T(8,128)} %project.4.kept) | copy-start | bytes 6291460
Sparse Core Ops, SparseCore 0:
  9.2 37.5 all-gather.1

commit v4 on v2

--- a/solution.py
+++ b/solution.py
@@ -70,6 +70,12 @@
         return (s + (9 - step) * ROW) % SEQ, hi, core
 
     return move
+
+
+def two_rows_on(s, hi, core):
+    if core == 0:
+        return (s + 2 * ROW, hi, core) if s + 2 * ROW < SEQ else None
+    return (s - 2 * ROW) % SEQ, hi, core
 
 
 def rope_tables(positions):
@@ -329,24 +335,25 @@
     own_value = lax.dynamic_index_in_dim(value_heads, hi, 1, keepdims=False)
     block = jnp.concatenate([own_key, own_value], axis=1)
 
-    near = [permute(block, along_rows(step)) for step in (1, 2, 3, 4)]
+    q_own = turn(queries, cosine, sine)
+    q_other = permute(q_own, other_core)
+    near = [permute(block, along_rows(step)) for step in (1, 2)]
     far = permute(block, far_block)
     half = lax.dynamic_slice_in_dim(block, core * (BLOCK // 2), BLOCK // 2, 0)
+    group_1 = jnp.concatenate([half, *near], axis=0)
+    near = jnp.concatenate(near, axis=0)
+    group_1, near, q_other, far, out_weight = lax.optimization_barrier(
+        (group_1, near, q_other, far, out_weight)
+    )
     shifts = (1, -1, 2)
-    group_1 = jnp.concatenate([half, near[0], near[1]], axis=0)
-    q_own = turn(queries, cosine, sine)
-    q_other = permute(q_own, other_core)
-    group_1, out_weight, q_other, *near[2:] = lax.optimization_barrier(
-        (group_1, out_weight, q_other, *near[2:])
-    )
+    group_2 = permute(near, two_rows_on)
+    columns_1 = [permute(group_1, in_row(shift)) for shift in shifts]
     other_weight = permute(out_weight, other_core)
-    columns_1 = [permute(group_1, in_row(shift)) for shift in shifts]
-    group_2 = jnp.concatenate([near[2], near[3]], axis=0)
 
     q_all = jnp.concatenate([q_own, q_other], axis=1)
     step = functools.partial(attend, ids, doc_lengths, q_all)
 
-    state = step([half] + near, [("half", 0)] + [(k, 0) for k in (1, 2, 3, 4)])
+    state = step([half, near, group_2], [("half", 0)] + [(k, 0) for k in (1, 2, 3, 4)])
     columns_2 = []
     for shift, keys in zip(shifts, columns_1):
         group_2, state = lax.optimization_barrier((group_2, state))

time: 108 us -> 95.5 us (0.88)
  the two profiles are of different devices: /device:TPU:6 before, /device:TPU:122 now
where the time goes in v4:
time: 95.5 us; the launch traced here: 95.6 us
  Pallas kernels  34.7 us (36%)
  starting transfers between devices  30.9 us (32%)
  waiting for transfers between devices  27.5 us (29%)
  local copies, waits for them, and re-layouts  1.32 us (1%)
    ppermute x17, starting transfers between devices, permute(): return lax.ppermute(x, ('seq', 'tensor'), device_perm(move))  30.9 us
    ppermute x17, waiting for transfers between devices, permute(): return lax.ppermute(x, ('seq', 'tensor'), device_perm(move))  27.5 us
    pallas_call x7, Pallas kernels, attend(): pl.pallas_call(functools.partial(attend_kernel, kinds, state is None), ou...  23.9 us
    pallas_call x3, Pallas kernels, project(): pl.pallas_call(functools.partial(project_kernel, other_side, first, mergi...  6.82 us
    pallas_call x4, Pallas kernels, finish(): pl.pallas_call(finish_kernel, out_shape=jax.ShapeDtypeStruct(kept.shape,...  2.99 us
  transfers between devices with their start and end apart: 17, of which 7 were waited for; matrix products, arithmetic and copies ran while one was open for 0% of the time, Pallas kernels for 31%

profile of v4, /device:TPU:122, one launch (start us, length us, event | category | flops | bytes accessed | tf_op | source)
XLA Modules:
  0.0 95.6 jit_solution(7139221961185898079)
XLA Ops:
  0.1 1.3 %constant_dynamic-slice_fusion.1 = (bf16[256,1,128]{2,1,0:T(2,128)(2,1)S(1)}, bf16[256,1,128]{2,1,0:T(2,128)(2,1)S(1)}) fusion(bf16[256,2,128]{2,1,0:T(2,128)(2,1)} %param.7, s32[]{:T(128)S(6)} %select_n.20, bf16[256,2,128]{2,1,0:T(2,128)(2,1)} %param.6), kind=kLoop, calls=%fused_computation.13 | loop fusion | bytes 262148 | tf_op jit(solution)/shard_map/jit(dynamic_index_in_dim)/dynamic_slice | solution.py:335
  1.4 0.6 subtract_convert_fusion
  2.0 0.1 pad_maximum_fusion.3
  2.1 5.5 %collective-permute-start.1 = (bf16[256,256]{1,0:T(8,128)(2,1)S(1)}, bf16[256,256]{1,0:T(8,128)(2,1)S(1)}, u32[]{:S(2)}, u32[]{:S(2)}) collective-permute-start(bf16[256,256]{1,0:T(8,128)(2,1)S(1)} %pad_maximum_fusion.3), channel_id=1, source_target_pairs={{0,32},{1,113},{2,34},{3,115},{4,36},{5,117},{6,38},{7,119},{8,40}... | collective-permute-start | bytes 393224 | tf_op jit(solution)/shard_map/ppermute | solution.py:45
  7.6 2.9 %collective-permute-start = (bf16[256,256]{1,0:T(8,128)(2,1)S(1)}, bf16[256,256]{1,0:T(8,128)(2,1)S(1)}, u32[]{:S(2)}, u32[]{:S(2)}) collective-permute-start(bf16[256,256]{1,0:T(8,128)(2,1)S(1)} %pad_maximum_fusion.3), channel_id=1, source_target_pairs={{0,16},{1,129},{2,18},{3,131},{4,20},{5,133},{6,22},{7,135},{8,24}... | collective-permute-start | bytes 393224 | tf_op jit(solution)/shard_map/ppermute | solution.py:45
  10.5 0.7 collective-permute-start.3
  11.2 1.0 %turn.1 = bf16[128,1024]{1,0:T(8,128)(2,1)S(1)} custom-call(bf16[256,512]{1,0:T(8,128)(2,1)S(1)} %copy-done, f32[256,64]{1,0:T(8,128)S(1)} %get-tuple-element.44.cosine, f32[256,64]{1,0:T(8,128)S(1)} %get-tuple-element.43.sine), custom_call_target="tpu_custom_call" | custom-call | flops 1 | bytes 1 | tf_op jit(solution)/shard_map/turn/pallas_call | solution.py:219
  12.2 0.1 collective-permute-start.2
  12.3 0.0 copy-start.1
  12.4 0.0 collective-permute-done.1
  12.4 2.1 %collective-permute-done = bf16[256,256]{1,0:T(8,128)(2,1)S(1)} collective-permute-done((bf16[256,256]{1,0:T(8,128)(2,1)S(1)}, bf16[256,256]{1,0:T(8,128)(2,1)S(1)}, u32[]{:S(2)}, u32[]{:S(2)}) %collective-permute-start) | collective-permute-done | bytes 131104 | tf_op jit(solution)/shard_map/ppermute | solution.py:45
  14.5 0.0 collective-permute-done.2
  14.5 0.1 collective-permute-start.11
  14.6 0.8 collective-permute-start.6
  15.4 5.3 %collective-permute-start.5 = (bf16[640,256]{1,0:T(8,128)(2,1)S(1)}, bf16[640,256]{1,0:T(8,128)(2,1)S(1)}, u32[]{:S(2)}, u32[]{:S(2)}) collective-permute-start(bf16[640,256]{1,0:T(8,128)(2,1)S(1)} %pad_maximum_fusion.1), channel_id=1, source_target_pairs={{0,4},{1,5},{2,6},{3,7},{4,8},{5,9},{6,10},{7,11},{8,12},{9,13},{1... | collective-permute-start | bytes 983048 | tf_op jit(solution)/shard_map/ppermute | solution.py:45
  20.7 2.4 %collective-permute-start.4 = (bf16[512,256]{1,0:T(8,128)(2,1)S(1)}, bf16[512,256]{1,0:T(8,128)(2,1)S(1)}, u32[]{:S(2)}, u32[]{:S(2)}) collective-permute-start(bf16[512,256]{1,0:T(8,128)(2,1)S(1)} %pad_maximum_fusion.2.rest_1_), channel_id=1, source_target_pairs={{0,32},{1,225},{2,34},{3,227},{4,36},{5,229},{6,38},{7,231},{8,40}... | collective-permute-start | bytes 786440 | tf_op jit(solution)/shard_map/ppermute | solution.py:45
  23.1 0.1 pad_add_fusion.ids
  23.1 1.4 %collective-permute-start.10 = (bf16[640,256]{1,0:T(8,128)(2,1)S(1)}, bf16[640,256]{1,0:T(8,128)(2,1)S(1)}, u32[]{:S(2)}, u32[]{:S(2)}) collective-permute-start(bf16[640,256]{1,0:T(8,128)(2,1)S(1)} %pad_maximum_fusion.1), channel_id=1, source_target_pairs={{0,8},{1,9},{2,10},{3,11},{4,12},{5,13},{6,14},{7,15},{8,0},{9,1},... | collective-permute-start | bytes 983048 | tf_op jit(solution)/shard_map/ppermute | solution.py:45
  24.6 8.2 %collective-permute-done.4.rest_2_ = bf16[512,256]{1,0:T(8,128)(2,1)S(1)} collective-permute-done((bf16[512,256]{1,0:T(8,128)(2,1)S(1)}, bf16[512,256]{1,0:T(8,128)(2,1)S(1)}, u32[]{:S(2)}, u32[]{:S(2)}) %collective-permute-start.4) | collective-permute-done | bytes 262176 | tf_op jit(solution)/shard_map/ppermute | solution.py:45
  32.8 5.0 %attend.7.rest_1_ = f32[136,2048]{1,0:T(8,128)S(1)} custom-call(s32[2]{0:T(128)S(1)} %pad_add_fusion.ids, s32[8]{0:T(128)S(1)} %copy-done.1, bf16[128,2048]{1,0:T(8,128)(2,1)S(1)} %pad_maximum_fusion.q_ref, bf16[128,256]{1,0:T(8,128)(2,1)S(1)} %constant_dynamic-slice_fusion.rest_0_, bf16[512,256]{1,0:T(8,128)(2,1)S(1)} %pad_maximum_fusion.2.rest_1_, ...), custom_call_target="tpu_custom_call" | custom-call | flops 1 | bytes 1 | tf_op jit(solution)/shard_map/attend/pallas_call | solution.py:197
  37.8 2.0 %collective-permute-start.9 = (bf16[512,256]{1,0:T(8,128)(2,1)S(1)}, bf16[512,256]{1,0:T(8,128)(2,1)S(1)}, u32[]{:S(2)}, u32[]{:S(2)}) collective-permute-start(bf16[512,256]{1,0:T(8,128)(2,1)S(1)} %collective-permute-done.4.rest_2_), channel_id=1, source_target_pairs={{0,4},{1,5},{2,6},{3,7},{4,8},{5,9},{6,10},{7,11},{8,12},{9,13},{1... | collective-permute-start | bytes 786440 | tf_op jit(solution)/shard_map/ppermute | solution.py:45
  39.8 0.0 collective-permute-done.5.rest_0_
  39.8 3.1 %attend.8.rest_1_ = f32[136,2048]{1,0:T(8,128)S(1)} custom-call(s32[2]{0:T(128)S(1)} %pad_add_fusion.ids, s32[8]{0:T(128)S(1)} %copy-done.1, bf16[128,2048]{1,0:T(8,128)(2,1)S(1)} %pad_maximum_fusion.q_ref, bf16[640,256]{1,0:T(8,128)(2,1)S(1)} %collective-permute-done.5.rest_0_, f32[136,2048]{1,0:T(8,128)S(1)} %attend.7.rest_1_), custom_call_target="tpu_custom_call", output_to_operand_aliasing={{}: (4, {})} | custom-call | flops 1 | bytes 1 | tf_op jit(solution)/shard_map/attend/pallas_call | solution.py:197
  42.9 0.2 collective-permute-start.8
  43.1 3.3 %attend.9.rest_2_ = f32[136,2048]{1,0:T(8,128)S(1)} custom-call(s32[2]{0:T(128)S(1)} %pad_add_fusion.ids, s32[8]{0:T(128)S(1)} %copy-done.1, bf16[128,2048]{1,0:T(8,128)(2,1)S(1)} %pad_maximum_fusion.q_ref, bf16[640,256]{1,0:T(8,128)(2,1)S(1)} %collective-permute-done.6.rest_0_, f32[136,2048]{1,0:T(8,128)S(1)} %attend.8.rest_1_), custom_call_target="tpu_custom_call", output_to_operand_aliasing={{}: (4, {})} | custom-call | flops 1 | bytes 1 | tf_op jit(solution)/shard_map/attend/pallas_call | solution.py:197
  46.4 2.2 %collective-permute-start.7 = (bf16[512,256]{1,0:T(8,128)(2,1)S(1)}, bf16[512,256]{1,0:T(8,128)(2,1)S(1)}, u32[]{:S(2)}, u32[]{:S(2)}) collective-permute-start(bf16[512,256]{1,0:T(8,128)(2,1)S(1)} %collective-permute-done.4.rest_2_), channel_id=1, source_target_pairs={{0,8},{1,9},{2,10},{3,11},{4,12},{5,13},{6,14},{7,15},{8,0},{9,1},... | collective-permute-start | bytes 786440 | tf_op jit(solution)/shard_map/ppermute | solution.py:45
  48.6 4.5 %attend.10.rest_1_ = f32[136,2048]{1,0:T(8,128)S(1)} custom-call(s32[2]{0:T(128)S(1)} %pad_add_fusion.ids, s32[8]{0:T(128)S(1)} %copy-done.1, bf16[128,2048]{1,0:T(8,128)(2,1)S(1)} %pad_maximum_fusion.q_ref, bf16[640,256]{1,0:T(8,128)(2,1)S(1)} %collective-permute-done.10.rest_0_, ...), custom_call_target="tpu_custom_call", output_to_operand_aliasing={{}: (5, {})} | custom-call | flops 1 | bytes 1 | tf_op jit(solution)/shard_map/attend/pallas_call | solution.py:197
  53.0 0.0 slice-start.1
  53.1 2.6 %attend.11.rest_1_ = f32[136,2048]{1,0:T(8,128)S(1)} custom-call(s32[2]{0:T(128)S(1)} %pad_add_fusion.ids, s32[8]{0:T(128)S(1)} %copy-done.1, bf16[128,2048]{1,0:T(8,128)(2,1)S(1)} %pad_maximum_fusion.q_ref, bf16[512,256]{1,0:T(8,128)(2,1)S(1)} %collective-permute-done.9.rest_0_, f32[136,2048]{1,0:T(8,128)S(1)} %attend.10.rest_1_), custom_call_target="tpu_custom_call", output_to_operand_aliasing={{}: (4, {})} | custom-call | flops 1 | bytes 1 | tf_op jit(solution)/shard_map/attend/pallas_call | solution.py:197
  55.7 2.6 %collective-permute-done.8.rest_0_ = bf16[512,256]{1,0:T(8,128)(2,1)S(1)} collective-permute-done((bf16[512,256]{1,0:T(8,128)(2,1)S(1)}, bf16[512,256]{1,0:T(8,128)(2,1)S(1)}, u32[]{:S(2)}, u32[]{:S(2)}) %collective-permute-start.8) | collective-permute-done | bytes 262176 | tf_op jit(solution)/shard_map/ppermute | solution.py:45
  58.3 2.6 %attend.12.rest_1_ = f32[136,2048]{1,0:T(8,128)S(1)} custom-call(s32[2]{0:T(128)S(1)} %pad_add_fusion.ids, s32[8]{0:T(128)S(1)} %copy-done.1, bf16[128,2048]{1,0:T(8,128)(2,1)S(1)} %pad_maximum_fusion.q_ref, bf16[512,256]{1,0:T(8,128)(2,1)S(1)} %collective-permute-done.8.rest_0_, f32[136,2048]{1,0:T(8,128)S(1)} %attend.11.rest_1_), custom_call_target="tpu_custom_call", output_to_operand_aliasing={{}: (4, {})} | custom-call | flops 1 | bytes 1 | tf_op jit(solution)/shard_map/attend/pallas_call | solution.py:197
  60.9 2.8 %attend.13.rest_0_ = f32[136,2048]{1,0:T(8,128)S(1)} custom-call(s32[2]{0:T(128)S(1)} %pad_add_fusion.ids, s32[8]{0:T(128)S(1)} %copy-done.1, bf16[128,2048]{1,0:T(8,128)(2,1)S(1)} %pad_maximum_fusion.q_ref, bf16[512,256]{1,0:T(8,128)(2,1)S(1)} %collective-permute-done.7.rest_0_, f32[136,2048]{1,0:T(8,128)S(1)} %attend.12.rest_1_), custom_call_target="tpu_custom_call", output_to_operand_aliasing={{}: (4, {})} | custom-call | flops 1 | bytes 1 | tf_op jit(solution)/shard_map/attend/pallas_call | solution.py:197
  63.8 0.1 collective-permute-start.12
  63.9 2.7 %collective-permute-done.12.rest_1_ = f32[136,2048]{1,0:T(8,128)S(1)} collective-permute-done((f32[136,2048]{1,0:T(8,128)S(1)}, f32[136,2048]{1,0:T(8,128)S(1)}, u32[]{:S(2)}, u32[]{:S(2)}) %collective-permute-start.12) | collective-permute-done | bytes 1114144 | tf_op jit(solution)/shard_map/ppermute | solution.py:45
  66.6 1.4 %project.3 = (bf16[256,1024]{1,0:T(8,128)(2,1)S(1)}, bf16[256,512]{1,0:T(8,128)(2,1)S(1)}) custom-call(s32[2]{0:T(128)S(1)} %pad_add_fusion.ids, f32[136,2048]{1,0:T(8,128)S(1)} %attend.13.rest_0_, f32[136,2048]{1,0:T(8,128)S(1)} %collective-permute-done.12.rest_1_, bf16[512,8192]{1,0:T(8,128)(2,1)S(1)} %bitcast.11, ...), custom_call_target="tpu_custom_call" | custom-call | flops 1 | bytes 1 | tf_op jit(solution)/shard_map/project/pallas_call | solution.py:281
  68.1 2.2 %collective-permute-start.16 = (bf16[256,512]{1,0:T(8,128)(2,1)S(1)}, bf16[256,512]{1,0:T(8,128)(2,1)S(1)}, u32[]{:S(2)}, u32[]{:S(2)}) collective-permute-start(bf16[256,512]{1,0:T(8,128)(2,1)S(1)} %get-tuple-element.40), channel_id=1, source_target_pairs={{0,2},{1,3},{2,0},{3,1},{4,6},{5,7},{6,4},{7,5},{8,10},{9,11},{10,... | collective-permute-start | bytes 786440 | tf_op jit(solution)/shard_map/ppermute | solution.py:45
  70.3 2.4 %project.5 = (bf16[256,512]{1,0:T(8,128)(2,1)S(1)}, bf16[256,512]{1,0:T(8,128)(2,1)S(1)}, bf16[256,512]{1,0:T(8,128)(2,1)S(1)}) custom-call(s32[2]{0:T(128)S(1)} %pad_add_fusion.ids, bf16[256,1024]{1,0:T(8,128)(2,1)S(1)} %get-tuple-element.36.rest_0_, bf16[512,8192]{1,0:T(8,128)(2,1)S(1)} %bitcast.11, ...), custom_call_target="tpu_custom_call" | custom-call | flops 1 | bytes 1 | tf_op jit(solution)/shard_map/project/pallas_call | solution.py:281
  72.7 1.5 %collective-permute-start.15 = (bf16[256,512]{1,0:T(8,128)(2,1)S(1)}, bf16[256,512]{1,0:T(8,128)(2,1)S(1)}, u32[]{:S(2)}, u32[]{:S(2)}) collective-permute-start(bf16[256,512]{1,0:T(8,128)(2,1)S(1)} %get-tuple-element.39), channel_id=1, source_target_pairs={{0,2},{1,3},{2,0},{3,1},{4,6},{5,7},{6,4},{7,5},{8,10},{9,11},{10,... | collective-permute-start | bytes 786440 | tf_op jit(solution)/shard_map/ppermute | solution.py:45
  74.2 2.1 %collective-permute-start.14 = (bf16[256,512]{1,0:T(8,128)(2,1)S(1)}, bf16[256,512]{1,0:T(8,128)(2,1)S(1)}, u32[]{:S(2)}, u32[]{:S(2)}) collective-permute-start(bf16[256,512]{1,0:T(8,128)(2,1)S(1)} %get-tuple-element.38), channel_id=1, source_target_pairs={{0,2},{1,3},{2,0},{3,1},{4,6},{5,7},{6,4},{7,5},{8,10},{9,11},{10,... | collective-permute-start | bytes 786440 | tf_op jit(solution)/shard_map/ppermute | solution.py:45
  76.3 1.4 %collective-permute-start.13 = (bf16[256,512]{1,0:T(8,128)(2,1)S(1)}, bf16[256,512]{1,0:T(8,128)(2,1)S(1)}, u32[]{:S(2)}, u32[]{:S(2)}) collective-permute-start(bf16[256,512]{1,0:T(8,128)(2,1)S(1)} %get-tuple-element.37), channel_id=1, source_target_pairs={{0,2},{1,3},{2,0},{3,1},{4,6},{5,7},{6,4},{7,5},{8,10},{9,11},{10,... | collective-permute-start | bytes 786440 | tf_op jit(solution)/shard_map/ppermute | solution.py:45
  77.7 3.0 %project.4.kept = f32[256,2048]{1,0:T(8,128)S(1)} custom-call(s32[2]{0:T(128)S(1)} %pad_add_fusion.ids, bf16[256,1024]{1,0:T(8,128)(2,1)S(1)} %get-tuple-element.36.rest_0_, bf16[512,8192]{1,0:T(8,128)(2,1)S(1)} %bitcast.11, bf16[512,8192]{1,0:T(8,128)(2,1)S(1)} %collective-permute-done.11.rest_3_.rest_2_), custom_call_target="tpu_custom_call" | custom-call | flops 1 | bytes 1 | tf_op jit(solution)/shard_map/project/pallas_call | solution.py:281
  80.7 0.7 finish.4.rest_0_
  81.5 3.0 %collective-permute-done.15.received = bf16[256,512]{1,0:T(8,128)(2,1)S(1)} collective-permute-done((bf16[256,512]{1,0:T(8,128)(2,1)S(1)}, bf16[256,512]{1,0:T(8,128)(2,1)S(1)}, u32[]{:S(2)}, u32[]{:S(2)}) %collective-permute-start.15) | collective-permute-done | bytes 262176 | tf_op jit(solution)/shard_map/ppermute | solution.py:45
  84.4 0.7 finish.5.rest_0_
  85.2 4.9 %collective-permute-done.14.received = bf16[256,512]{1,0:T(8,128)(2,1)S(1)} collective-permute-done((bf16[256,512]{1,0:T(8,128)(2,1)S(1)}, bf16[256,512]{1,0:T(8,128)(2,1)S(1)}, u32[]{:S(2)}, u32[]{:S(2)}) %collective-permute-start.14) | collective-permute-done | bytes 262176 | tf_op jit(solution)/shard_map/ppermute | solution.py:45
  90.1 0.7 finish.6.rest_0_
  90.8 4.1 %collective-permute-done.13.received = bf16[256,512]{1,0:T(8,128)(2,1)S(1)} collective-permute-done((bf16[256,512]{1,0:T(8,128)(2,1)S(1)}, bf16[256,512]{1,0:T(8,128)(2,1)S(1)}, u32[]{:S(2)}, u32[]{:S(2)}) %collective-permute-start.13) | collective-permute-done | bytes 262176 | tf_op jit(solution)/shard_map/ppermute | solution.py:45
  94.9 0.7 finish.7
  (22 shorter events, 0.2 us)
Async XLA Ops:
  0.0 11.2 %copy-start = (bf16[256,512]{1,0:T(8,128)(2,1)S(1)}, bf16[256,512]{1,0:T(8,128)(2,1)}, u32[]{:S(2)}) copy-start(bf16[256,512]{1,0:T(8,128)(2,1)} %queries.1) | copy-start | bytes 786436
  2.1 10.3 %collective-permute-start.1 = (bf16[256,256]{1,0:T(8,128)(2,1)S(1)}, bf16[256,256]{1,0:T(8,128)(2,1)S(1)}, u32[]{:S(2)}, u32[]{:S(2)}) collective-permute-start(bf16[256,256]{1,0:T(8,128)(2,1)S(1)} %pad_maximum_fusion.3), channel_id=1, source_target_pairs={{0,32},{1,113},{2,34},{3,115},{4,36},{5,117},{6,38},{7,119},{8,40}... | collective-permute-start | bytes 393224 | tf_op jit(solution)/shard_map/ppermute | solution.py:45
  7.6 6.9 %collective-permute-start = (bf16[256,256]{1,0:T(8,128)(2,1)S(1)}, bf16[256,256]{1,0:T(8,128)(2,1)S(1)}, u32[]{:S(2)}, u32[]{:S(2)}) collective-permute-start(bf16[256,256]{1,0:T(8,128)(2,1)S(1)} %pad_maximum_fusion.3), channel_id=1, source_target_pairs={{0,16},{1,129},{2,18},{3,131},{4,20},{5,133},{6,22},{7,135},{8,24}... | collective-permute-start | bytes 393224 | tf_op jit(solution)/shard_map/ppermute | solution.py:45
  10.5 4.0 %collective-permute-start.3 = (bf16[256,256]{1,0:T(8,128)(2,1)S(1)}, bf16[256,256]{1,0:T(8,128)(2,1)S(1)}, u32[]{:S(2)}, u32[]{:S(2)}) collective-permute-start(bf16[256,256]{1,0:T(8,128)(2,1)S(1)} %pad_maximum_fusion.3), channel_id=1, source_target_pairs={{12,144},{14,146},{28,160},{30,162},{44,176},{46,178},{60,192},{62... | collective-permute-start | bytes 393224 | tf_op jit(solution)/shard_map/ppermute | solution.py:45
  12.2 2.3 %collective-permute-start.2 = (bf16[128,1024]{1,0:T(8,128)(2,1)S(1)}, bf16[128,1024]{1,0:T(8,128)(2,1)S(1)}, u32[]{:S(2)}, u32[]{:S(2)}) collective-permute-start(bf16[128,1024]{1,0:T(8,128)(2,1)S(1)} %turn.1), channel_id=1, source_target_pairs={{0,1},{1,0},{2,3},{3,2},{4,5},{5,4},{6,7},{7,6},{8,9},{9,8},{10,11... | collective-permute-start | bytes 786440 | tf_op jit(solution)/shard_map/ppermute | solution.py:45
  12.3 20.4 %copy-start.1 = (s32[8]{0:T(128)S(1)}, s32[8]{0:T(128)}, u32[]{:S(2)}) copy-start(s32[8]{0:T(128)} %lengths.13) | copy-start | bytes 100
  14.5 38.5 %collective-permute-start.11 = (bf16[512,8192]{1,0:T(8,128)(2,1)}, bf16[512,8192]{1,0:T(8,128)(2,1)S(1)}, u32[]{:S(2)}, u32[]{:S(2)}) collective-permute-start(bf16[512,8192]{1,0:T(8,128)(2,1)} %rest_1_.1), channel_id=1, source_target_pairs={{0,1},{1,0},{2,3},{3,2},{4,5},{5,4},{6,7},{7,6},{8,9},{9,8},{10,11... | collective-permute-start | bytes 25165832 | tf_op jit(solution)/shard_map/ppermute | solution.py:45
  14.6 28.5 %collective-permute-start.6 = (bf16[640,256]{1,0:T(8,128)(2,1)S(1)}, bf16[640,256]{1,0:T(8,128)(2,1)S(1)}, u32[]{:S(2)}, u32[]{:S(2)}) collective-permute-start(bf16[640,256]{1,0:T(8,128)(2,1)S(1)} %pad_maximum_fusion.1), channel_id=1, source_target_pairs={{0,12},{1,13},{2,14},{3,15},{4,0},{5,1},{6,2},{7,3},{8,4},{9,5},{1... | collective-permute-start | bytes 983048 | tf_op jit(solution)/shard_map/ppermute | solution.py:45
  15.4 24.4 %collective-permute-start.5 = (bf16[640,256]{1,0:T(8,128)(2,1)S(1)}, bf16[640,256]{1,0:T(8,128)(2,1)S(1)}, u32[]{:S(2)}, u32[]{:S(2)}) collective-permute-start(bf16[640,256]{1,0:T(8,128)(2,1)S(1)} %pad_maximum_fusion.1), channel_id=1, source_target_pairs={{0,4},{1,5},{2,6},{3,7},{4,8},{5,9},{6,10},{7,11},{8,12},{9,13},{1... | collective-permute-start | bytes 983048 | tf_op jit(solution)/shard_map/ppermute | solution.py:45
  20.7 12.1 %collective-permute-start.4 = (bf16[512,256]{1,0:T(8,128)(2,1)S(1)}, bf16[512,256]{1,0:T(8,128)(2,1)S(1)}, u32[]{:S(2)}, u32[]{:S(2)}) collective-permute-start(bf16[512,256]{1,0:T(8,128)(2,1)S(1)} %pad_maximum_fusion.2.rest_1_), channel_id=1, source_target_pairs={{0,32},{1,225},{2,34},{3,227},{4,36},{5,229},{6,38},{7,231},{8,40}... | collective-permute-start | bytes 786440 | tf_op jit(solution)/shard_map/ppermute | solution.py:45
  23.1 25.4 %collective-permute-start.10 = (bf16[640,256]{1,0:T(8,128)(2,1)S(1)}, bf16[640,256]{1,0:T(8,128)(2,1)S(1)}, u32[]{:S(2)}, u32[]{:S(2)}) collective-permute-start(bf16[640,256]{1,0:T(8,128)(2,1)S(1)} %pad_maximum_fusion.1), channel_id=1, source_target_pairs={{0,8},{1,9},{2,10},{3,11},{4,12},{5,13},{6,14},{7,15},{8,0},{9,1},... | collective-permute-start | bytes 983048 | tf_op jit(solution)/shard_map/ppermute | solution.py:45
  37.8 15.3 %collective-permute-start.9 = (bf16[512,256]{1,0:T(8,128)(2,1)S(1)}, bf16[512,256]{1,0:T(8,128)(2,1)S(1)}, u32[]{:S(2)}, u32[]{:S(2)}) collective-permute-start(bf16[512,256]{1,0:T(8,128)(2,1)S(1)} %collective-permute-done.4.rest_2_), channel_id=1, source_target_pairs={{0,4},{1,5},{2,6},{3,7},{4,8},{5,9},{6,10},{7,11},{8,12},{9,13},{1... | collective-permute-start | bytes 786440 | tf_op jit(solution)/shard_map/ppermute | solution.py:45
  42.9 15.4 %collective-permute-start.8 = (bf16[512,256]{1,0:T(8,128)(2,1)S(1)}, bf16[512,256]{1,0:T(8,128)(2,1)S(1)}, u32[]{:S(2)}, u32[]{:S(2)}) collective-permute-start(bf16[512,256]{1,0:T(8,128)(2,1)S(1)} %collective-permute-done.4.rest_2_), channel_id=1, source_target_pairs={{0,12},{1,13},{2,14},{3,15},{4,0},{5,1},{6,2},{7,3},{8,4},{9,5},{1... | collective-permute-start | bytes 786440 | tf_op jit(solution)/shard_map/ppermute | solution.py:45
  43.1 23.5 %slice-start = ((s8[8388608]{0:T(1024)(128)(4,1)}), s8[4194304]{0:T(1024)(128)(4,1)S(1)}, s32[]{:S(2)}) async-start(s8[8388608]{0:T(1024)(128)(4,1)} %bitcast.10), calls=%async_computation | async-start | bytes 8388608
  46.4 14.5 %collective-permute-start.7 = (bf16[512,256]{1,0:T(8,128)(2,1)S(1)}, bf16[512,256]{1,0:T(8,128)(2,1)S(1)}, u32[]{:S(2)}, u32[]{:S(2)}) collective-permute-start(bf16[512,256]{1,0:T(8,128)(2,1)S(1)} %collective-permute-done.4.rest_2_), channel_id=1, source_target_pairs={{0,8},{1,9},{2,10},{3,11},{4,12},{5,13},{6,14},{7,15},{8,0},{9,1},... | collective-permute-start | bytes 786440 | tf_op jit(solution)/shard_map/ppermute | solution.py:45
  53.0 13.6 %slice-start.1 = ((s8[8388608]{0:T(1024)(128)(4,1)}), s8[4194304]{0:T(1024)(128)(4,1)S(1)}, s32[]{:S(2)}) async-start(s8[8388608]{0:T(1024)(128)(4,1)} %bitcast.10), calls=%async_computation.1 | async-start | bytes 8388608
  63.8 2.8 %collective-permute-start.12 = (f32[136,2048]{1,0:T(8,128)S(1)}, f32[136,2048]{1,0:T(8,128)S(1)}, u32[]{:S(2)}, u32[]{:S(2)}) collective-permute-start(f32[136,2048]{1,0:T(8,128)S(1)} %attend.13.rest_0_), channel_id=1, source_target_pairs={{0,1},{1,0},{2,3},{3,2},{4,5},{5,4},{6,7},{7,6},{8,9},{9,8},{10,11... | collective-permute-start | bytes 3342344 | tf_op jit(solution)/shard_map/ppermute | solution.py:45
  68.1 12.6 %collective-permute-start.16 = (bf16[256,512]{1,0:T(8,128)(2,1)S(1)}, bf16[256,512]{1,0:T(8,128)(2,1)S(1)}, u32[]{:S(2)}, u32[]{:S(2)}) collective-permute-start(bf16[256,512]{1,0:T(8,128)(2,1)S(1)} %get-tuple-element.40), channel_id=1, source_target_pairs={{0,2},{1,3},{2,0},{3,1},{4,6},{5,7},{6,4},{7,5},{8,10},{9,11},{10,... | collective-permute-start | bytes 786440 | tf_op jit(solution)/shard_map/ppermute | solution.py:45
  72.7 11.8 %collective-permute-start.15 = (bf16[256,512]{1,0:T(8,128)(2,1)S(1)}, bf16[256,512]{1,0:T(8,128)(2,1)S(1)}, u32[]{:S(2)}, u32[]{:S(2)}) collective-permute-start(bf16[256,512]{1,0:T(8,128)(2,1)S(1)} %get-tuple-element.39), channel_id=1, source_target_pairs={{0,2},{1,3},{2,0},{3,1},{4,6},{5,7},{6,4},{7,5},{8,10},{9,11},{10,... | collective-permute-start | bytes 786440 | tf_op jit(solution)/shard_map/ppermute | solution.py:45
  74.2 15.9 %collective-permute-start.14 = (bf16[256,512]{1,0:T(8,128)(2,1)S(1)}, bf16[256,512]{1,0:T(8,128)(2,1)S(1)}, u32[]{:S(2)}, u32[]{:S(2)}) collective-permute-start(bf16[256,512]{1,0:T(8,128)(2,1)S(1)} %get-tuple-element.38), channel_id=1, source_target_pairs={{0,2},{1,3},{2,0},{3,1},{4,6},{5,7},{6,4},{7,5},{8,10},{9,11},{10,... | collective-permute-start | bytes 786440 | tf_op jit(solution)/shard_map/ppermute | solution.py:45
  76.3 18.6 %collective-permute-start.13 = (bf16[256,512]{1,0:T(8,128)(2,1)S(1)}, bf16[256,512]{1,0:T(8,128)(2,1)S(1)}, u32[]{:S(2)}, u32[]{:S(2)}) collective-permute-start(bf16[256,512]{1,0:T(8,128)(2,1)S(1)} %get-tuple-element.37), channel_id=1, source_target_pairs={{0,2},{1,3},{2,0},{3,1},{4,6},{5,7},{6,4},{7,5},{8,10},{9,11},{10,... | collective-permute-start | bytes 786440 | tf_op jit(solution)/shard_map/ppermute | solution.py:45
